TPU v7x, 32 devices: a whole 2x2x4 slice. The times are simulated.
32 devices in a mesh: section: 2 (over x), dp: 8 (over z, y), tensor: 2 (over core).
Axes of the slice: x: 2, y: 2, z: 4, core: 2. Of those that a mesh axis runs over, the one named last changes fastest.
Arguments:
- x_in: bfloat16 [2, 2048, 2048], P(None, 'dp'), may hold values from -6 to 6
- cotangent: bfloat16 [2, 2048, 2048], P(None, 'dp'), may hold values from -6 to 6
- layout: int32 [2, 2048], P(None, 'dp'), may hold values from 0 to 2, as said below
- w_qkv: bfloat16 [2, 2048, 3, 2048], P('section', 'dp', None, 'tensor'), may hold values from -0.125 to 0.125
- b_qv: float32 [2, 2, 2048], P('section', None, 'tensor'), may hold values from -3 to 3
- w_out: bfloat16 [2, 2048, 2048], P('section', 'dp', 'tensor'), may hold values from -0.5 to 0.5
- w_fc1: bfloat16 [2, 2048, 8192], P('section', 'dp', 'tensor'), may hold values from -0.125 to 0.125
- b_fc1: float32 [2, 8192], P('section', 'tensor'), may hold values from -3 to 3
- w_fc2: bfloat16 [2, 2048, 8192], P('section', 'dp', 'tensor'), may hold values from -0.0625 to 0.0625
- gains: float32 [2, 2, 2048], P('section'), may hold values from 0.25 to 1.75
- biases: float32 [2, 4, 2048], P('section'), may hold values from -2 to 2
Outputs:
- section_outputs: bfloat16 [2, 2, 2048, 2048], P('section', None, 'dp')
- input_grads: bfloat16 [2, 2, 2048, 2048], P('section', None, 'dp')
- grad_w_qkv: float32 [2, 2048, 3, 2048], P('section', 'dp', None, 'tensor')
- grad_b_qv: float32 [2, 2, 2048], P('section', None, 'tensor')
- grad_w_out: float32 [2, 2048, 2048], P('section', 'dp', 'tensor')
- grad_w_fc1: float32 [2, 2048, 8192], P('section', 'dp', 'tensor')
- grad_b_fc1: float32 [2, 8192], P('section', 'tensor')
- grad_w_fc2: float32 [2, 2048, 8192], P('section', 'dp', 'tensor')
- grad_gains: float32 [2, 2, 2048], P('section')
- grad_biases: float32 [2, 4, 2048], P('section')
Inputs may be any that keep to these rules, and one draw needn't show every extreme that they name: `layout`: in each group of 256 tokens the segment numbers never fall: a prompt of segment 0 with 64 to 128 tokens, then continuations 1 to 2 in order, each non-empty, of nearly equal lengths.
All inputs are finite; a program needn't handle non-finite values.
Results may differ from a plain program's by a relative error of at most 0.018.
Values may be sent and summed in bfloat16 or wider, within the bound.
A program may use at most 384 MiB of HBM per device.

v0:
```python
from functools import reduce

import jax
import jax.numpy as jnp
from jax import lax
from jax.sharding import PartitionSpec as P

HEADS = 32
HEAD_DIM = 64


epsilon = 1e-05


def from_behind(block, axis, distance):
    devices = range(lax.axis_size(axis))
    route = [(i - distance, i) for i in devices if i - distance in devices]
    return lax.ppermute(block, axis, route)


def layer_norm(inputs, gain_vec, shift_vec):
    centred = inputs - jnp.mean(inputs, axis=-1, keepdims=True)
    spread = jnp.mean(centred * centred, axis=-1, keepdims=True)
    return centred * lax.rsqrt(spread + epsilon) * gain_vec + shift_vec


def exact_gelu(values):
    return jax.nn.gelu(values, approximate=False)


def geometry(segment):
    length = segment.shape[0]
    places = jnp.arange(length, dtype=jnp.int32)
    same_seg = segment[:, None] == segment[None, :]
    starts = jnp.min(jnp.where(same_seg, places[None, :], length), axis=1)
    prompt_len = jnp.sum((segment == 0).astype(jnp.int32))
    position = jnp.where(segment == 0, places, prompt_len + places - starts)
    allowed = (position[None, :] <= position[:, None]) & ((segment[None, :] == 0) | same_seg)
    offset = (position[:, None] - position[None, :]).astype(jnp.float32)
    return (offset, allowed)


def attention_scores(queries, key_rows, offset, allowed, head_slopes):
    score_scale = float(HEAD_DIM) ** (-0.5)
    scores = (
        jnp.einsum("qhd,khd->hqk", queries, key_rows, preferred_element_type=jnp.float32)
        * score_scale
    )
    scores = scores - head_slopes[:, None, None] * offset[None]
    return jnp.where(allowed[None], scores, -1000000000.0)


def contract_last(left, right):
    return lax.dot_general(
        left, right, (((1,), (1,)), ((), ())), preferred_element_type=jnp.float32
    )


def forward_pass(inputs, segment, weights, head_slopes):
    attn_full, proj_full, up_full, down_full, bias_qv, bias_up, gain_rows, shift_rows = weights
    row_count = inputs.shape[0]
    shard_width = proj_full.shape[1]
    local_heads = shard_width // HEAD_DIM
    widened = inputs.astype(jnp.float32)
    normed = layer_norm(widened, gain_rows[0], shift_rows[0]).astype(jnp.bfloat16)
    projected = jnp.dot(normed, attn_full, preferred_element_type=jnp.float32).reshape(
        row_count, 3, shard_width
    )
    queries = (projected[:, 0] + bias_qv[0]).astype(jnp.bfloat16)
    key_rows = projected[:, 1].astype(jnp.bfloat16)
    value_rows = (projected[:, 2] + bias_qv[1]).astype(jnp.bfloat16)
    offset, allowed = geometry(segment)
    scores = attention_scores(
        queries.reshape(row_count, local_heads, HEAD_DIM),
        key_rows.reshape(row_count, local_heads, HEAD_DIM),
        offset,
        allowed,
        head_slopes,
    )
    row_max = jnp.max(scores, axis=-1, keepdims=True)
    lifted = jnp.exp(scores - row_max)
    row_total = jnp.sum(lifted, axis=-1, keepdims=True)
    probs = lifted / row_total
    log_total = row_max[..., 0] + jnp.log(row_total[..., 0])
    mixed = (
        jnp.einsum(
            "hqk,khd->qhd",
            probs.astype(jnp.bfloat16),
            value_rows.reshape(row_count, local_heads, HEAD_DIM),
            preferred_element_type=jnp.float32,
        )
        .reshape(row_count, shard_width)
        .astype(jnp.bfloat16)
    )
    branch = lax.psum(contract_last(mixed, proj_full), "tensor")
    hidden = widened + branch + shift_rows[2]
    normed_two = layer_norm(hidden, gain_rows[1], shift_rows[1]).astype(jnp.bfloat16)
    upward = jnp.dot(normed_two, up_full, preferred_element_type=jnp.float32) + bias_up
    activated = exact_gelu(upward).astype(jnp.bfloat16)
    down_sum = lax.psum(contract_last(activated, down_full), "tensor")
    result = hidden + down_sum + shift_rows[3]
    stash_item = (
        inputs,
        normed,
        queries,
        key_rows,
        value_rows,
        mixed,
        log_total,
        hidden,
        normed_two,
        upward,
        activated,
    )
    return (result, stash_item)


def backward_pass(grad_out, stash_item, segment, weights, head_slopes):
    attn_full, proj_full, up_full, down_full, bias_qv, bias_up, gain_rows, shift_rows = weights
    (
        inputs,
        normed,
        queries,
        key_rows,
        value_rows,
        mixed,
        log_total,
        hidden,
        normed_two,
        upward,
        activated,
    ) = stash_item
    row_count, shard_width = mixed.shape
    local_heads = shard_width // HEAD_DIM
    score_scale = float(HEAD_DIM) ** (-0.5)
    grad_wide = grad_out.astype(jnp.float32)
    grad_act = jnp.dot(grad_out, down_full, preferred_element_type=jnp.float32)
    gelu_value, gelu_back = jax.vjp(exact_gelu, upward)
    grad_up = gelu_back(grad_act)[0].astype(jnp.bfloat16)
    grad_norm_two = lax.psum(contract_last(grad_up, up_full), "tensor")
    ln_value, second_back = jax.vjp(layer_norm, hidden, gain_rows[1], shift_rows[1])
    grad_hidden_ln, grad_gain_two, grad_shift_two = second_back(grad_norm_two)
    grad_hidden = grad_wide + grad_hidden_ln
    grad_branch = grad_hidden.astype(jnp.bfloat16)
    grad_mixed = jnp.dot(grad_branch, proj_full, preferred_element_type=jnp.float32).astype(
        jnp.bfloat16
    )
    query_heads = queries.reshape(row_count, local_heads, HEAD_DIM)
    key_heads = key_rows.reshape(row_count, local_heads, HEAD_DIM)
    value_heads = value_rows.reshape(row_count, local_heads, HEAD_DIM)
    mixed_heads = grad_mixed.reshape(row_count, local_heads, HEAD_DIM)
    offset, allowed = geometry(segment)
    scores = attention_scores(query_heads, key_heads, offset, allowed, head_slopes)
    probs = jnp.exp(scores - log_total[..., None])
    grad_probs = jnp.einsum(
        "qhd,khd->hqk", mixed_heads, value_heads, preferred_element_type=jnp.float32
    )
    grad_values = (
        jnp.einsum(
            "hqk,qhd->khd",
            probs.astype(jnp.bfloat16),
            mixed_heads,
            preferred_element_type=jnp.float32,
        )
        .reshape(row_count, shard_width)
        .astype(jnp.bfloat16)
    )
    centre = jnp.sum(probs * grad_probs, axis=-1, keepdims=True)
    grad_scores = (probs * (grad_probs - centre)).astype(jnp.bfloat16)
    grad_queries = (
        (
            jnp.einsum("hqk,khd->qhd", grad_scores, key_heads, preferred_element_type=jnp.float32)
            * score_scale
        )
        .reshape(row_count, shard_width)
        .astype(jnp.bfloat16)
    )
    grad_keys = (
        (
            jnp.einsum("hqk,qhd->khd", grad_scores, query_heads, preferred_element_type=jnp.float32)
            * score_scale
        )
        .reshape(row_count, shard_width)
        .astype(jnp.bfloat16)
    )
    grad_proj = jnp.stack([grad_queries, grad_keys, grad_values], axis=1).reshape(
        row_count, 3 * shard_width
    )
    grad_normed = lax.psum(contract_last(grad_proj, attn_full), "tensor")
    ln_first, first_back = jax.vjp(
        layer_norm, inputs.astype(jnp.float32), gain_rows[0], shift_rows[0]
    )
    grad_in_ln, grad_gain_one, grad_shift_one = first_back(grad_normed)
    grad_in = grad_hidden + grad_in_ln
    small_grads = (
        jnp.stack([grad_gain_one, grad_gain_two]),
        jnp.stack(
            [
                grad_shift_one,
                grad_shift_two,
                jnp.sum(grad_hidden, axis=0),
                jnp.sum(grad_wide, axis=0),
            ]
        ),
        jnp.stack(
            [
                jnp.sum(grad_queries.astype(jnp.float32), axis=0),
                jnp.sum(grad_values.astype(jnp.float32), axis=0),
            ]
        ),
        jnp.sum(grad_up.astype(jnp.float32), axis=0),
    )
    operands = (normed, grad_proj, grad_branch, mixed, normed_two, grad_up, grad_out, activated)
    return (grad_in, small_grads, operands)


def row_product(left, right):
    return lax.dot_general(
        left, right, (((0,), (0,)), ((), ())), preferred_element_type=jnp.float32
    )


def attention_terms(operands):
    normed, grad_proj, grad_branch, mixed, normed_two, grad_up, grad_out, activated = operands
    return jnp.concatenate(
        [row_product(normed, grad_proj), row_product(grad_branch, mixed)], axis=1
    )


def feedforward_terms(operands):
    normed, grad_proj, grad_branch, mixed, normed_two, grad_up, grad_out, activated = operands
    return jnp.concatenate(
        [row_product(normed_two, grad_up), row_product(grad_out, activated)], axis=1
    )


def weight_terms(operands):
    return jnp.concatenate([attention_terms(operands), feedforward_terms(operands)], axis=1)


def shards(x_in, cotangent, layout, w_qkv, b_qv, w_out, w_fc1, b_fc1, w_fc2, gains, biases):
    attn_full, proj_full, up_full, down_full = (
        lax.all_gather(w_qkv[0], "dp", axis=0, tiled=True),
        lax.all_gather(w_out[0], "dp", axis=0, tiled=True),
        lax.all_gather(w_fc1[0], "dp", axis=0, tiled=True),
        lax.all_gather(w_fc2[0], "dp", axis=0, tiled=True),
    )
    model_width, shard_width = proj_full.shape
    hidden_width = up_full.shape[1]
    shard_rows = w_qkv.shape[1]
    attn_full = attn_full.reshape(model_width, 3 * shard_width)
    weights = (attn_full, proj_full, up_full, down_full, b_qv[0], b_fc1[0], gains[0], biases[0])
    local_heads = shard_width // HEAD_DIM
    head_ids = lax.axis_index("tensor") * local_heads + jnp.arange(local_heads, dtype=jnp.int32)
    head_slopes = jnp.exp2(-8.0 * (head_ids + 1).astype(jnp.float32) / HEADS)
    section_index = lax.axis_index("section")
    section_count = lax.axis_size("section")
    micro_count = x_in.shape[0]
    tick_count = micro_count + section_count - 1
    received = jnp.zeros(x_in.shape[1:], jnp.bfloat16)
    forward_outs = []
    stash_list = []
    for tick_num in range(tick_count):
        micro_index = jnp.clip(tick_num - section_index, 0, micro_count - 1)
        first_in = lax.dynamic_index_in_dim(x_in, micro_index, 0, keepdims=False)
        layer_in = jnp.where(section_index == 0, first_in, received)
        segment = lax.dynamic_index_in_dim(layout, micro_index, 0, keepdims=False)
        result, stash_item = forward_pass(layer_in, segment, weights, head_slopes)
        sent = result.astype(jnp.bfloat16)
        forward_outs.append(sent)
        stash_list.append(stash_item)
        received = from_behind(sent, "section", 1)
    stash_all = jax.tree.map(lambda *items: jnp.stack(items), *stash_list)
    section_outputs = lax.dynamic_slice_in_dim(
        jnp.stack(forward_outs), section_index, micro_count, 0
    )
    received = jnp.zeros(x_in.shape[1:], jnp.bfloat16)
    backward_outs = []
    small_list = []
    operand_list = []
    for tick_num in range(tick_count):
        micro_raw = tick_num - (section_count - 1 - section_index)
        is_valid = (micro_raw >= 0) & (micro_raw < micro_count)
        micro_index = jnp.clip(micro_raw, 0, micro_count - 1)
        last_in = lax.dynamic_index_in_dim(cotangent, micro_index, 0, keepdims=False)
        grad_out = jnp.where(section_index == section_count - 1, last_in, received)
        segment = lax.dynamic_index_in_dim(layout, micro_index, 0, keepdims=False)
        stash_item = jax.tree.map(
            lambda stacked: lax.dynamic_index_in_dim(
                stacked, micro_index + section_index, 0, keepdims=False
            ),
            stash_all,
        )
        grad_in, small_grads, operands = backward_pass(
            grad_out, stash_item, segment, weights, head_slopes
        )
        sent = grad_in.astype(jnp.bfloat16)
        backward_outs.append(sent)
        received = from_behind(sent, "section", -1)
        small_list.append(jax.tree.map(lambda piece: jnp.where(is_valid, piece, 0.0), small_grads))
        normed, grad_proj, grad_branch, mixed, normed_two, grad_up, grad_kept, activated = operands
        zero_bf = jnp.zeros((), jnp.bfloat16)
        masked = (
            normed,
            jnp.where(is_valid, grad_proj, zero_bf),
            jnp.where(is_valid, grad_branch, zero_bf),
            mixed,
            normed_two,
            jnp.where(is_valid, grad_up, zero_bf),
            jnp.where(is_valid, grad_kept, zero_bf),
            activated,
        )
        operand_list.append(masked)
    joined = tuple((jnp.concatenate(parts, axis=0) for parts in zip(*operand_list)))
    qkv_end = 3 * shard_width
    proj_end = qkv_end + shard_width
    total_terms = lax.psum_scatter(
        weight_terms(joined).astype(jnp.bfloat16), "dp", scatter_dimension=0, tiled=True
    ).astype(jnp.float32)
    attn_terms = total_terms[:, :proj_end]
    mlp_terms = total_terms[:, proj_end:]
    input_grads = lax.dynamic_slice_in_dim(
        jnp.stack(backward_outs), section_count - 1 - section_index, micro_count, 0
    )
    small_sum = jax.tree.map(lambda *parts: reduce(jnp.add, parts), *small_list)
    gain_grad, shift_grad, bias_qv_grad, bias_up_grad = (
        lax.psum(small_sum[0][None].astype(jnp.bfloat16), "dp").astype(jnp.float32),
        lax.psum(small_sum[1][None].astype(jnp.bfloat16), "dp").astype(jnp.float32),
        lax.psum(small_sum[2][None].astype(jnp.bfloat16), "dp").astype(jnp.float32),
        lax.psum(small_sum[3][None].astype(jnp.bfloat16), "dp").astype(jnp.float32),
    )
    grad_attn = attn_terms[:, :qkv_end].reshape(shard_rows, 3, shard_width)[None]
    grad_proj_w = attn_terms[:, qkv_end:proj_end][None]
    grad_up_w = mlp_terms[:, :hidden_width][None]
    grad_down_w = mlp_terms[:, hidden_width:][None]
    return (
        section_outputs[None],
        input_grads[None],
        grad_attn,
        bias_qv_grad,
        grad_proj_w,
        grad_up_w,
        bias_up_grad,
        grad_down_w,
        gain_grad,
        shift_grad,
    )


def solution(mesh):
    return jax.shard_map(
        shards,
        mesh=mesh,
        in_specs=(
            P(None, "dp", None),
            P(None, "dp", None),
            P(None, "dp"),
            P("section", "dp", None, "tensor"),
            P("section", None, "tensor"),
            P("section", "dp", "tensor"),
            P("section", "dp", "tensor"),
            P("section", "tensor"),
            P("section", "dp", "tensor"),
            P("section", None, None),
            P("section", None, None),
        ),
        out_specs=(
            P("section", None, "dp", None),
            P("section", None, "dp", None),
            P("section", "dp", None, "tensor"),
            P("section", None, "tensor"),
            P("section", "dp", "tensor"),
            P("section", "dp", "tensor"),
            P("section", "tensor"),
            P("section", "dp", "tensor"),
            P("section", None, None),
            P("section", None, None),
        ),
        check_vma=False,
    )
```

profile of v0, /device:TPU:0, one launch (start us, length us, event | category | flops | bytes accessed | tf_op | source)
XLA Modules:
  0.0 2346.8 jit_solution(620239613701559910)
XLA Ops:
  19.4 170.0 %all-gather.9.cloned.1.call-done = bf16[1,2048,3,1024]{3,1,2,0:T(8,128)(2,1)} async-done(((bf16[1,256,3,1024]{3,1,2,0:T(8,128)(2,1)}), bf16[1,2048,3,1024]{3,1,2,0:T(8,128)(2,1)}) %all-gather.9.cloned.1.call-update) | async-done | bytes 12582928 | tf_op jit(solution)/shard_map/all_gather | solution.py:243
  224.3 38.9 %all-gather.11.cloned.1.call-done = bf16[1,2048,1024]{2,1,0:T(8,128)(2,1)} async-done(((bf16[1,256,1024]{2,1,0:T(8,128)(2,1)}), bf16[1,2048,1024]{2,1,0:T(8,128)(2,1)}) %all-gather.11.cloned.1.call-update) | async-done | bytes 4194320 | tf_op jit(solution)/shard_map/all_gather | solution.py:244
  269.4 18.2 all-reduce.15.cloned.1.call-done
  289.9 228.7 %all-gather.13.cloned.1.call-done = bf16[1,2048,4096]{2,1,0:T(8,128)(2,1)} async-done(((bf16[1,256,4096]{2,1,0:T(8,128)(2,1)}), bf16[1,2048,4096]{2,1,0:T(8,128)(2,1)}) %all-gather.13.cloned.1.call-update) | async-done | bytes 16777232 | tf_op jit(solution)/shard_map/all_gather | solution.py:245
  518.6 18.6 fusion.62
  537.3 209.4 %all-gather.15.cloned.1.call-done = bf16[1,2048,4096]{2,1,0:T(8,128)(2,1)} async-done(((bf16[1,256,4096]{2,1,0:T(8,128)(2,1)}), bf16[1,2048,4096]{2,1,0:T(8,128)(2,1)}) %all-gather.15.cloned.1.call-update) | async-done | bytes 16777232 | tf_op jit(solution)/shard_map/all_gather | solution.py:246
  759.0 19.5 all-reduce.17.cloned.1.call-done
  786.2 22.1 collective-permute-done
  830.3 23.1 all-reduce.19.cloned.1.call-done
  857.2 19.0 fusion.65
  893.0 18.2 all-reduce.21.cloned.1.call-done
  922.3 18.7 collective-permute-done.1
  991.6 18.9 fusion.68
  1021.4 19.5 broadcast_select_fusion.2
  1107.7 19.0 all-reduce.27.cloned.1.call-done
  1135.3 26.2 %collective-permute-done.2 = bf16[256,2048]{1,0:T(8,128)(2,1)} collective-permute-done((bf16[256,2048]{1,0:T(8,128)(2,1)}, bf16[256,2048]{1,0:T(8,128)(2,1)}, u32[]{:S(2)}, u32[]{:S(2)}) %collective-permute-start.2) | collective-permute-done | bytes 1048608 | tf_op jit(solution)/shard_map/ppermute | solution.py:18
  1164.2 19.6 broadcast_select_fusion.1
  1294.1 20.3 collective-permute-done.3
  1316.4 19.2 broadcast_select_fusion
  1407.1 20.4 convolution_convert_fusion
  1462.8 19.9 convolution_convert_fusion.1
  1482.7 33.2 %pad_maximum_fusion = bf16[2048,12288]{1,0:T(8,128)(2,1)} fusion(bf16[2048,4096]{1,0:T(8,128)(2,1)} %convolution_convert_fusion, bf16[2048,4096]{1,0:T(8,128)(2,1)} %convolution_convert_fusion.1, bf16[2048,1024]{1,0:T(8,128)(2,1)} %copy.154, bf16[2048,3072]{1,0:T(8,128)(2,1)} %convolution_convert_fusion.2), kind=kLoop, calls=%fused_computation | loop fusion | flops 201326592 | bytes 100663296 | tf_op jit(solution)/shard_map/concatenate | solution.py:238
  1531.5 41.5 %all-reduce.2 = (bf16[1,2,1024]{2,1,0:T(2,128)(2,1)S(1)}, bf16[1,4096]{1,0:T(2,128)(2,1)S(1)}, bf16[1,2,2048]{2,1,0:T(2,128)(2,1)S(1)}, bf16[1,4,2048]{2,1,0:T(4,128)(2,1)S(1)}) all-reduce(bf16[1,2,1024]{2,1,0:T(2,128)(2,1)S(1)} %fusion.357, ...), channel_id=1, replica_groups=mesh['section'=2,'dp'=8,'tensor'=2] {'dp'}, use_global_device_ids=true, to_apply=%region_76.77 | all-reduce | flops 18432 | bytes 73728 | tf_op jit(solution)/shard_map/psum | solution.py:329
  1582.6 724.5 %reduce-scatter.4.cloned.1.call-done = bf16[256,12288]{1,0:T(8,128)(2,1)} async-done(((bf16[2048,12288]{1,0:T(8,128)(2,1)}), bf16[256,12288]{1,0:T(8,128)(2,1)}) %reduce-scatter.4.cloned.1.call-update) | async-done | bytes 6291472
  (633 shorter events, 543.6 us)
Async XLA Ops:
  7.2 182.2 %all-gather.9.cloned.1.call-start = ((), (), s32[]{:S(2)}) async-start(), calls=%async_computation.11 | async-start | bytes 14155776 | tf_op jit(solution)/shard_map/all_gather | solution.py:243
  7.9 255.2 %all-gather.11.cloned.1.call-start = ((), (), s32[]{:S(2)}) async-start(), calls=%async_computation.12 | async-start | bytes 4718592 | tf_op jit(solution)/shard_map/all_gather | solution.py:244
  8.7 278.9 %all-reduce.15.cloned.1.call-start = ((), (), s32[]{:S(2)}) async-start(), calls=%async_computation.1 | async-start | bytes 4194304 | tf_op jit(solution)/shard_map/psum | solution.py:95
  18.8 1266.2 %copy-start.72 = (f32[1,1,2048]{2,1,0:T(1,128)}, f32[1,1,2048]{2,1,0:T(1,128)S(1)}, u32[]{:S(2)}) copy-start(f32[1,1,2048]{2,1,0:T(1,128)S(1)} %get-tuple-element.176) | copy-start | bytes 24580
  18.9 834.6 %copy-start.91 = (f32[1,1,2048]{2,1,0:T(1,128)}, f32[1,1,2048]{2,1,0:T(1,128)S(1)}, u32[]{:S(2)}) copy-start(f32[1,1,2048]{2,1,0:T(1,128)S(1)} %get-tuple-element.172) | copy-start | bytes 24580
  18.9 892.3 %copy-start.86 = (f32[1,1,2048]{2,1,0:T(1,128)}, f32[1,1,2048]{2,1,0:T(1,128)S(1)}, u32[]{:S(2)}) copy-start(f32[1,1,2048]{2,1,0:T(1,128)S(1)} %get-tuple-element.171) | copy-start | bytes 24580
  18.9 892.3 %copy-start.88 = (f32[1,1,2048]{2,1,0:T(1,128)}, f32[1,1,2048]{2,1,0:T(1,128)S(1)}, u32[]{:S(2)}) copy-start(f32[1,1,2048]{2,1,0:T(1,128)S(1)} %get-tuple-element.174) | copy-start | bytes 24580
  268.0 250.6 %all-gather.13.cloned.1.call-start = ((), (), s32[]{:S(2)}) async-start(), calls=%async_computation.13 | async-start | bytes 18874368 | tf_op jit(solution)/shard_map/all_gather | solution.py:245
  268.6 478.1 %all-gather.15.cloned.1.call-start = ((), (), s32[]{:S(2)}) async-start(), calls=%async_computation.14 | async-start | bytes 18874368 | tf_op jit(solution)/shard_map/all_gather | solution.py:246
  269.2 509.3 %all-reduce.17.cloned.1.call-start = ((), (), s32[]{:S(2)}) async-start(), calls=%async_computation.2 | async-start | bytes 4194304 | tf_op jit(solution)/shard_map/psum | solution.py:100
  758.9 94.5 %all-reduce.19.cloned.1.call-start = ((), (), s32[]{:S(2)}) async-start(), calls=%async_computation.3 | async-start | bytes 4194304 | tf_op jit(solution)/shard_map/psum | solution.py:95
  781.8 26.5 %collective-permute-start = (bf16[256,2048]{1,0:T(8,128)(2,1)S(1)}, bf16[256,2048]{1,0:T(8,128)(2,1)S(1)}, u32[]{:S(2)}, u32[]{:S(2)}) collective-permute-start(bf16[256,2048]{1,0:T(8,128)(2,1)S(1)} %get-tuple-element.148), channel_id=1, source_target_pairs={{0,16},{1,17},{2,18},{3,19},{4,20},{5,21},{6,22},{7,23},{8,24},{9,... | collective-permute-start | bytes 3145736 | tf_op jit(solution)/shard_map/ppermute | solution.py:18
  830.1 81.0 %all-reduce.21.cloned.1.call-start = ((), (), s32[]{:S(2)}) async-start(), calls=%async_computation.4 | async-start | bytes 4194304 | tf_op jit(solution)/shard_map/psum | solution.py:100
  888.6 99.1 %all-reduce.23.cloned.1.call-start = ((), (), s32[]{:S(2)}) async-start(), calls=%async_computation.5 | async-start | bytes 4194304 | tf_op jit(solution)/shard_map/psum | solution.py:95
  914.4 26.6 %collective-permute-start.1 = (bf16[256,2048]{1,0:T(8,128)(2,1)S(1)}, bf16[256,2048]{1,0:T(8,128)(2,1)S(1)}, u32[]{:S(2)}, u32[]{:S(2)}) collective-permute-start(bf16[256,2048]{1,0:T(8,128)(2,1)S(1)} %get-tuple-element.150), channel_id=1, source_target_pairs={{0,16},{1,17},{2,18},{3,19},{4,20},{5,21},{6,22},{7,23},{8,24},{9,... | collective-permute-start | bytes 3145736 | tf_op jit(solution)/shard_map/ppermute | solution.py:18
  964.4 111.3 %all-reduce.25.cloned.1.call-start = ((), (), s32[]{:S(2)}) async-start(), calls=%async_computation.6 | async-start | bytes 4194304 | tf_op jit(solution)/shard_map/psum | solution.py:140
  1053.2 73.5 %all-reduce.27.cloned.1.call-start = ((), (), s32[]{:S(2)}) async-start(), calls=%async_computation.7 | async-start | bytes 4194304 | tf_op jit(solution)/shard_map/psum | solution.py:189
  1104.1 113.8 %all-reduce.29.cloned.1.call-start = ((), (), s32[]{:S(2)}) async-start(), calls=%async_computation.8 | async-start | bytes 4194304 | tf_op jit(solution)/shard_map/psum | solution.py:140
  1134.0 27.5 %collective-permute-start.2 = (bf16[256,2048]{1,0:T(8,128)(2,1)}, bf16[256,2048]{1,0:T(8,128)(2,1)}, u32[]{:S(2)}, u32[]{:S(2)}) collective-permute-start(bf16[256,2048]{1,0:T(8,128)(2,1)} %get-tuple-element.125), channel_id=1, source_target_pairs={{16,0},{17,1},{18,2},{19,3},{20,4},{21,5},{22,6},{23,7},{24,8},{25... | collective-permute-start | bytes 3145736 | tf_op jit(solution)/shard_map/ppermute | solution.py:18
  1196.1 82.7 %all-reduce.31.cloned.1.call-start = ((), (), s32[]{:S(2)}) async-start(), calls=%async_computation.9 | async-start | bytes 4194304 | tf_op jit(solution)/shard_map/psum | solution.py:189
  1256.3 115.2 %all-reduce.33.cloned.1.call-start = ((), (), s32[]{:S(2)}) async-start(), calls=%async_computation.10 | async-start | bytes 4194304 | tf_op jit(solution)/shard_map/psum | solution.py:140
  1287.1 27.3 %collective-permute-start.3 = (bf16[256,2048]{1,0:T(8,128)(2,1)S(1)}, bf16[256,2048]{1,0:T(8,128)(2,1)S(1)}, u32[]{:S(2)}, u32[]{:S(2)}) collective-permute-start(bf16[256,2048]{1,0:T(8,128)(2,1)S(1)} %get-tuple-element.127), channel_id=1, source_target_pairs={{16,0},{17,1},{18,2},{19,3},{20,4},{21,5},{22,6},{23,7},{24,8},{25... | collective-permute-start | bytes 3145736 | tf_op jit(solution)/shard_map/ppermute | solution.py:18
  1346.0 112.9 %all-reduce.35.cloned.1.call-start = ((), (), s32[]{:S(2)}) async-start(), calls=%async_computation.16 | async-start | bytes 8388608 | tf_op jit(solution)/shard_map/psum | solution.py:100
  1407.0 900.1 %reduce-scatter.4.cloned.1.call-start = ((), (), s32[]{:S(2)}) async-start(), calls=%async_computation.15 | async-start | bytes 56623104
  (164 other events, 6265.1 us)
Sparse Core Ops, SparseCore 0:
  10.2 179.1 all-gather.8
  191.5 71.5 all-gather.10
  268.1 19.4 all-reduce.14
  289.8 228.7 all-gather.12
  520.8 225.7 all-gather.14
  759.1 19.3 all-reduce.16
  830.2 23.1 all-reduce.18
  888.7 22.3 all-reduce.20
  964.6 23.1 all-reduce.22
  1053.3 22.3 all-reduce.24
  1104.2 22.3 all-reduce.26
  1196.2 21.5 all-reduce.28
  1256.4 22.3 all-reduce.30
  1346.0 21.5 all-reduce.32
  1407.2 28.8 all-reduce.34
  1516.1 790.9 reduce-scatter.3
where the time goes:
time: 2360 us; the launch traced here: 2350 us
  waiting for transfers between devices  1600 us (68%)
  matrix products  349 us (15%)
  other arithmetic  185 us (8%)
  local copies, waits for them, and re-layouts  141 us (6%)
  blocking collectives  41.5 us (2%)
    unnamed x17, waiting for transfers between devices  727 us
    all_gather x1, waiting for transfers between devices, shards(): lax.all_gather(w_fc1[0], 'dp', axis=0, tiled=True)  229 us
    all_gather x1, waiting for transfers between devices, shards(): lax.all_gather(w_fc2[0], 'dp', axis=0, tiled=True)  209 us
    all_gather x1, waiting for transfers between devices, shards(): lax.all_gather(w_qkv[0], 'dp', axis=0, tiled=True)  170 us
    dot_general x12, matrix products, contract_last(): lax.dot_general(left, right, (((1,), (1,)), ((), ())), preferred_element_...  111 us
    ppermute x4, waiting for transfers between devices, from_behind(): return lax.ppermute(block, axis, route)  87.2 us
    dot_general x4, matrix products, row_product(): lax.dot_general(left, right, (((0,), (0,)), ((), ())), preferred_element_...  61 us
    dot_general x3, matrix products, backward_pass(): grad_act = jnp.dot(grad_out, down_full, preferred_element_type=jnp.float32)  58.4 us
  transfers between devices with their start and end apart: 20, of which 18 were waited for; matrix products, arithmetic and copies ran while one was open for 10% of the time, Pallas kernels for 0%

commit v1 on v0

v1 whole, which is shorter than its diff:
```python
import jax
import jax.numpy as jnp
from jax import lax
from jax.sharding import Mesh, PartitionSpec as P

HEADS = 32
HEAD_DIM = 64
GROUP = 256
EPS = 1e-05
BF = jnp.bfloat16
F32 = jnp.float32
DP = ("zh", "zl", "y")


def dot(a, b):
    return jnp.dot(a, b, preferred_element_type=F32)


def dot_t(a, b):
    return lax.dot_general(a, b, (((1,), (1,)), ((), ())), preferred_element_type=F32)


def row_dot(a, b):
    return lax.dot_general(a, b, (((0,), (0,)), ((), ())), preferred_element_type=F32)


def swap(v, axis, offset=1):
    n = lax.axis_size(axis)
    return lax.ppermute(v, axis, [(i, i ^ offset) for i in range(n)])


def pick(v, index, dim):
    return lax.dynamic_index_in_dim(v, index, dim, keepdims=False)


def in_order(mine, other, index, dim):
    first = jnp.where(index == 0, mine, other)
    second = jnp.where(index == 0, other, mine)
    return jnp.stack([first, second], axis=dim)


def normalize(v):
    centred = v - jnp.mean(v, axis=-1, keepdims=True)
    scale = lax.rsqrt(jnp.mean(centred * centred, axis=-1, keepdims=True) + EPS)
    return centred * scale, scale


def gelu_parts(u):
    cdf = 0.5 * (1.0 + lax.erf(u * (0.5**0.5)))
    pdf = jnp.exp(-0.5 * u * u) * 0.3989422804014327
    return u * cdf, cdf + u * pdf


def geometry(segment):
    length = segment.shape[0]
    places = jnp.arange(length, dtype=jnp.int32)
    same_seg = segment[:, None] == segment[None, :]
    starts = jnp.min(jnp.where(same_seg, places[None, :], length), axis=1)
    prompt_len = jnp.sum((segment == 0).astype(jnp.int32))
    position = jnp.where(segment == 0, places, prompt_len + places - starts)
    allowed = (position[None, :] <= position[:, None]) & ((segment[None, :] == 0) | same_seg)
    offset = (position[:, None] - position[None, :]).astype(F32)
    return offset, allowed


def gather_weights(own, s, zh, zl, y):
    rows, _, c = own.shape
    outer = lax.axis_size("zh")
    halves = own.reshape(rows, 2, 2, c)
    kept = pick(halves, s, 1)
    recv = swap(pick(halves, 1 - s, 1), "s")
    out = []
    for layer in range(2):
        mine = jnp.where(s == layer, kept, recv)
        a = in_order(pick(mine, zl, 1), swap(pick(mine, 1 - zl, 1), "zl"), zl, 0)
        pieces = [a] + [swap(a, "zh", k) for k in range(1, outer)]
        pieces = jnp.stack([jnp.stack([p, swap(p, "y")]) for p in pieces])
        full = jnp.stack(
            [jnp.stack([pick(pick(pieces, zh ^ i, 0), y ^ j, 0) for j in range(2)], axis=1) for i in range(outer)]
        )
        out.append(full.reshape(outer * 4 * rows, c))
    return out


def scatter_grads(grads, s, zh, zl, y):
    outer = lax.axis_size("zh")
    c = grads[0].shape[1]
    rows = grads[0].shape[0] // (outer * 4)
    quarters = []
    for g in grads:
        v = g.reshape(outer, 2, 2, rows, c)
        v = pick(v, y, 2).astype(F32) + swap(pick(v, 1 - y, 2), "y").astype(F32)
        total = pick(v, zh, 0)
        v = v.astype(BF)
        for k in range(1, outer):
            total = total + swap(pick(v, zh ^ k, 0), "zh", k).astype(F32)
        total = total.astype(BF)
        quarters.append(in_order(pick(total, zl, 0), swap(pick(total, 1 - zl, 0), "zl"), zl, 1))
    mine = jnp.where(s == 0, quarters[0], quarters[1])
    other = jnp.where(s == 0, quarters[1], quarters[0])
    return in_order(mine, swap(other, "s"), s, 1).reshape(rows, 4, c).astype(F32)


def shards(x_in, cotangent, layout, w_qkv, b_qv, w_out, w_fc1, b_fc1, w_fc2, gains, biases):
    s, zh, zl, y, t = (lax.axis_index(a) for a in ("s", "zh", "zl", "y", "t"))
    mb, rows_mb, width = x_in.shape
    wrows = w_out.shape[1]
    block = w_out.shape[2]
    hid = w_fc1.shape[2]
    cq, hq = block // 4, hid // 4
    groups = mb * rows_mb // GROUP
    total_rows = 2 * mb * rows_mb
    share = rows_mb // 4

    att_own = jnp.concatenate(
        [w_qkv[0].reshape(wrows, 3, 4, cq).transpose(0, 2, 1, 3).reshape(wrows, 4, 3 * cq), w_out[0].reshape(wrows, 4, cq)],
        axis=2,
    )
    ff_own = jnp.concatenate([w_fc1[0].reshape(wrows, 4, hq), w_fc2[0].reshape(wrows, 4, hq)], axis=2)
    w_att = gather_weights(att_own, s, zh, zl, y)
    w_ff = gather_weights(ff_own, s, zh, zl, y)

    small_sizes = (2 * block, hid, 2 * width, 4 * width)
    small = jnp.concatenate([b_qv[0].reshape(-1), b_fc1[0], gains[0].reshape(-1), biases[0].reshape(-1)])
    small_other = swap(small, "s")
    params = []
    for layer in range(2):
        v = jnp.where(s == layer, small, small_other)
        a, b, c, d = jnp.split(v, [small_sizes[0], sum(small_sizes[:2]), sum(small_sizes[:3])])
        quarter = s * 2 + zl
        params.append(
            (
                pick(a.reshape(2, 4, cq), quarter, 1),
                pick(b.reshape(4, hq), quarter, 0),
                c.reshape(2, width),
                d.reshape(4, width),
            )
        )

    def from_pair(v):
        half = v.shape[-1] // 2
        part = lax.dynamic_slice_in_dim(v, t * half, half, v.ndim - 1)
        got = swap(part, "zl")
        other = swap(got, "t")
        other = jnp.where(t == 0, jnp.concatenate([got, other], -1), jnp.concatenate([other, got], -1))
        return in_order(v, other, zl, 0)

    x0 = from_pair(x_in)
    cot = from_pair(cotangent)
    segments = in_order(layout, swap(layout, "zl"), zl, 0).reshape(-1, GROUP)
    offset, allowed = jax.vmap(geometry)(segments)
    local_heads = cq // HEAD_DIM
    head_ids = t * (block // HEAD_DIM) + (s * 2 + zl) * local_heads + jnp.arange(local_heads, dtype=jnp.int32)
    slopes = jnp.exp2(-8.0 * (head_ids + 1).astype(F32) / HEADS)
    score_scale = float(HEAD_DIM) ** -0.5

    def own_rows(v):
        v = pick(v.reshape(2, mb, 2, 2, share, width), zl, 0)
        return pick(pick(v, s, 1), t, 1).astype(F32)

    def reduce_rows(p):
        v = p.reshape(2, mb, 2, 2, share, width)
        v = pick(v, t, 3) + swap(pick(v, 1 - t, 3).astype(BF), "t").astype(F32)
        v = pick(v, s, 2) + swap(pick(v, 1 - s, 2).astype(BF), "s").astype(F32)
        return pick(v, zl, 0) + swap(pick(v, 1 - zl, 0).astype(BF), "zl").astype(F32)

    def spread_local(v):
        v = in_order(v, swap(v, "s"), s, 1)
        return in_order(v, swap(v, "t"), t, 2)

    def spread_rows(v):
        v = in_order(v, swap(v, "zl"), zl, 0)
        v = in_order(v, swap(v, "s"), s, 2)
        return in_order(v, swap(v, "t"), t, 3).reshape(total_rows, width)

    def heads_of(v):
        return v.reshape(2 * groups, GROUP, local_heads, HEAD_DIM)

    def scores_of(q, k):
        sc = jnp.einsum("gqhd,gkhd->ghqk", heads_of(q), heads_of(k), preferred_element_type=F32) * score_scale
        sc = sc - slopes[None, :, None, None] * offset[:, None]
        return jnp.where(allowed[:, None], sc, -1000000000.0)

    def forward(x, layer):
        b_q, b_up, gain, shift = params[layer]
        wa, wf = w_att[layer], w_ff[layer]
        xf = x.reshape(total_rows, width).astype(F32)
        vh, _ = normalize(xf)
        normed = (vh * gain[0] + shift[0]).astype(BF)
        proj = dot(normed, wa[:, : 3 * cq])
        q = (proj[:, :cq] + b_q[0]).astype(BF)
        k = proj[:, cq : 2 * cq].astype(BF)
        v = (proj[:, 2 * cq :] + b_q[1]).astype(BF)
        sc = scores_of(q, k)
        top = jnp.max(sc, axis=-1, keepdims=True)
        lifted = jnp.exp(sc - top)
        total = jnp.sum(lifted, axis=-1, keepdims=True)
        probs = (lifted / total).astype(BF)
        log_total = top + jnp.log(total)
        mixed = jnp.einsum("ghqk,gkhd->gqhd", probs, heads_of(v), preferred_element_type=F32)
        mixed = mixed.reshape(total_rows, cq).astype(BF)
        branch = reduce_rows(dot_t(mixed, wa[:, 3 * cq :]))
        hidden = own_rows(x) + branch + shift[2]
        vh2, _ = normalize(hidden)
        normed_two = spread_rows((vh2 * gain[1] + shift[1]).astype(BF))
        upward = dot(normed_two, wf[:, :hq]) + b_up
        act = gelu_parts(upward)[0].astype(BF)
        down = reduce_rows(dot_t(act, wf[:, hq:]))
        result = (hidden + down + shift[3]).astype(BF)
        return result, (x, normed, q, k, v, mixed, log_total, hidden, normed_two, upward, act)

    out0, stash0 = forward(x0, 0)
    x1 = spread_rows(out0)
    out1, stash1 = forward(x1, 1)
    sec0 = pick(x1.reshape(2, mb, rows_mb, width), zl, 0)
    sec1 = spread_local(out1).reshape(mb, rows_mb, width)
    section_outputs = jnp.where(s == 0, sec0, sec1)[None]

    def ln_back(e, v, gain):
        vh, r = normalize(v)
        f = e * gain
        grad = r * (f - jnp.mean(f, -1, keepdims=True) - vh * jnp.mean(f * vh, -1, keepdims=True))
        return grad, jnp.sum(e * vh, (0, 1)), jnp.sum(e, (0, 1))

    def backward(g, stash, layer):
        b_q, b_up, gain, shift = params[layer]
        wa, wf = w_att[layer], w_ff[layer]
        x, normed, q, k, v, mixed, log_total, hidden, normed_two, upward, act = stash
        g = g.reshape(total_rows, width)
        g_own = own_rows(g)
        slope_up = gelu_parts(upward)[1]
        grad_up = (dot(g, wf[:, hq:]) * slope_up).astype(BF)
        e2 = reduce_rows(dot_t(grad_up, wf[:, :hq]))
        terms_ff = jnp.concatenate([row_dot(normed_two, grad_up), row_dot(g, act)], axis=1).astype(BF)
        grad_ln2, gain2, shift2 = ln_back(e2, hidden, gain[1])
        grad_hidden = g_own + grad_ln2
        grad_branch = spread_rows(grad_hidden.astype(BF))
        grad_mixed = dot(grad_branch, wa[:, 3 * cq :]).astype(BF)
        probs = jnp.exp(scores_of(q, k) - log_total)
        gm = heads_of(grad_mixed)
        grad_probs = jnp.einsum("gqhd,gkhd->ghqk", gm, heads_of(v), preferred_element_type=F32)
        grad_v = jnp.einsum("ghqk,gqhd->gkhd", probs.astype(BF), gm, preferred_element_type=F32)
        centre = jnp.sum(probs * grad_probs, axis=-1, keepdims=True)
        grad_sc = (probs * (grad_probs - centre)).astype(BF)
        grad_q = jnp.einsum("ghqk,gkhd->gqhd", grad_sc, heads_of(k), preferred_element_type=F32) * score_scale
        grad_k = jnp.einsum("ghqk,gqhd->gkhd", grad_sc, heads_of(q), preferred_element_type=F32) * score_scale
        grad_proj = jnp.concatenate([a.reshape(total_rows, cq).astype(BF) for a in (grad_q, grad_k, grad_v)], axis=1)
        e1 = reduce_rows(dot_t(grad_proj, wa[:, : 3 * cq]))
        terms_att = jnp.concatenate([row_dot(normed, grad_proj), row_dot(grad_branch, mixed)], axis=1).astype(BF)
        grad_ln1, gain1, shift1 = ln_back(e1, own_rows(x), gain[0])
        grad_in = (grad_hidden + grad_ln1).astype(BF)
        rows_small = jnp.stack([gain1, gain2, shift1, shift2, jnp.sum(grad_hidden, (0, 1)), jnp.sum(g_own, (0, 1))])
        sums = jnp.sum(grad_proj.astype(F32), 0)
        cols_small = (jnp.stack([sums[:cq], sums[2 * cq :]]), jnp.sum(grad_up.astype(F32), 0))
        return grad_in, terms_att, terms_ff, rows_small, cols_small

    gin1, ta1, tf1, rs1, cs1 = backward(cot, stash1, 1)
    g0 = spread_rows(gin1)
    gin0, ta0, tf0, rs0, cs0 = backward(g0, stash0, 0)
    grad_ff = scatter_grads((tf0, tf1), s, zh, zl, y)
    grad_att = scatter_grads((ta0, ta1), s, zh, zl, y)
    in1 = pick(g0.reshape(2, mb, rows_mb, width), zl, 0)
    in0 = spread_local(gin0).reshape(mb, rows_mb, width)
    input_grads = jnp.where(s == 0, in0, in1)[None]

    pieces = []
    for rs, (cqv, cup) in ((rs0, cs0), (rs1, cs1)):
        place = (t * 4 + s * 2 + zl).astype(jnp.int32)
        wide_qv = lax.dynamic_update_slice(jnp.zeros((2, 8, cq), F32), cqv[:, None], (0, place, 0))
        wide_up = lax.dynamic_update_slice(jnp.zeros((8, hq), F32), cup[None], (place, 0))
        pieces.append(jnp.concatenate([rs.reshape(-1), wide_qv.reshape(-1), wide_up.reshape(-1)]))
    total = lax.psum(jnp.stack(pieces), ("s", "zh", "zl", "y", "t"))
    total = pick(total, s, 0)
    grad_gains = total[: 2 * width].reshape(1, 2, width)
    grad_biases = total[2 * width : 6 * width].reshape(1, 4, width)
    grad_b_qv = pick(total[6 * width : 6 * width + 16 * cq].reshape(1, 2, 2, 4 * cq), t, 2)
    grad_b_fc1 = pick(total[6 * width + 16 * cq :].reshape(1, 2, 4 * hq), t, 1)

    g_qkv = grad_att[:, :, : 3 * cq].reshape(wrows, 4, 3, cq).transpose(0, 2, 1, 3).reshape(1, wrows, 3, block)
    g_out = grad_att[:, :, 3 * cq :].reshape(1, wrows, block)
    g_fc1 = grad_ff[:, :, :hq].reshape(1, wrows, hid)
    g_fc2 = grad_ff[:, :, hq:].reshape(1, wrows, hid)
    return section_outputs, input_grads, g_qkv, grad_b_qv, g_out, g_fc1, grad_b_fc1, g_fc2, grad_gains, grad_biases


def solution(mesh):
    n_s, n_dp, n_t = mesh.shape["section"], mesh.shape["dp"], mesh.shape["tensor"]
    fine = Mesh(mesh.devices.reshape(n_s, n_dp // 4, 2, 2, n_t), ("s", "zh", "zl", "y", "t"))
    return jax.shard_map(
        shards,
        mesh=fine,
        in_specs=(
            P(None, DP, None),
            P(None, DP, None),
            P(None, DP),
            P("s", DP, None, "t"),
            P("s", None, "t"),
            P("s", DP, "t"),
            P("s", DP, "t"),
            P("s", "t"),
            P("s", DP, "t"),
            P("s", None, None),
            P("s", None, None),
        ),
        out_specs=(
            P("s", None, DP, None),
            P("s", None, DP, None),
            P("s", DP, None, "t"),
            P("s", None, "t"),
            P("s", DP, "t"),
            P("s", DP, "t"),
            P("s", "t"),
            P("s", DP, "t"),
            P("s", None, None),
            P("s", None, None),
        ),
        check_vma=False,
    )
```

time: 2360 us -> 1780 us (0.75)
  waiting for transfers between devices: 1600 us -> 1070 us
  matrix products: 349 us -> 138 us
  local copies, waits for them, and re-layouts: 141 us -> 257 us
  starting transfers between devices: 13.7 us -> 74.4 us
  blocking collectives: 41.5 us -> 0 us
    ppermute x4 -> x84, waiting for transfers between devices: 87.2 us -> 962 us  [swap(): return lax.ppermute(v, axis, [(i, i ^ offset) for i in range(n)])]
    unnamed x17 -> x1, waiting for transfers between devices: 727 us -> 0.02 us
    all_gather x4 -> x0, waiting for transfers between devices: 647 us -> none  [the longest x1 229 us: shards(): lax.all_gather(w_fc1[0], 'dp', axis=0, tiled=True)]
    dot_general x49 -> x36, matrix products: 349 us -> 138 us  [the longest x8 41.3 us: row_dot(): lax.dot_general(a, b, (((0,), (0,)), ((), ())), preferred_element_type=F32)]
    ppermute x4 -> x84, starting transfers between devices: 10.6 us -> 74.3 us  [swap(): return lax.ppermute(v, axis, [(i, i ^ offset) for i in range(n)])]
    another operation x14 -> x85, other arithmetic: 34.3 us -> 95.9 us  [the longest x58 48.6 us: in_order(): return jnp.stack([first, second], axis=dim)]
    reduce_sum x36 -> x22, other arithmetic: 69.2 us -> 18.8 us  [the longest x4 6.13 us: ln_back(): return (grad, jnp.sum(e * vh, (0, 1)), jnp.sum(e, (0, 1)))]
    dot_general x0 -> x7, local copies, waits for them, and re-layouts: none -> 45.4 us  [row_dot(): lax.dot_general(a, b, (((0,), (0,)), ((), ())), preferred_element_type=F32)]
  transfers between devices with their start and end apart: 20 -> 85, of which waited for: 18 -> 49; matrix products, arithmetic and copies ran while one was open for 10% -> 23% of each run, Pallas kernels for 0% -> 0%
where the time goes in v1:
time: 1780 us; the launch traced here: 1770 us
  waiting for transfers between devices  1070 us (60%)
  local copies, waits for them, and re-layouts  257 us (14%)
  other arithmetic  208 us (12%)
  matrix products  138 us (8%)
  starting transfers between devices  74.4 us (4%)
    ppermute x84, waiting for transfers between devices, swap(): return lax.ppermute(v, axis, [(i, i ^ offset) for i in range(n)])  962 us
    psum x1, waiting for transfers between devices, shards(): total = lax.psum(jnp.stack(pieces), ('s', 'zh', 'zl', 'y', 't'))  111 us
    ppermute x84, starting transfers between devices, swap(): return lax.ppermute(v, axis, [(i, i ^ offset) for i in range(n)])  74.3 us
    unnamed x344, local copies, waits for them, and re-layouts  72.9 us
    another operation x58, other arithmetic, in_order(): return jnp.stack([first, second], axis=dim)  48.6 us
    dot_general x7, local copies, waits for them, and re-layouts, row_dot(): lax.dot_general(a, b, (((0,), (0,)), ((), ())), preferred_element_type=F32)  45.4 us
    dot_general x8, matrix products, row_dot(): lax.dot_general(a, b, (((0,), (0,)), ((), ())), preferred_element_type=F32)  41.3 us
    dot_general x8, matrix products, dot_t(): lax.dot_general(a, b, (((1,), (1,)), ((), ())), preferred_element_type=F32)  37.3 us
  transfers between devices with their start and end apart: 85, of which 49 were waited for; matrix products, arithmetic and copies ran while one was open for 23% of the time, Pallas kernels for 0%

profile of v1, /device:TPU:0, one launch (start us, length us, event | category | flops | bytes accessed | tf_op | source)
XLA Modules:
  0.0 1769.4 jit_solution(9045890458418376528)
XLA Ops:
  29.0 20.3 %collective-permute-done.3 = bf16[256,2,1024]{2,0,1:T(8,128)(2,1)} collective-permute-done((bf16[256,2,1024]{2,0,1:T(8,128)(2,1)}, bf16[256,2,1024]{2,0,1:T(8,128)(2,1)}, u32[]{:S(2)}, u32[]{:S(2)}) %collective-permute-start.3) | collective-permute-done | bytes 1048608 | tf_op jit(solution)/shard_map/ppermute | solution.py:29
  74.0 37.0 %collective-permute-done.6 = bf16[2,256,1024]{2,1,0:T(8,128)(2,1)S(1)} collective-permute-done((bf16[2,256,1024]{2,1,0:T(8,128)(2,1)S(1)}, bf16[2,256,1024]{2,1,0:T(8,128)(2,1)S(1)}, u32[]{:S(2)}, u32[]{:S(2)}) %collective-permute-start.6) | collective-permute-done | bytes 1048608 | tf_op jit(solution)/shard_map/ppermute | solution.py:29
  114.0 21.4 %collective-permute-done.7 = bf16[2,256,1024]{2,1,0:T(8,128)(2,1)S(1)} collective-permute-done((bf16[2,256,1024]{2,1,0:T(8,128)(2,1)S(1)}, bf16[2,256,1024]{2,1,0:T(8,128)(2,1)S(1)}, u32[]{:S(2)}, u32[]{:S(2)}) %collective-permute-start.7) | collective-permute-done | bytes 1048608 | tf_op jit(solution)/shard_map/ppermute | solution.py:29
  198.6 38.8 %collective-permute-done.15 = bf16[256,2,2048]{2,0,1:T(8,128)(2,1)} collective-permute-done((bf16[256,2,2048]{2,0,1:T(8,128)(2,1)}, bf16[256,2,2048]{2,0,1:T(8,128)(2,1)}, u32[]{:S(2)}, u32[]{:S(2)}) %collective-permute-start.15) | collective-permute-done | bytes 2097184 | tf_op jit(solution)/shard_map/ppermute | solution.py:29
  287.9 43.1 %collective-permute-done.12 = bf16[2,64,2048]{2,1,0:T(8,128)(2,1)S(1)} collective-permute-done((bf16[2,64,2048]{2,1,0:T(8,128)(2,1)S(1)}, bf16[2,64,2048]{2,1,0:T(8,128)(2,1)S(1)}, u32[]{:S(2)}, u32[]{:S(2)}) %collective-permute-start.12) | collective-permute-done | bytes 524320 | tf_op jit(solution)/shard_map/ppermute | solution.py:29
  333.8 25.6 %collective-permute-done.18 = bf16[2,256,2048]{2,1,0:T(8,128)(2,1)} collective-permute-done((bf16[2,256,2048]{2,1,0:T(8,128)(2,1)}, bf16[2,256,2048]{2,1,0:T(8,128)(2,1)}, u32[]{:S(2)}, u32[]{:S(2)}) %collective-permute-start.18) | collective-permute-done | bytes 2097184 | tf_op jit(solution)/shard_map/ppermute | solution.py:29
  366.9 36.2 %collective-permute-done.19 = bf16[2,256,2048]{2,1,0:T(8,128)(2,1)} collective-permute-done((bf16[2,256,2048]{2,1,0:T(8,128)(2,1)}, bf16[2,256,2048]{2,1,0:T(8,128)(2,1)}, u32[]{:S(2)}, u32[]{:S(2)}) %collective-permute-start.19) | collective-permute-done | bytes 2097184 | tf_op jit(solution)/shard_map/ppermute | solution.py:29
  444.1 24.7 %collective-permute-done.21 = bf16[2,2,64,2048]{3,2,1,0:T(8,128)(2,1)S(1)} collective-permute-done((bf16[2,2,64,2048]{3,2,1,0:T(8,128)(2,1)S(1)}, bf16[2,2,64,2048]{3,2,1,0:T(8,128)(2,1)S(1)}, u32[]{:S(2)}, u32[]{:S(2)}) %collective-permute-start.21) | collective-permute-done | bytes 1048608 | tf_op jit(solution)/shard_map/ppermute | solution.py:29
  520.8 31.6 %collective-permute-done.28 = bf16[2,256,1024]{2,1,0:T(8,128)(2,1)} collective-permute-done((bf16[2,256,1024]{2,1,0:T(8,128)(2,1)S(1)}, bf16[2,256,1024]{2,1,0:T(8,128)(2,1)}, u32[]{:S(2)}, u32[]{:S(2)}) %collective-permute-start.28) | collective-permute-done | bytes 1048608 | tf_op jit(solution)/shard_map/ppermute | solution.py:29
  554.4 21.6 %collective-permute-done.29 = bf16[2,256,1024]{2,1,0:T(8,128)(2,1)} collective-permute-done((bf16[2,256,1024]{2,1,0:T(8,128)(2,1)}, bf16[2,256,1024]{2,1,0:T(8,128)(2,1)}, u32[]{:S(2)}, u32[]{:S(2)}) %collective-permute-start.29) | collective-permute-done | bytes 1048608 | tf_op jit(solution)/shard_map/ppermute | solution.py:29
  634.7 19.4 %collective-permute-done.36 = bf16[256,2048]{1,0:T(8,128)(2,1)S(1)} collective-permute-done((bf16[256,2048]{1,0:T(8,128)(2,1)S(1)}, bf16[256,2048]{1,0:T(8,128)(2,1)S(1)}, u32[]{:S(2)}, u32[]{:S(2)}) %collective-permute-start.36) | collective-permute-done | bytes 1048608 | tf_op jit(solution)/shard_map/ppermute | solution.py:29
  662.8 49.4 %collective-permute-done.32 = bf16[2,64,2048]{2,1,0:T(8,128)(2,1)S(1)} collective-permute-done((bf16[2,64,2048]{2,1,0:T(8,128)(2,1)S(1)}, bf16[2,64,2048]{2,1,0:T(8,128)(2,1)S(1)}, u32[]{:S(2)}, u32[]{:S(2)}) %collective-permute-start.32) | collective-permute-done | bytes 524320 | tf_op jit(solution)/shard_map/ppermute | solution.py:29
  713.9 27.1 %collective-permute-done.33 = bf16[2,64,2048]{2,1,0:T(8,128)(2,1)S(1)} collective-permute-done((bf16[2,64,2048]{2,1,0:T(8,128)(2,1)S(1)}, bf16[2,64,2048]{2,1,0:T(8,128)(2,1)S(1)}, u32[]{:S(2)}, u32[]{:S(2)}) %collective-permute-start.33) | collective-permute-done | bytes 524320 | tf_op jit(solution)/shard_map/ppermute | solution.py:29
  769.9 21.7 %collective-permute-done.37 = bf16[2,256,2048]{2,1,0:T(8,128)(2,1)S(1)} collective-permute-done((bf16[2,256,2048]{2,1,0:T(8,128)(2,1)S(1)}, bf16[2,256,2048]{2,1,0:T(8,128)(2,1)S(1)}, u32[]{:S(2)}, u32[]{:S(2)}) %collective-permute-start.37) | collective-permute-done | bytes 2097184 | tf_op jit(solution)/shard_map/ppermute | solution.py:29
  792.0 41.6 %collective-permute-done.39 = bf16[2,256,2048]{2,1,0:T(8,128)(2,1)S(1)} collective-permute-done((bf16[2,256,2048]{2,1,0:T(8,128)(2,1)S(1)}, bf16[2,256,2048]{2,1,0:T(8,128)(2,1)S(1)}, u32[]{:S(2)}, u32[]{:S(2)}) %collective-permute-start.39) | collective-permute-done | bytes 2097184 | tf_op jit(solution)/shard_map/ppermute | solution.py:29
  889.4 22.1 %collective-permute-done.48 = bf16[2,2,64,2048]{3,2,1,0:T(8,128)(2,1)S(1)} collective-permute-done((bf16[2,2,64,2048]{3,2,1,0:T(8,128)(2,1)S(1)}, bf16[2,2,64,2048]{3,2,1,0:T(8,128)(2,1)S(1)}, u32[]{:S(2)}, u32[]{:S(2)}) %collective-permute-start.48) | collective-permute-done | bytes 1048608 | tf_op jit(solution)/shard_map/ppermute | solution.py:29
  914.4 19.2 %collective-permute-done.41 = bf16[2,2,64,2048]{3,2,1,0:T(8,128)(2,1)S(1)} collective-permute-done((bf16[2,2,64,2048]{3,2,1,0:T(8,128)(2,1)S(1)}, bf16[2,2,64,2048]{3,2,1,0:T(8,128)(2,1)S(1)}, u32[]{:S(2)}, u32[]{:S(2)}) %collective-permute-start.41) | collective-permute-done | bytes 1048608 | tf_op jit(solution)/shard_map/ppermute | solution.py:29
  964.4 22.7 %collective-permute-done.51 = bf16[2,2,64,2048]{3,2,1,0:T(8,128)(2,1)S(1)} collective-permute-done((bf16[2,2,64,2048]{3,2,1,0:T(8,128)(2,1)S(1)}, bf16[2,2,64,2048]{3,2,1,0:T(8,128)(2,1)S(1)}, u32[]{:S(2)}, u32[]{:S(2)}) %collective-permute-start.51) | collective-permute-done | bytes 1048608 | tf_op jit(solution)/shard_map/ppermute | solution.py:29
  1115.0 35.6 %collective-permute-done.80 = bf16[2,2,256,2048]{3,2,1,0:T(8,128)(2,1)} collective-permute-done((bf16[2,2,256,2048]{3,2,1,0:T(8,128)(2,1)}, bf16[2,2,256,2048]{3,2,1,0:T(8,128)(2,1)}, u32[]{:S(2)}, u32[]{:S(2)}) %collective-permute-start.80) | collective-permute-done | bytes 4194336 | tf_op jit(solution)/shard_map/ppermute | solution.py:29
  1278.8 39.8 %collective-permute-done.77 = bf16[2,2,256,2048]{3,2,1,0:T(8,128)(2,1)} collective-permute-done((bf16[2,2,256,2048]{3,2,1,0:T(8,128)(2,1)}, bf16[2,2,256,2048]{3,2,1,0:T(8,128)(2,1)}, u32[]{:S(2)}, u32[]{:S(2)}) %collective-permute-start.77) | collective-permute-done | bytes 4194336 | tf_op jit(solution)/shard_map/ppermute | solution.py:29
  1353.7 63.5 %collective-permute-done.78 = bf16[2,256,2048]{2,1,0:T(8,128)(2,1)} collective-permute-done((bf16[2,256,2048]{2,1,0:T(8,128)(2,1)}, bf16[2,256,2048]{2,1,0:T(8,128)(2,1)}, u32[]{:S(2)}, u32[]{:S(2)}) %collective-permute-start.78) | collective-permute-done | bytes 2097184 | tf_op jit(solution)/shard_map/ppermute | solution.py:29
  1427.2 19.7 %collective-permute-done.79 = bf16[256,2048]{1,0:T(8,128)(2,1)} collective-permute-done((bf16[256,2048]{1,0:T(8,128)(2,1)}, bf16[256,2048]{1,0:T(8,128)(2,1)}, u32[]{:S(2)}, u32[]{:S(2)}) %collective-permute-start.79) | collective-permute-done | bytes 1048608 | tf_op jit(solution)/shard_map/ppermute | solution.py:29
  1515.1 37.9 %collective-permute-done.70 = bf16[2,2,256,1024]{3,2,1,0:T(8,128)(2,1)} collective-permute-done((bf16[2,2,256,1024]{3,2,1,0:T(8,128)(2,1)S(1)}, bf16[2,2,256,1024]{3,2,1,0:T(8,128)(2,1)}, u32[]{:S(2)}, u32[]{:S(2)}) %collective-permute-start.70) | collective-permute-done | bytes 2097184 | tf_op jit(solution)/shard_map/ppermute | solution.py:29
  1625.3 111.3 %all-reduce.2.cloned.1.call-done = f32[2,24576]{1,0:T(2,128)} async-done(((f32[2,24576]{1,0:T(2,128)}), f32[2,24576]{1,0:T(2,128)}) %all-reduce.2.cloned.1.call-update) | async-done | bytes 196624 | tf_op jit(solution)/shard_map/psum | solution.py:272
  (873 shorter events, 920.5 us)
Async XLA Ops:
  7.2 1729.4 %all-reduce.2.cloned.1.call-start = ((), (), s32[]{:S(2)}) async-start(), calls=%async_computation | async-start | bytes 393216 | tf_op jit(solution)/shard_map/psum | solution.py:272
  64.0 49.8 %collective-permute-start.5 = (bf16[2,256,1024]{2,1,0:T(8,128)(2,1)S(1)}, bf16[2,256,1024]{2,1,0:T(8,128)(2,1)S(1)}, u32[]{:S(2)}, u32[]{:S(2)}) collective-permute-start(bf16[2,256,1024]{2,1,0:T(8,128)(2,1)S(1)} %get-tuple-element.202), channel_id=1, source_target_pairs={{0,2},{2,0},{1,3},{3,1},{4,6},{6,4},{5,7},{7,5},{8,10},{10,8},{9,1... | collective-permute-start | bytes 3145736 | tf_op jit(solution)/shard_map/ppermute | solution.py:29
  197.0 62.3 %collective-permute-start.10 = (bf16[2,2,64,2048]{3,2,1,0:T(8,128)(2,1)S(1)}, bf16[2,2,64,2048]{3,2,1,0:T(8,128)(2,1)S(1)}, u32[]{:S(2)}, u32[]{:S(2)}) collective-permute-start(bf16[2,2,64,2048]{3,2,1,0:T(8,128)(2,1)S(1)} %fusion.174), channel_id=1, source_target_pairs={{0,16},{16,0},{1,17},{17,1},{2,18},{18,2},{3,19},{19,3},{4,20},{20... | collective-permute-start | bytes 3145736 | tf_op jit(solution)/shard_map/ppermute | solution.py:29
  268.9 90.5 %collective-permute-start.18 = (bf16[2,256,2048]{2,1,0:T(8,128)(2,1)}, bf16[2,256,2048]{2,1,0:T(8,128)(2,1)}, u32[]{:S(2)}, u32[]{:S(2)}) collective-permute-start(bf16[2,256,2048]{2,1,0:T(8,128)(2,1)} %get-tuple-element.169), channel_id=1, source_target_pairs={{0,8},{8,0},{1,9},{9,1},{2,10},{10,2},{3,11},{11,3},{4,12},{12,4},... | collective-permute-start | bytes 6291464 | tf_op jit(solution)/shard_map/ppermute | solution.py:29
  287.3 77.5 %collective-permute-start.17 = (bf16[2,256,2048]{2,1,0:T(8,128)(2,1)}, bf16[2,256,2048]{2,1,0:T(8,128)(2,1)}, u32[]{:S(2)}, u32[]{:S(2)}) collective-permute-start(bf16[2,256,2048]{2,1,0:T(8,128)(2,1)} %get-tuple-element.169), channel_id=1, source_target_pairs={{0,2},{2,0},{1,3},{3,1},{4,6},{6,4},{5,7},{7,5},{8,10},{10,8},{9,1... | collective-permute-start | bytes 6291464 | tf_op jit(solution)/shard_map/ppermute | solution.py:29
  364.3 55.8 %collective-permute-start.14 = (bf16[2,2,2,64,2048]{4,3,1,0,2:T(8,128)(2,1)}, bf16[2,2,2,64,2048]{4,3,1,0,2:T(8,128)(2,1)}, u32[]{:S(2)}, u32[]{:S(2)}) collective-permute-start(bf16[2,2,2,64,2048]{4,3,1,0,2:T(8,128)(2,1)} %pad_maximum_fusion.12), channel_id=1, source_target_pairs={{0,1},{1,0},{2,3},{3,2},{4,5},{5,4},{6,7},{7,6},{8,9},{9,8},{10,11... | collective-permute-start | bytes 6291464 | tf_op jit(solution)/shard_map/ppermute | solution.py:29
  520.3 61.8 %collective-permute-start.25 = (bf16[2,2,2,64,2048]{4,3,1,0,2:T(8,128)(2,1)}, bf16[2,2,2,64,2048]{4,3,1,0,2:T(8,128)(2,1)}, u32[]{:S(2)}, u32[]{:S(2)}) collective-permute-start(bf16[2,2,2,64,2048]{4,3,1,0,2:T(8,128)(2,1)} %pad_maximum_fusion.14), channel_id=1, source_target_pairs={{0,1},{1,0},{2,3},{3,2},{4,5},{5,4},{6,7},{7,6},{8,9},{9,8},{10,11... | collective-permute-start | bytes 6291464 | tf_op jit(solution)/shard_map/ppermute | solution.py:29
  633.5 80.3 %collective-permute-start.45 = (bf16[2,256,1024]{2,1,0:T(8,128)(2,1)S(1)}, bf16[2,256,1024]{2,1,0:T(8,128)(2,1)S(1)}, u32[]{:S(2)}, u32[]{:S(2)}) collective-permute-start(bf16[2,256,1024]{2,1,0:T(8,128)(2,1)S(1)} %constant_dynamic-slice_fusion.11), channel_id=1, source_target_pairs={{0,4},{4,0},{1,5},{5,1},{2,6},{6,2},{3,7},{7,3},{8,12},{12,8},{9,1... | collective-permute-start | bytes 3145736 | tf_op jit(solution)/shard_map/ppermute | solution.py:29
  657.4 54.7 %collective-permute-start.32 = (bf16[2,64,2048]{2,1,0:T(8,128)(2,1)S(1)}, bf16[2,64,2048]{2,1,0:T(8,128)(2,1)S(1)}, u32[]{:S(2)}, u32[]{:S(2)}) collective-permute-start(bf16[2,64,2048]{2,1,0:T(8,128)(2,1)S(1)} %fusion.237), channel_id=1, source_target_pairs={{0,4},{4,0},{1,5},{5,1},{2,6},{6,2},{3,7},{7,3},{8,12},{12,8},{9,1... | collective-permute-start | bytes 1572872 | tf_op jit(solution)/shard_map/ppermute | solution.py:29
  658.9 93.4 %collective-permute-start.38 = (bf16[2,256,2048]{2,1,0:T(8,128)(2,1)S(1)}, bf16[2,256,2048]{2,1,0:T(8,128)(2,1)S(1)}, u32[]{:S(2)}, u32[]{:S(2)}) collective-permute-start(bf16[2,256,2048]{2,1,0:T(8,128)(2,1)S(1)} %get-tuple-element.161), channel_id=1, source_target_pairs={{0,8},{8,0},{1,9},{9,1},{2,10},{10,2},{3,11},{11,3},{4,12},{12,4},... | collective-permute-start | bytes 6291464 | tf_op jit(solution)/shard_map/ppermute | solution.py:29
  752.3 81.3 %collective-permute-start.39 = (bf16[2,256,2048]{2,1,0:T(8,128)(2,1)S(1)}, bf16[2,256,2048]{2,1,0:T(8,128)(2,1)S(1)}, u32[]{:S(2)}, u32[]{:S(2)}) collective-permute-start(bf16[2,256,2048]{2,1,0:T(8,128)(2,1)S(1)} %collective-permute-done.38), channel_id=1, source_target_pairs={{0,2},{2,0},{1,3},{3,1},{4,6},{6,4},{5,7},{7,5},{8,10},{10,8},{9,1... | collective-permute-start | bytes 6291464 | tf_op jit(solution)/shard_map/ppermute | solution.py:29
  767.6 80.6 %collective-permute-start.35 = (bf16[2,2,2,64,2048]{4,3,1,0,2:T(8,128)(2,1)}, bf16[2,2,2,64,2048]{4,3,1,0,2:T(8,128)(2,1)}, u32[]{:S(2)}, u32[]{:S(2)}) collective-permute-start(bf16[2,2,2,64,2048]{4,3,1,0,2:T(8,128)(2,1)} %pad_maximum_fusion.15), channel_id=1, source_target_pairs={{0,1},{1,0},{2,3},{3,2},{4,5},{5,4},{6,7},{7,6},{8,9},{9,8},{10,11... | collective-permute-start | bytes 6291464 | tf_op jit(solution)/shard_map/ppermute | solution.py:29
  1057.4 93.2 %collective-permute-start.80 = (bf16[2,2,256,2048]{3,2,1,0:T(8,128)(2,1)}, bf16[2,2,256,2048]{3,2,1,0:T(8,128)(2,1)}, u32[]{:S(2)}, u32[]{:S(2)}) collective-permute-start(bf16[2,2,256,2048]{3,2,1,0:T(8,128)(2,1)} %fusion.23), channel_id=1, source_target_pairs={{0,2},{2,0},{1,3},{3,1},{4,6},{6,4},{5,7},{7,5},{8,10},{10,8},{9,1... | collective-permute-start | bytes 12582920 | tf_op jit(solution)/shard_map/ppermute | solution.py:29
  1155.9 93.8 %collective-permute-start.81 = (bf16[2,256,2048]{2,1,0:T(8,128)(2,1)}, bf16[2,256,2048]{2,1,0:T(8,128)(2,1)}, u32[]{:S(2)}, u32[]{:S(2)}) collective-permute-start(bf16[2,256,2048]{2,1,0:T(8,128)(2,1)} %fusion.73), channel_id=1, source_target_pairs={{0,8},{8,0},{1,9},{9,1},{2,10},{10,2},{3,11},{11,3},{4,12},{12,4},... | collective-permute-start | bytes 6291464 | tf_op jit(solution)/shard_map/ppermute | solution.py:29
  1177.6 80.3 %collective-permute-start.73 = (bf16[2,2,256,1024]{3,2,1,0:T(8,128)(2,1)}, bf16[2,2,256,1024]{3,2,1,0:T(8,128)(2,1)}, u32[]{:S(2)}, u32[]{:S(2)}) collective-permute-start(bf16[2,2,256,1024]{3,2,1,0:T(8,128)(2,1)} %fusion.75), channel_id=1, source_target_pairs={{0,2},{2,0},{1,3},{3,1},{4,6},{6,4},{5,7},{7,5},{8,10},{10,8},{9,1... | collective-permute-start | bytes 6291464 | tf_op jit(solution)/shard_map/ppermute | solution.py:29
  1225.3 93.3 %collective-permute-start.77 = (bf16[2,2,256,2048]{3,2,1,0:T(8,128)(2,1)}, bf16[2,2,256,2048]{3,2,1,0:T(8,128)(2,1)}, u32[]{:S(2)}, u32[]{:S(2)}) collective-permute-start(bf16[2,2,256,2048]{3,2,1,0:T(8,128)(2,1)} %fusion.27), channel_id=1, source_target_pairs={{0,2},{2,0},{1,3},{3,1},{4,6},{6,4},{5,7},{7,5},{8,10},{10,8},{9,1... | collective-permute-start | bytes 12582920 | tf_op jit(solution)/shard_map/ppermute | solution.py:29
  1261.4 68.1 %collective-permute-start.74 = (bf16[2,256,1024]{2,1,0:T(8,128)(2,1)}, bf16[2,256,1024]{2,1,0:T(8,128)(2,1)S(1)}, u32[]{:S(2)}, u32[]{:S(2)}) collective-permute-start(bf16[2,256,1024]{2,1,0:T(8,128)(2,1)} %fusion.183), channel_id=1, source_target_pairs={{0,8},{8,0},{1,9},{9,1},{2,10},{10,2},{3,11},{11,3},{4,12},{12,4},... | collective-permute-start | bytes 3145736 | tf_op jit(solution)/shard_map/ppermute | solution.py:29
  1323.8 93.4 %collective-permute-start.78 = (bf16[2,256,2048]{2,1,0:T(8,128)(2,1)}, bf16[2,256,2048]{2,1,0:T(8,128)(2,1)}, u32[]{:S(2)}, u32[]{:S(2)}) collective-permute-start(bf16[2,256,2048]{2,1,0:T(8,128)(2,1)} %fusion.72), channel_id=1, source_target_pairs={{0,8},{8,0},{1,9},{9,1},{2,10},{10,2},{3,11},{11,3},{4,12},{12,4},... | collective-permute-start | bytes 6291464 | tf_op jit(solution)/shard_map/ppermute | solution.py:29
  1328.1 93.8 %collective-permute-start.82 = (bf16[256,2048]{1,0:T(8,128)(2,1)}, bf16[256,2048]{1,0:T(8,128)(2,1)}, u32[]{:S(2)}, u32[]{:S(2)}) collective-permute-start(bf16[256,2048]{1,0:T(8,128)(2,1)} %dynamic-slice_bitcast_fusion), channel_id=1, source_target_pairs={{0,4},{4,0},{1,5},{5,1},{2,6},{6,2},{3,7},{7,3},{8,12},{12,8},{9,1... | collective-permute-start | bytes 3145736 | tf_op jit(solution)/shard_map/ppermute | solution.py:29
  1332.5 92.3 %collective-permute-start.75 = (bf16[256,1024]{1,0:T(8,128)(2,1)}, bf16[256,1024]{1,0:T(8,128)(2,1)}, u32[]{:S(2)}, u32[]{:S(2)}) collective-permute-start(bf16[256,1024]{1,0:T(8,128)(2,1)} %dynamic-slice_bitcast_fusion.4), channel_id=1, source_target_pairs={{0,4},{4,0},{1,5},{5,1},{2,6},{6,2},{3,7},{7,3},{8,12},{12,8},{9,1... | collective-permute-start | bytes 1572872 | tf_op jit(solution)/shard_map/ppermute | solution.py:29
  1353.7 97.9 %collective-permute-start.64 = (bf16[2,2,2,64,2048]{4,3,1,0,2:T(8,128)(2,1)}, bf16[2,2,2,64,2048]{4,3,1,0,2:T(8,128)(2,1)}, u32[]{:S(2)}, u32[]{:S(2)}) collective-permute-start(bf16[2,2,2,64,2048]{4,3,1,0,2:T(8,128)(2,1)} %pad_maximum_fusion.20), channel_id=1, source_target_pairs={{0,1},{1,0},{2,3},{3,2},{4,5},{5,4},{6,7},{7,6},{8,9},{9,8},{10,11... | collective-permute-start | bytes 6291464 | tf_op jit(solution)/shard_map/ppermute | solution.py:29
  1450.6 55.6 %collective-permute-start.83 = (bf16[256,2,2048]{2,0,1:T(8,128)(2,1)}, bf16[256,2,2048]{2,0,1:T(8,128)(2,1)}, u32[]{:S(2)}, u32[]{:S(2)}) collective-permute-start(bf16[256,2,2048]{2,0,1:T(8,128)(2,1)} %broadcast_select_fusion), channel_id=1, source_target_pairs={{0,16},{16,0},{1,17},{17,1},{2,18},{18,2},{3,19},{19,3},{4,20},{20... | collective-permute-start | bytes 6291464 | tf_op jit(solution)/shard_map/ppermute | solution.py:29
  1612.0 125.7 %collective-permute-start.68 = (bf16[2,64,2048]{2,1,0:T(8,128)(2,1)S(1)}, bf16[2,64,2048]{2,1,0:T(8,128)(2,1)S(1)}, u32[]{:S(2)}, u32[]{:S(2)}) collective-permute-start(bf16[2,64,2048]{2,1,0:T(8,128)(2,1)S(1)} %fusion.166), channel_id=1, source_target_pairs={{0,16},{16,0},{1,17},{17,1},{2,18},{18,2},{3,19},{19,3},{4,20},{20... | collective-permute-start | bytes 1572872 | tf_op jit(solution)/shard_map/ppermute | solution.py:29
  1624.4 118.7 %collective-permute-start.76 = (bf16[256,2,1024]{2,0,1:T(8,128)(2,1)}, bf16[256,2,1024]{2,0,1:T(8,128)(2,1)}, u32[]{:S(2)}, u32[]{:S(2)}) collective-permute-start(bf16[256,2,1024]{2,0,1:T(8,128)(2,1)} %broadcast_select_fusion.6), channel_id=1, source_target_pairs={{0,16},{16,0},{1,17},{17,1},{2,18},{18,2},{3,19},{19,3},{4,20},{20... | collective-permute-start | bytes 3145736 | tf_op jit(solution)/shard_map/ppermute | solution.py:29
  (223 other events, 3943.5 us)
Sparse Core Ops, SparseCore 0:
  1614.1 122.4 all-reduce.1

commit v2 on v1

v2 whole, which is shorter than its diff:
```python
import functools

import jax
import jax.numpy as jnp
from jax import lax
from jax.experimental import pallas as pl
from jax.experimental.pallas import tpu as pltpu
from jax.sharding import Mesh, PartitionSpec as P

HEADS = 32
HEAD_DIM = 64
GROUP = 256
EPS = 1e-05
BF = jnp.bfloat16
F32 = jnp.float32
DP = ("zh", "zl", "y")
MESH = pl.DeviceIdType.MESH
REL = ((1, 1), (0, 1), (1, 0), (0, 0))
CHUNK = 16
FAR = 1e30


def dot(a, b):
    return jnp.dot(a, b, preferred_element_type=F32)


def dot_t(a, b):
    return lax.dot_general(a, b, (((1,), (1,)), ((), ())), preferred_element_type=F32)


def row_dot(a, b):
    return lax.dot_general(a, b, (((0,), (0,)), ((), ())), preferred_element_type=F32)


def normalize(v):
    centred = v - jnp.mean(v, axis=-1, keepdims=True)
    scale = lax.rsqrt(jnp.mean(centred * centred, axis=-1, keepdims=True) + EPS)
    return centred * scale, scale


def geometry(segment):
    length = segment.shape[0]
    places = jnp.arange(length, dtype=jnp.int32)
    same_seg = segment[:, None] == segment[None, :]
    starts = jnp.min(jnp.where(same_seg, places[None, :], length), axis=1)
    prompt_len = jnp.sum((segment == 0).astype(jnp.int32))
    position = jnp.where(segment == 0, places, prompt_len + places - starts)
    allowed = (position[None, :] <= position[:, None]) & ((segment[None, :] == 0) | same_seg)
    offset = (position[:, None] - position[None, :]).astype(F32)
    return jnp.where(allowed, offset, FAR)


class Place:
    def __init__(self):
        self.s, self.zh, self.zl, self.y, self.t = (lax.axis_index(a) for a in ("s", "zh", "zl", "y", "t"))
        self.outer = lax.axis_size("zh")
        self.far = self.outer * 2

    def block(self, zh, zl, y):
        return (zh * 2 + zl) * 2 + y

    def meet(self):
        barrier = pltpu.get_barrier_semaphore()
        others = [{"t": self.t ^ 1}, {"y": self.y ^ 1}]
        others += [{"s": self.s ^ 1, "zl": self.zl ^ k} for k in range(2)]
        others += [{"zh": self.zh ^ (k // 2), "zl": self.zl ^ (k % 2)} for k in range(1, self.far)]
        for other in others:
            pl.semaphore_signal(barrier, inc=1, device_id=other, device_id_type=MESH)
        pl.semaphore_wait(barrier, len(others))


def remote(src, dst, send, recv, **where):
    return pltpu.make_async_remote_copy(
        src_ref=src, dst_ref=dst, send_sem=send, recv_sem=recv, device_id=where, device_id_type=MESH
    )


class Sums:
    def __init__(self, me, part, full, tbuf, rbuf, sems):
        self.me, self.part, self.full, self.tbuf, self.rbuf, self.sems = me, part, full, tbuf, rbuf, sems
        s, zl, t = me.s, me.zl, me.t
        self.core, self.chip = [], []
        for i, (ds, dzl) in enumerate(REL):
            self.core.append(
                remote(part.at[zl ^ dzl, :, s ^ ds, t ^ 1], tbuf.at[i], sems.at[0, i], sems.at[1, i], t=t ^ 1)
            )
        for i, (ds, dzl) in enumerate(REL[:3]):
            self.chip.append(
                remote(
                    part.at[zl ^ dzl, :, s ^ ds, t], rbuf.at[i], sems.at[2, i], sems.at[3, i], s=s ^ ds, zl=zl ^ dzl
                )
            )

    def to_core(self, *which):
        for i in which:
            self.core[i].start()

    def to_chip(self, *which):
        me, part, tbuf = self.me, self.part, self.tbuf
        for i in which:
            ds, dzl = REL[i]
            self.core[i].wait_recv()
            a, b = me.zl ^ dzl, me.s ^ ds
            mb, share = part.shape[1], part.shape[4]

            def add(j, carry, i=i, a=a, b=b, share=share):
                m, r = j // (share // CHUNK), pl.ds(pl.multiple_of((j % (share // CHUNK)) * CHUNK, CHUNK), CHUNK)
                v = part[a, m, b, me.t, r].astype(F32) + tbuf[i, m, r].astype(F32)
                part[a, m, b, me.t, r] = v.astype(BF)
                return carry

            lax.fori_loop(0, mb * share // CHUNK, add, 0)
            self.chip[i].start()

    def finish(self, row_fn):
        me, part, tbuf, rbuf, full = self.me, self.part, self.tbuf, self.rbuf, self.full
        self.core[3].wait_recv()
        for c in self.chip:
            c.wait_recv()
        mb, share = part.shape[1], part.shape[4]

        def add(j, carry):
            m, r = j // (share // CHUNK), pl.ds(pl.multiple_of((j % (share // CHUNK)) * CHUNK, CHUNK), CHUNK)
            v = part[me.zl, m, me.s, me.t, r].astype(F32) + tbuf[3, m, r].astype(F32)
            v = v + rbuf[0, m, r].astype(F32) + rbuf[1, m, r].astype(F32) + rbuf[2, m, r].astype(F32)
            full[me.zl, m, me.s, me.t, r] = row_fn(m, r, v)
            return carry

        lax.fori_loop(0, mb * share // CHUNK, add, 0)
        for c in self.core + self.chip:
            c.wait_send()

    def spread(self):
        me, full, sems = self.me, self.full, self.sems
        own = full.at[me.zl, :, me.s, me.t]
        self.out = [
            remote(own, own, sems.at[4, i], sems.at[5, i], s=me.s ^ ds, zl=me.zl ^ dzl)
            for i, (ds, dzl) in enumerate(REL[:3])
        ]
        for c in self.out:
            c.start()
        self.cross = [None] * 4
        self.forward(3, own)

    def forward(self, i, piece):
        me, sems = self.me, self.sems
        self.cross[i] = remote(piece, piece, sems.at[6, i], sems.at[7, i], t=me.t ^ 1)
        self.cross[i].start()

    def collect(self):
        me, full = self.me, self.full
        for i in (2, 1, 0):
            ds, dzl = REL[i]
            self.out[i].wait_recv()
            self.forward(i, full.at[me.zl ^ dzl, :, me.s ^ ds, me.t])
        for c in self.cross:
            c.wait_recv()
        for c in self.cross + self.out:
            c.wait_send()


def sums_scratch(mb, share, width):
    return [
        pltpu.VMEM((2, mb, 2, 2, share, width), BF),
        pltpu.VMEM((4, mb, share, width), BF),
        pltpu.VMEM((3, mb, share, width), BF),
        pltpu.SemaphoreType.DMA((8, 4)),
    ]


class Fetch:
    def __init__(self, me, layer, pairs, sems):
        self.me, self.pairs = me, pairs
        self.first, self.far, self.near = [], [], []
        home = me.block(me.zh, me.zl, me.y)
        for p, (half, whole) in enumerate(pairs):
            c = whole.shape[-1]
            src = lambda q, half=half, c=c: half.at[layer, :, :, pl.ds(pl.multiple_of(q * c, c), c)]
            dst = whole.at[:, home]
            sem = lambda a, k, p=p: sems.at[p, a, k]
            self.first.append(pltpu.make_async_copy(src(me.zl), dst, sem(4, 0)))
            for k in reversed(range(1, me.far)):
                zh, zl = me.zh ^ (k // 2), me.zl ^ (k % 2)
                self.far.append((p, k, remote(src(zl), dst, sem(0, k), sem(1, k), zh=zh, zl=zl)))
            self.near.append(remote(src(me.zl), dst, sem(2, 0), sem(3, 0), y=me.y ^ 1))
        self.sem = sems

    def start(self):
        for c in self.first:
            c.start()
        for _, _, c in self.far:
            c.start()
        for c in self.near:
            c.start()

    def pass_on(self, lo=0, hi=None):
        me = self.me
        for p, k, c in self.far[lo:hi]:
            c.wait_recv()
            whole = self.pairs[p][1]
            piece = whole.at[:, me.block(me.zh ^ (k // 2), me.zl ^ (k % 2), me.y)]
            on = remote(piece, piece, self.sem.at[p, 2, k], self.sem.at[p, 3, k], y=me.y ^ 1)
            on.start()
            self.near.append(on)

    def finish(self):
        for c in self.first:
            c.wait()
        for _, _, c in self.far:
            c.wait_send()
        for c in self.near:
            c.wait()


def fetch_sems(pairs, far):
    return pltpu.SemaphoreType.DMA((pairs, 5, far))


class Deliver:
    def __init__(self, me, quads, sems):
        self.me, self.quads, self.sems = me, quads, sems
        self.near, self.far = [], []
        for p, (terms, ybuf, zbuf, out) in enumerate(quads):
            for k in reversed(range(me.far)):
                zh, zl = me.zh ^ (k // 2), me.zl ^ (k % 2)
                src = terms.at[:, me.block(zh, zl, me.y ^ 1)]
                self.near.append((p, k, remote(src, ybuf.at[:, k], sems.at[p, 0, k], sems.at[p, 1, k], y=me.y ^ 1)))
                if k:
                    self.far.append(
                        remote(ybuf.at[:, k], zbuf.at[:, k - 1], sems.at[p, 2, k], sems.at[p, 3, k], zh=zh, zl=zl)
                    )

    def start(self):
        for _, _, c in self.near:
            c.start()

    def add(self, lo=0, hi=None):
        me = self.me
        for p, k, c in self.near[lo:hi]:
            terms, ybuf, zbuf, out = self.quads[p]
            c.wait_recv()
            kinds, rows = ybuf.shape[0], ybuf.shape[2]
            b = me.block(me.zh ^ (k // 2), me.zl ^ (k % 2), me.y)

            def step(j, carry, k=k, b=b, rows=rows, terms=terms, ybuf=ybuf):
                m, r = j // (rows // CHUNK), pl.ds(pl.multiple_of((j % (rows // CHUNK)) * CHUNK, CHUNK), CHUNK)
                ybuf[m, k, r] = (ybuf[m, k, r].astype(F32) + terms[m, b, r].astype(F32)).astype(BF)
                return carry

            lax.fori_loop(0, kinds * rows // CHUNK, step, 0)
            if k:
                self.far[p * (me.far - 1) + (me.far - 1 - k)].start()

    def finish(self):
        me = self.me
        for c in self.far:
            c.wait_recv()
        for p, (terms, ybuf, zbuf, out) in enumerate(self.quads):
            kinds, rows, c = ybuf.shape[0], ybuf.shape[2], ybuf.shape[3]

            def step(j, carry, rows=rows, c=c, ybuf=ybuf, zbuf=zbuf, out=out):
                m, r = j // (rows // CHUNK), pl.ds(pl.multiple_of((j % (rows // CHUNK)) * CHUNK, CHUNK), CHUNK)
                same, other = ybuf[m, 0, r].astype(F32), zbuf[m, 0, r].astype(F32)
                for k in range(2, me.far):
                    if k % 2:
                        other = other + zbuf[m, k - 1, r].astype(F32)
                    else:
                        same = same + zbuf[m, k - 1, r].astype(F32)
                out[me.zl, m, r] = same.astype(BF)
                out[me.zl ^ 1, m, r] = other.astype(BF)
                return carry

            lax.fori_loop(0, kinds * rows // CHUNK, step, 0)
        for _, _, c in self.near:
            c.wait_send()
        for c in self.far:
            c.wait_send()


def deliver_sems(pairs, far):
    return pltpu.SemaphoreType.DMA((pairs, 4, far))


VM = pl.BlockSpec(memory_space=pltpu.VMEM)
SM = pl.BlockSpec(memory_space=pltpu.SMEM)
AN = pl.BlockSpec(memory_space=pl.ANY)


def call(body, cid, ins, in_specs, outs, out_specs, scratch, flops=0):
    return pl.pallas_call(
        body,
        out_shape=[jax.ShapeDtypeStruct(sh, dt) for sh, dt in outs],
        in_specs=in_specs,
        out_specs=out_specs,
        scratch_shapes=scratch,
        compiler_params=pltpu.CompilerParams(
            collective_id=cid, has_side_effects=True, vmem_limit_bytes=60 * 1024 * 1024
        ),
    )(*ins)


def fetch_first(qkv, o, up, dn, x_in, cot, qkv_h, o_h, up_h, dn_h, w_qkv, w_o, x_all, c_all, sems, xsems, fsems):
    me = Place()
    me.meet()
    other, jobs = me.s ^ 1, []
    for p, (own, half) in enumerate(((qkv, qkv_h), (o, o_h), (up, up_h), (dn, dn_h))):
        w = own.shape[-1] // 2
        cols = lambda q, w=w: pl.ds(pl.multiple_of(q * w, w), w)
        there = remote(own.at[:, :, cols(other)], half.at[me.s], sems.at[0, p], sems.at[1, p], s=other)
        here = pltpu.make_async_copy(own.at[:, :, cols(me.s)], half.at[me.s], sems.at[2, p])
        there.start()
        here.start()
        jobs.append((there, here))
    moved = []
    for a, (own, full) in enumerate(((x_in, x_all), (cot, c_all))):
        local = pltpu.make_async_copy(own, full.at[me.zl], xsems.at[a, 4])
        across = remote(own.at[:, :, me.t], full.at[me.zl, :, :, me.t], xsems.at[a, 0], xsems.at[a, 1], zl=me.zl ^ 1)
        local.start()
        across.start()
        moved.append([local, across, full])
    for there, here in jobs[:2]:
        here.wait()
        there.wait_recv()
    pack = Fetch(me, 0, ((qkv_h, w_qkv), (o_h, w_o)), fsems)
    pack.start()
    crossed = []
    for a, (local, across, full) in enumerate(moved):
        across.wait_recv()
        piece = full.at[me.zl ^ 1, :, :, me.t]
        c = remote(piece, piece, xsems.at[a, 2], xsems.at[a, 3], t=me.t ^ 1)
        c.start()
        crossed.append(c)
    pack.pass_on()
    pack.finish()
    for there, here in jobs[2:]:
        here.wait()
        there.wait_recv()
    for there, _ in jobs:
        there.wait_send()
    for (local, across, _), c in zip(moved, crossed):
        local.wait()
        across.wait_send()
        c.wait()


def rows_of(ref, a, m):
    v = ref[a, m]
    return v.reshape(-1, v.shape[-1])


def put_rows(ref, a, m, v):
    ref[a, m] = v.reshape(ref.shape[2:])


def group_place(me, i, mb):
    return (me.zl ^ 1) if i < mb else me.zl, i % mb


def norm_rows(src, dst, a, m, gain, shift):
    share = src.shape[4]

    def step(j, carry):
        q, r = j // (share // CHUNK), pl.ds(pl.multiple_of((j % (share // CHUNK)) * CHUNK, CHUNK), CHUNK)
        vh, _ = normalize(src[a, m, q // 2, q % 2, r].astype(F32))
        dst[a, m, q // 2, q % 2, r] = (vh * gain + shift).astype(BF)
        return carry

    lax.fori_loop(0, 4 * share // CHUNK, step, 0)


def lanes(width):
    return lax.broadcasted_iota(jnp.int32, (1, width), 1)


def head_mask(h):
    return (lanes(2 * HEAD_DIM) // HEAD_DIM) == h


def softmax_parts(q, k, pen, slope):
    sc = dot_t(q, k) * (float(HEAD_DIM) ** -0.5) - slope * pen
    lifted = jnp.exp(sc - jnp.max(sc, axis=-1, keepdims=True))
    return lifted / jnp.sum(lifted, axis=-1, keepdims=True)


def att_forward(
    layer, has_fetch, x, wqkv, wo, bias, vecs, slopes, pen, *rest
):
    rest = list(rest)
    n_in = 2 if has_fetch else 0
    halves, rest = rest[:n_in], rest[n_in:]
    normed, proj, mixed, hidden, full = rest[:5]
    wholes, rest = rest[5 : 5 + n_in], rest[5 + n_in :]
    part, tbuf, rbuf, sems = rest[:4]
    me = Place()
    me.meet()
    fetch = None
    if has_fetch:
        fetch = Fetch(me, has_fetch[0], tuple(zip(halves, wholes)), rest[4])
        fetch.start()
    sums = Sums(me, part, full, tbuf, rbuf, sems)
    mb = x.shape[1]
    cq = wo.shape[-1]

    def group(a, m):
        norm_rows(x, normed, a, m, vecs[0:1], vecs[1:2])
        nv = rows_of(normed, a, m)
        for k in range(3):
            v = dot(nv, wqkv[k])
            if k == 0:
                v = v + bias[0:1]
            if k == 2:
                v = v + bias[1:2]
            proj[k, a, m] = v.astype(BF)
        pv = pen[a, m]
        for pair in range(cq // (2 * HEAD_DIM)):
            cols = slice(pair * 2 * HEAD_DIM, (pair + 1) * 2 * HEAD_DIM)
            q, k, v = proj[0, a, m, :, cols], proj[1, a, m, :, cols], proj[2, a, m, :, cols]
            got = []
            for h in range(2):
                probs = softmax_parts(jnp.where(head_mask(h), q, jnp.zeros_like(q)), k, pv, slopes[pair * 2 + h])
                got.append(dot(probs.astype(BF), v))
            mixed[a, m, :, cols] = jnp.where(head_mask(0), got[0], got[1]).astype(BF)
        put_rows(part, a, m, dot_t(mixed[a, m], wo[...]).astype(BF))

    lax.fori_loop(0, mb, lambda m, c: (group(me.zl ^ 1, m), c)[1], 0)
    sums.to_core(0, 1)
    lax.fori_loop(0, mb, lambda m, c: (group(me.zl, m), c)[1], 0)
    sums.to_core(2, 3)
    sums.to_chip(0, 1, 2)
    if fetch:
        fetch.pass_on(0, 3)

    def rows(m, r, v):
        hid = x[me.zl, m, me.s, me.t, r].astype(F32) + v + vecs[4:5]
        hidden[m, r] = hid
        vh, _ = normalize(hid)
        return (vh * vecs[2:3] + vecs[3:4]).astype(BF)

    sums.finish(rows)
    sums.spread()
    sums.collect()
    if fetch:
        fetch.pass_on(3)
        fetch.finish()


def ff_forward(layer, has_fetch, x, wup, wdn, bias, vecs, hidden, *rest):
    rest = list(rest)
    n_in = 2 if has_fetch else 0
    halves, rest = rest[:n_in], rest[n_in:]
    upward, act, full = rest[:3]
    wholes, rest = rest[3 : 3 + n_in], rest[3 + n_in :]
    part, tbuf, rbuf, sems = rest[:4]
    me = Place()
    me.meet()
    fetch = None
    if has_fetch:
        fetch = Fetch(me, has_fetch[0], tuple(zip(halves, wholes)), rest[4])
        fetch.start()
    sums = Sums(me, part, full, tbuf, rbuf, sems)
    mb = x.shape[1]
    hq = wup.shape[-1]
    tile = 512

    def group(a, m):
        nv = rows_of(x, a, m)
        for j in range(hq // tile):
            cols = slice(j * tile, (j + 1) * tile)
            u = dot(nv, wup[:, cols]) + bias[:, cols]
            upward[a, m, :, cols] = u
            act[a, m, :, cols] = (u * (0.5 + 0.5 * lax.erf(u * (0.5**0.5)))).astype(BF)
        put_rows(part, a, m, dot_t(act[a, m], wdn[...]).astype(BF))

    lax.fori_loop(0, mb, lambda m, c: (group(me.zl ^ 1, m), c)[1], 0)
    sums.to_core(0, 1)
    lax.fori_loop(0, mb, lambda m, c: (group(me.zl, m), c)[1], 0)
    sums.to_core(2, 3)
    sums.to_chip(0, 1, 2)
    if fetch:
        fetch.pass_on(0, 3)
    sums.finish(lambda m, r, v: (hidden[m, r] + v + vecs[5:6]).astype(BF))
    sums.spread()
    sums.collect()
    if fetch:
        fetch.pass_on(3)
        fetch.finish()


def ln_back(e, v, gain):
    vh, r = normalize(v)
    f = e * gain
    grad = r * (f - jnp.mean(f, -1, keepdims=True) - vh * jnp.mean(f * vh, -1, keepdims=True))
    return grad, e * vh


def fold(v):
    return v[:8] + v[8:]


def ff_backward(layer, has_deliver, g, normed_two, act, upward, wup, wdn, vecs, hidden, *rest):
    rest = list(rest)
    n_in = has_deliver
    terms, rest = rest[:n_in], rest[n_in:]
    g_up, g_dn, grad_hidden, small, small_up, full = rest[:6]
    outs, rest = rest[6 : 6 + n_in], rest[6 + n_in :]
    part, tbuf, rbuf, sems, gu = rest[:5]
    me = Place()
    me.meet()
    deliver = None
    if n_in:
        bufs = rest[5:]
        deliver = Deliver(me, [(terms[i], bufs[2 * i], bufs[2 * i + 1], outs[i]) for i in range(n_in)], bufs[-1])
        deliver.start()
    sums = Sums(me, part, full, tbuf, rbuf, sems)
    mb = g.shape[1]
    hq = wup.shape[-1]
    tile = 512
    small[...] = jnp.zeros_like(small)
    small_up[...] = jnp.zeros_like(small_up)

    def group(a, m):
        gv = rows_of(g, a, m)
        for j in range(hq // tile):
            cols = slice(j * tile, (j + 1) * tile)
            u = upward[a, m, :, cols]
            slope = 0.5 + 0.5 * lax.erf(u * (0.5**0.5)) + u * (jnp.exp(-0.5 * u * u) * 0.3989422804014327)
            v = (dot(gv, wdn[:, cols]) * slope).astype(BF)
            gu[a, m, :, cols] = v
            small_up[:, cols] += jnp.sum(v.astype(F32).reshape(-1, 8, tile), axis=0)
        put_rows(part, a, m, dot_t(gu[a, m], wup[...]).astype(BF))

    lax.fori_loop(0, mb, lambda m, c: (group(me.zl ^ 1, m), c)[1], 0)
    sums.to_core(0, 1)
    lax.fori_loop(0, mb, lambda m, c: (group(me.zl, m), c)[1], 0)
    sums.to_core(2, 3)
    sums.to_chip(0, 1, 2)

    def flat(ref):
        v = ref[...]
        return v.reshape(-1, v.shape[-1])

    nt = 256
    width = g.shape[-1]

    def product(dst, left, right):
        def step(j, carry):
            cols = pl.ds(pl.multiple_of(j * nt, nt), nt)
            lv = left[:, :, :, :, :, cols].reshape(-1, nt)
            dst[cols] = row_dot(lv, flat(right)).astype(BF)
            return carry

        lax.fori_loop(0, width // nt, step, 0)

    product(g_dn, g, act)

    def rows(m, r, e):
        grad, ev = ln_back(e, hidden[m, r], vecs[2:3])
        go = g[me.zl, m, me.s, me.t, r].astype(F32)
        grad = go + grad
        grad_hidden[m, r] = grad
        small[0] += fold(ev)
        small[1] += fold(e)
        small[2] += fold(grad)
        small[3] += fold(go)
        return grad.astype(BF)

    sums.finish(rows)
    sums.spread()
    if deliver:
        deliver.add()
    product(g_up, normed_two, gu)
    sums.collect()
    if deliver:
        deliver.finish()


def att_backward(
    layer, has_deliver, gb, x, normed, proj, mixed, wqkv, wo, vecs, slopes, pen, grad_hidden, *rest
):
    rest = list(rest)
    n_in = has_deliver
    terms, rest = rest[:n_in], rest[n_in:]
    g_qkv, g_o, small, small_p, full = rest[:5]
    outs, rest = rest[5 : 5 + n_in], rest[5 + n_in :]
    part, tbuf, rbuf, sems, gp = rest[:5]
    me = Place()
    me.meet()
    deliver = None
    if n_in:
        bufs = rest[5:]
        deliver = Deliver(me, [(terms[i], bufs[2 * i], bufs[2 * i + 1], outs[i]) for i in range(n_in)], bufs[-1])
        deliver.start()
    sums = Sums(me, part, full, tbuf, rbuf, sems)
    mb = x.shape[1]
    cq = wo.shape[-1]
    small[...] = jnp.zeros_like(small)
    small_p[...] = jnp.zeros_like(small_p)
    scale = float(HEAD_DIM) ** -0.5

    def group(a, m):
        gm_all = dot(rows_of(gb, a, m), wo[...]).astype(BF)
        pv = pen[a, m]
        for pair in range(cq // (2 * HEAD_DIM)):
            cols = slice(pair * 2 * HEAD_DIM, (pair + 1) * 2 * HEAD_DIM)
            q, k, v = proj[0, a, m, :, cols], proj[1, a, m, :, cols], proj[2, a, m, :, cols]
            gm = gm_all[:, cols]
            gq, gk, gv = [], [], []
            for h in range(2):
                zero = jnp.zeros_like(q)
                probs = softmax_parts(jnp.where(head_mask(h), q, zero), k, pv, slopes[pair * 2 + h])
                gpr = dot_t(jnp.where(head_mask(h), gm, zero), v)
                gv.append(row_dot(probs.astype(BF), gm))
                pg = probs * gpr
                gs = (pg - probs * jnp.sum(pg, axis=-1, keepdims=True)).astype(BF)
                gq.append(dot(gs, k))
                gk.append(row_dot(gs, q))
            for i, (both, f) in enumerate(((gq, scale), (gk, scale), (gv, 1.0))):
                out = (jnp.where(head_mask(0), both[0], both[1]) * f).astype(BF)
                gp[i, a, m, :, cols] = out
                small_p[i, :, cols] += jnp.sum(out.astype(F32).reshape(-1, 8, 2 * HEAD_DIM), axis=0)
        total = dot_t(gp[0, a, m], wqkv[0]) + dot_t(gp[1, a, m], wqkv[1]) + dot_t(gp[2, a, m], wqkv[2])
        put_rows(part, a, m, total.astype(BF))

    lax.fori_loop(0, mb, lambda m, c: (group(me.zl ^ 1, m), c)[1], 0)
    sums.to_core(0, 1)
    lax.fori_loop(0, mb, lambda m, c: (group(me.zl, m), c)[1], 0)
    sums.to_core(2, 3)
    sums.to_chip(0, 1, 2)

    nt = 256
    width = gb.shape[-1]

    def product(dst, left, right):
        def step(j, carry):
            cols = pl.ds(pl.multiple_of(j * nt, nt), nt)
            lv = left[:, :, :, :, :, cols].reshape(-1, nt)
            dst[cols] = row_dot(lv, right()).astype(BF)
            return carry

        lax.fori_loop(0, width // nt, step, 0)

    product(g_o, gb, lambda: mixed[...].reshape(-1, cq))

    def rows(m, r, e):
        grad, ev = ln_back(e, x[me.zl, m, me.s, me.t, r].astype(F32), vecs[0:1])
        small[0] += fold(ev)
        small[1] += fold(e)
        return (grad_hidden[m, r] + grad).astype(BF)

    sums.finish(rows)
    sums.spread()
    if deliver:
        deliver.add()
    for k in range(3):
        product(g_qkv.at[k], normed, lambda k=k: gp[k].reshape(-1, cq))
    sums.collect()
    if deliver:
        deliver.finish()


def deliver_last(n_in, *refs):
    refs = list(refs)
    terms, refs = refs[:n_in], refs[n_in:]
    outs, bufs = refs[:n_in], refs[n_in:]
    me = Place()
    me.meet()
    deliver = Deliver(me, [(terms[i], bufs[2 * i], bufs[2 * i + 1], outs[i]) for i in range(n_in)], bufs[-1])
    deliver.start()
    deliver.add()
    deliver.finish()


def swap(v, axis, offset=1):
    n = lax.axis_size(axis)
    return lax.ppermute(v, axis, [(i, i ^ offset) for i in range(n)])


def pick(v, index, dim):
    return lax.dynamic_index_in_dim(v, index, dim, keepdims=False)


def in_order(mine, other, index, dim):
    first = jnp.where(index == 0, mine, other)
    second = jnp.where(index == 0, other, mine)
    return jnp.stack([first, second], axis=dim)


def shards(x_in, cotangent, layout, w_qkv, b_qv, w_out, w_fc1, b_fc1, w_fc2, gains, biases):
    s, zh, zl, y, t = (lax.axis_index(a) for a in ("s", "zh", "zl", "y", "t"))
    outer = lax.axis_size("zh")
    far, nb = outer * 2, outer * 4
    mb, rows_mb, width = x_in.shape
    wrows = w_out.shape[1]
    block = w_out.shape[2]
    hid = w_fc1.shape[2]
    cq, hq = block // 4, hid // 4
    share = rows_mb // 4
    tokens = (2, mb, 2, 2, share, width)

    small_sizes = (2 * block, hid, 2 * width, 4 * width)
    small = jnp.concatenate([b_qv[0].reshape(-1), b_fc1[0], gains[0].reshape(-1), biases[0].reshape(-1)])
    small_other = swap(small, "s")
    quarter = s * 2 + zl
    params = []
    for layer in range(2):
        v = jnp.where(s == layer, small, small_other)
        a, b, c, d = jnp.split(v, [small_sizes[0], sum(small_sizes[:2]), sum(small_sizes[:3])])
        c, d = c.reshape(2, width), d.reshape(4, width)
        params.append(
            (
                pick(a.reshape(2, 4, cq), quarter, 1),
                pick(b.reshape(4, hq), quarter, 0)[None],
                jnp.stack([c[0], d[0], c[1], d[1], d[2], d[3]]),
            )
        )
    segments = in_order(layout, swap(layout, "zl"), zl, 0).reshape(2 * mb, rows_mb)
    pen = jax.vmap(geometry)(segments).reshape(2, mb, GROUP, GROUP)
    local_heads = cq // HEAD_DIM
    head_ids = t * (block // HEAD_DIM) + quarter * local_heads + jnp.arange(local_heads, dtype=jnp.int32)
    slopes = jnp.exp2(-8.0 * (head_ids + 1).astype(F32) / HEADS)

    qkv_own = w_qkv[0].transpose(1, 0, 2)
    res = call(
        fetch_first,
        0,
        (
            qkv_own,
            w_out,
            w_fc1,
            w_fc2,
            x_in.reshape(mb, 2, 2, share, width),
            cotangent.reshape(mb, 2, 2, share, width),
        ),
        [AN] * 6,
        [
            ((2, 3, wrows, 2 * cq), BF),
            ((2, 1, wrows, 2 * cq), BF),
            ((2, 1, wrows, 2 * hq), BF),
            ((2, 1, wrows, 2 * hq), BF),
            ((3, nb, wrows, cq), BF),
            ((1, nb, wrows, cq), BF),
            (tokens, BF),
            (tokens, BF),
        ],
        [AN] * 8,
        [pltpu.SemaphoreType.DMA((3, 4)), pltpu.SemaphoreType.DMA((2, 5)), fetch_sems(2, far)],
    )
    qkv_h, o_h, up_h, dn_h, wqkv0, wo0, x0, cot = res
    act_scratch = sums_scratch(mb, share, width)
    att_w = [((3, nb, wrows, cq), BF), ((1, nb, wrows, cq), BF)]
    ff_w = [((1, nb, wrows, hq), BF)] * 2

    def att_fwd(layer, cid, x, wqkv, wo):
        bias, _, vecs = params[layer]
        res = call(
            functools.partial(att_forward, layer, (layer,)),
            cid,
            (x, wqkv.reshape(3, width, cq), wo.reshape(width, cq), bias, vecs, slopes, pen, up_h, dn_h),
            [VM] * 5 + [SM, VM] + [AN] * 2,
            [
                (tokens, BF),
                ((3, 2, mb, rows_mb, cq), BF),
                ((2, mb, rows_mb, cq), BF),
                ((mb, share, width), F32),
                (tokens, BF),
            ]
            + ff_w,
            [VM] * 5 + [AN] * 2,
            act_scratch + [fetch_sems(2, far)],
        )
        return res

    def ff_fwd(layer, cid, nt, wup, wdn, hidden, nxt):
        _, bias, vecs = params[layer]
        ins = [nt, wup.reshape(width, hq), wdn.reshape(width, hq), bias, vecs, hidden]
        outs = [((2, mb, rows_mb, hq), F32), ((2, mb, rows_mb, hq), BF), (tokens, BF)]
        sp, so = [VM] * 6, [VM] * 3
        scratch = list(act_scratch)
        if nxt is not None:
            ins += [qkv_h, o_h]
            sp += [AN] * 2
            outs += att_w
            so += [AN] * 2
            scratch.append(fetch_sems(2, far))
        return call(
            functools.partial(ff_forward, layer, None if nxt is None else (nxt,)), cid, ins, sp, outs, so, scratch
        )

    normed0, proj0, mixed0, hidden0, nt0, wup0, wdn0 = att_fwd(0, 1, x0, wqkv0, wo0)
    upward0, act0, x1, wqkv1, wo1 = ff_fwd(0, 2, nt0, wup0, wdn0, hidden0, 1)
    normed1, proj1, mixed1, hidden1, nt1, wup1, wdn1 = att_fwd(1, 3, x1, wqkv1, wo1)
    upward1, act1, x2 = ff_fwd(1, 4, nt1, wup1, wdn1, hidden1, None)

    def deliver_parts(shapes):
        scratch = []
        for k, c in shapes:
            scratch += [pltpu.VMEM((k, far, wrows, c), BF), pltpu.VMEM((k, far - 1, wrows, c), BF)]
        return [((2, k, wrows, c), BF) for k, c in shapes], scratch + [deliver_sems(len(shapes), far)]

    att_shapes, ff_shapes = ((3, cq), (1, cq)), ((1, hq), (1, hq))

    def ff_bwd(layer, cid, g, nt, act, upward, wup, wdn, hidden, terms):
        vecs = params[layer][2]
        outs = [
            ((width, hq), BF),
            ((width, hq), BF),
            ((mb, share, width), F32),
            ((4, 8, width), F32),
            ((8, hq), F32),
            (tokens, BF),
        ]
        scratch = act_scratch + [pltpu.VMEM((2, mb, rows_mb, hq), BF)]
        d_outs, d_scratch = deliver_parts(att_shapes) if terms else ([], [])
        ins = [g, nt, act, upward, wup.reshape(width, hq), wdn.reshape(width, hq), vecs, hidden] + list(terms)
        return call(
            functools.partial(ff_backward, layer, len(terms)),
            cid,
            ins,
            [VM] * len(ins),
            outs + d_outs,
            [VM] * (len(outs) + len(d_outs)),
            scratch + d_scratch,
        )

    def att_bwd(layer, cid, gb, x, normed, proj, mixed, wqkv, wo, grad_hidden, terms):
        vecs = params[layer][2]
        outs = [((3, width, cq), BF), ((width, cq), BF), ((2, 8, width), F32), ((3, 8, cq), F32), (tokens, BF)]
        scratch = act_scratch + [pltpu.VMEM((3, 2, mb, rows_mb, cq), BF)]
        d_outs, d_scratch = deliver_parts(ff_shapes)
        ins = [
            gb, x, normed, proj, mixed, wqkv.reshape(3, width, cq), wo.reshape(width, cq), vecs, slopes, pen, grad_hidden
        ] + list(terms)
        return call(
            functools.partial(att_backward, layer, len(terms)),
            cid,
            ins,
            [VM] * 8 + [SM] + [VM] * (len(ins) - 9),
            outs + d_outs,
            [VM] * (len(outs) + len(d_outs)),
            scratch + d_scratch,
        )

    def as_ff(*terms):
        return [v.reshape(1, nb, wrows, hq) for v in terms]

    def as_att(a, b):
        return [a.reshape(3, nb, wrows, cq), b.reshape(1, nb, wrows, cq)]

    g_up1, g_dn1, gh1, sf1, su1, gb1 = ff_bwd(1, 5, cot, nt1, act1, upward1, wup1, wdn1, hidden1, ())
    g_qkv1, g_o1, sa1, sp1, g0, d_up1, d_dn1 = att_bwd(
        1, 6, gb1, x1, normed1, proj1, mixed1, wqkv1, wo1, gh1, as_ff(g_up1, g_dn1)
    )
    g_up0, g_dn0, gh0, sf0, su0, gb0, d_qkv1, d_o1 = ff_bwd(
        0, 7, g0, nt0, act0, upward0, wup0, wdn0, hidden0, as_att(g_qkv1, g_o1)
    )
    g_qkv0, g_o0, sa0, sp0, gin, d_up0, d_dn0 = att_bwd(
        0, 8, gb0, x0, normed0, proj0, mixed0, wqkv0, wo0, gh0, as_ff(g_up0, g_dn0)
    )
    d_outs, d_scratch = deliver_parts(att_shapes)
    d_qkv0, d_o0 = call(
        functools.partial(deliver_last, 2), 9, as_att(g_qkv0, g_o0), [VM] * 2, d_outs, [VM] * 2, d_scratch
    )

    def home(d0, d1):
        k, c = d0.shape[1], d0.shape[3]
        mine = jnp.where(s == 0, d0, d1)
        got = swap(jnp.where(s == 0, d1, d0), "s")
        both = in_order(mine, got, s, 0)
        return both.transpose(3, 2, 0, 1, 4).reshape(wrows, k, 4 * c).astype(F32)

    g_qkv = home(d_qkv0, d_qkv1)[None]
    g_out = home(d_o0, d_o1).reshape(1, wrows, block)
    g_fc1 = home(d_up0, d_up1).reshape(1, wrows, hid)
    g_fc2 = home(d_dn0, d_dn1).reshape(1, wrows, hid)

    sec0 = pick(x1.reshape(2, mb, rows_mb, width), zl, 0)
    sec1 = pick(x2.reshape(2, mb, rows_mb, width), zl, 0)
    section_outputs = jnp.where(s == 0, sec0, sec1)[None]
    in0 = pick(gin.reshape(2, mb, rows_mb, width), zl, 0)
    in1 = pick(g0.reshape(2, mb, rows_mb, width), zl, 0)
    input_grads = jnp.where(s == 0, in0, in1)[None]

    pieces = []
    for sf, su, sa, sp in ((sf0, su0, sa0, sp0), (sf1, su1, sa1, sp1)):
        sf, su, sa, sp = (jnp.sum(v, axis=-2) for v in (sf, su, sa, sp))
        place = (t * 4 + quarter).astype(jnp.int32)
        wide_qv = lax.dynamic_update_slice(jnp.zeros((2, 8, cq), F32), jnp.stack([sp[0], sp[2]])[:, None], (0, place, 0))
        wide_up = lax.dynamic_update_slice(jnp.zeros((8, hq), F32), su[None], (place, 0))
        rows_small = jnp.stack([sa[0], sf[0], sa[1], sf[1], sf[2], sf[3]])
        pieces.append(jnp.concatenate([rows_small.reshape(-1), wide_qv.reshape(-1), wide_up.reshape(-1)]))
    total = lax.psum(jnp.stack(pieces), ("s", "zh", "zl", "y", "t"))
    total = pick(total, s, 0)
    grad_gains = total[: 2 * width].reshape(1, 2, width)
    grad_biases = total[2 * width : 6 * width].reshape(1, 4, width)
    grad_b_qv = pick(total[6 * width : 6 * width + 16 * cq].reshape(1, 2, 2, 4 * cq), t, 2)
    grad_b_fc1 = pick(total[6 * width + 16 * cq :].reshape(1, 2, 4 * hq), t, 1)
    return section_outputs, input_grads, g_qkv, grad_b_qv, g_out, g_fc1, grad_b_fc1, g_fc2, grad_gains, grad_biases


def solution(mesh):
    n_s, n_dp, n_t = mesh.shape["section"], mesh.shape["dp"], mesh.shape["tensor"]
    fine = Mesh(mesh.devices.reshape(n_s, n_dp // 4, 2, 2, n_t), ("s", "zh", "zl", "y", "t"))
    return jax.shard_map(
        shards,
        mesh=fine,
        in_specs=(
            P(None, DP, None),
            P(None, DP, None),
            P(None, DP),
            P("s", DP, None, "t"),
            P("s", None, "t"),
            P("s", DP, "t"),
            P("s", DP, "t"),
            P("s", "t"),
            P("s", DP, "t"),
            P("s", None, None),
            P("s", None, None),
        ),
        out_specs=(
            P("s", None, DP, None),
            P("s", None, DP, None),
            P("s", DP, None, "t"),
            P("s", None, "t"),
            P("s", DP, "t"),
            P("s", DP, "t"),
            P("s", "t"),
            P("s", DP, "t"),
            P("s", None, None),
            P("s", None, None),
        ),
        check_vma=False,
    )
```

time: 1780 us -> 1530 us (0.86)
  Pallas kernels: 0 us -> 1310 us
  waiting for transfers between devices: 1070 us -> 114 us
  local copies, waits for them, and re-layouts: 257 us -> 40.9 us
  other arithmetic: 208 us -> 27.6 us
  matrix products: 138 us -> 0 us
  starting transfers between devices: 74.4 us -> 8.74 us
    pallas_call x0 -> x10, Pallas kernels: none -> 1310 us  [call(): pl.pallas_call(body, out_shape=[jax.ShapeDtypeStruct(sh, dt) for sh, dt i...]
    ppermute x84 -> x6, waiting for transfers between devices: 962 us -> 0.02 us  [swap(): return lax.ppermute(v, axis, [(i, i ^ offset) for i in range(n)])]
    dot_general x36 -> x0, matrix products: 138 us -> none  [the longest x8 41.3 us: row_dot(): lax.dot_general(a, b, (((0,), (0,)), ((), ())), preferred_element_type=F32)]
    ppermute x84 -> x6, starting transfers between devices: 74.3 us -> 8.7 us  [swap(): return lax.ppermute(v, axis, [(i, i ^ offset) for i in range(n)])]
    unnamed x344 -> x58, local copies, waits for them, and re-layouts: 72.9 us -> 20.4 us
    another operation x26 -> x4, other arithmetic: 46.4 us -> 0.09 us  [the longest x2 0.07 us: shards(): rows_small = jnp.stack([sa[0], sf[0], sa[1], sf[1], sf[2], sf[3]])]
    dot_general x7 -> x0, local copies, waits for them, and re-layouts: 45.4 us -> none  [row_dot(): lax.dot_general(a, b, (((0,), (0,)), ((), ())), preferred_element_type=F32)]
    another operation x58 -> x7, other arithmetic: 48.6 us -> 5.73 us  [in_order(): return jnp.stack([first, second], axis=dim)]
  transfers between devices with their start and end apart: 85 -> 7, of which waited for: 49 -> 1; matrix products, arithmetic and copies ran while one was open for 23% -> 3% of each run, Pallas kernels for 0% -> 20%
where the time goes in v2:
time: 1530 us; the launch traced here: 1520 us
  Pallas kernels  1310 us (86%)
  waiting for transfers between devices  114 us (7%)
  local copies, waits for them, and re-layouts  40.9 us (3%)
  other arithmetic  27.6 us (2%)
    pallas_call x10, Pallas kernels, call(): pl.pallas_call(body, out_shape=[jax.ShapeDtypeStruct(sh, dt) for sh, dt i...  1310 us
    psum x1, waiting for transfers between devices, shards(): total = lax.psum(jnp.stack(pieces), ('s', 'zh', 'zl', 'y', 't'))  114 us
  transfers between devices with their start and end apart: 7, of which 1 were waited for; matrix products, arithmetic and copies ran while one was open for 3% of the time, Pallas kernels for 20%

profile of v2, /device:TPU:0, one launch (start us, length us, event | category | flops | bytes accessed | tf_op | source)
XLA Modules:
  0.0 1518.4 jit_solution(15201232503901362643)
XLA Ops:
  10.1 2.9 collective-permute-start
  13.1 1.6 collective-permute-start.1
  15.2 242.5 %shard_map.186 = (bf16[2,3,256,512]{3,2,1,0:T(8,128)(2,1)}, bf16[2,1,256,512]{3,2,1,0:T(8,128)(2,1)}, bf16[2,1,256,2048]{3,2,1,0:T(8,128)(2,1)}, bf16[2,1,256,20...) custom-call(bf16[3,256,1024]{2,1,0:T(8,128)(2,1)} %bitcast.195, ...), custom_call_target="tpu_custom_call" | custom-call | tf_op jit(solution)/shard_map/pallas_call | solution.py:290
  263.7 165.0 %shard_map.187 = (bf16[2,2,2,2,64,2048]{5,4,3,2,1,0:T(8,128)(2,1)}, bf16[3,2,2,256,256]{4,3,2,1,0:T(8,128)(2,1)}, bf16[2,2,256,256]{3,2,1,0:T(8,128)(2,1)}, f32[...) custom-call(bf16[2,2,2,2,64,2048]{5,4,3,2,1,0:T(8,128)(2,1)} %get-tu, ...), custom_call_target="tpu_custom_call" | custom-call | tf_op jit(solution)/shard_map/pallas_call | solution.py:290
  428.7 106.3 %shard_map.188 = (f32[2,2,256,1024]{3,2,1,0:T(8,128)}, bf16[2,2,256,1024]{3,2,1,0:T(8,128)(2,1)}, bf16[2,2,2,2,64,2048]{5,4,3,2,1,0:T(8,128)(2,1)}, bf16[3,8,256...) custom-call(bf16[2,2,2,2,64,2048]{5,4,3,2,1,0:T(8,128)(2,1)} %get-tuple-element.75.x.normed_two, ...), custom_call_target="tpu_custom_call" | custom-call | tf_op jit(solution)/shard_map/pallas_call | solution.py:290
  535.1 166.6 %shard_map.189 = (bf16[2,2,2,2,64,2048]{5,4,3,2,1,0:T(8,128)(2,1)}, bf16[3,2,2,256,256]{4,3,2,1,0:T(8,128)(2,1)}, bf16[2,2,256,256]{3,2,1,0:T(8,128)(2,1)}, f32[...) custom-call(bf16[2,2,2,2,64,2048]{5,4,3,2,1,0:T(8,128)(2,1)} %get-tu, ...), custom_call_target="tpu_custom_call" | custom-call | tf_op jit(solution)/shard_map/pallas_call | solution.py:290
  701.7 73.3 %shard_map.190 = (f32[2,2,256,1024]{3,2,1,0:T(8,128)}, bf16[2,2,256,1024]{3,2,1,0:T(8,128)(2,1)}, bf16[2,2,2,2,64,2048]{5,4,3,2,1,0:T(8,128)(2,1)}) custom-call(bf16[2,2,2,2,64,2048]{5,4,3,2,1,0:T(8,128)(2,1)} %get-tuple-element.84.x.normed_two, bf16[2048,1024]{1,0:T(8,128)(2,1)} %bitcast.172, bf16[2048,1024]{1,0:T(8,128)(2,1)} %bitcast.174, ...), custom_call_target="tpu_custom_call" | custom-call | tf_op jit(solution)/shard_map/pallas_call | solution.py:290
  774.9 80.3 %shard_map.191 = (bf16[2048,1024]{1,0:T(8,128)(2,1)}, bf16[2048,1024]{1,0:T(8,128)(2,1)}, f32[2,64,2048]{2,1,0:T(8,128)}, f32[4,8,2048]{2,1,0:T(8,128)}, f32[8,1...) custom-call(bf16[2,2,2,2,64,2048]{5,4,3,2,1,0:T(8,128)(2,1)} %get-tuple-element.89.g, ...), custom_call_target="tpu_custom_call" | custom-call | tf_op jit(solution)/shard_map/pallas_call | solution.py:290
  855.3 151.6 %shard_map.192 = (bf16[3,2048,256]{2,1,0:T(8,128)(2,1)}, bf16[2048,256]{1,0:T(8,128)(2,1)}, f32[2,8,2048]{2,1,0:T(8,128)}, f32[3,8,256]{2,1,0:T(8,128)}, bf16[2,...) custom-call(bf16[2,2,2,2,64,2048]{5,4,3,2,1,0:T(8,128)(2,1)} %get-tuple-eleme, ...), custom_call_target="tpu_custom_call" | custom-call | tf_op jit(solution)/shard_map/pallas_call | solution.py:290
  1006.9 113.7 %shard_map.193 = (bf16[2048,1024]{1,0:T(8,128)(2,1)}, bf16[2048,1024]{1,0:T(8,128)(2,1)}, f32[2,64,2048]{2,1,0:T(8,128)}, f32[4,8,2048]{2,1,0:T(8,128)}, f32[8,1...) custom-call(bf16[2,2,2,2,64,2048]{5,4,3,2,1,0:T(8,128)(2,1)} %get-tu, ...), custom_call_target="tpu_custom_call" | custom-call | tf_op jit(solution)/shard_map/pallas_call | solution.py:290
  1121.9 151.0 %shard_map.194 = (bf16[3,2048,256]{2,1,0:T(8,128)(2,1)}, bf16[2048,256]{1,0:T(8,128)(2,1)}, f32[2,8,2048]{2,1,0:T(8,128)}, f32[3,8,256]{2,1,0:T(8,128)}, bf16[2,...) custom-call(bf16[2,2,2,2,64,2048]{5,4,3,2,1,0:T(8,128)(2,1)} %get-tuple-eleme, ...), custom_call_target="tpu_custom_call" | custom-call | tf_op jit(solution)/shard_map/pallas_call | solution.py:290
  1273.0 2.5 bitcast_select_fusion.1
  1278.6 61.5 %shard_map.195 = (bf16[2,3,256,256]{3,2,1,0:T(8,128)(2,1)}, bf16[2,1,256,256]{3,2,1,0:T(8,128)(2,1)}) custom-call(bf16[3,8,256,256]{3,2,1,0:T(8,128)(2,1)} %bitcast.192, bf16[1,8,256,256]{3,2,1,0:T(8,128)(2,1)} %bitcast.199), custom_call_target="tpu_custom_call" | custom-call | tf_op jit(solution)/shard_map/pallas_call | solution.py:290
  1346.2 6.0 dynamic-slice_select_fusion
  1352.2 113.9 %all-reduce.2.cloned.1.call-done = f32[2,24576]{1,0:T(2,128)} async-done(((f32[2,24576]{1,0:T(2,128)}), f32[2,24576]{1,0:T(2,128)}) %all-reduce.2.cloned.1.call-update) | async-done | bytes 196624 | tf_op jit(solution)/shard_map/psum | solution.py:891
  1472.5 1.5 select_bitcast_fusion.3
  1474.2 2.4 copy.63
  1476.6 3.7 copy.84
  1483.0 2.3 convert_bitcast_fusion
  1485.3 5.4 copy.83
  1490.7 5.7 copy.87
  1497.8 2.3 convert_bitcast_fusion.1
  1500.1 5.4 copy.76
  1505.5 5.6 copy.86
  (147 shorter events, 30.1 us)
Async XLA Ops:
  7.2 1458.9 %all-reduce.2.cloned.1.call-start = ((), (), s32[]{:S(2)}) async-start(), calls=%async_computation | async-start | bytes 393216 | tf_op jit(solution)/shard_map/psum | solution.py:891
  10.1 249.7 %collective-permute-start = (f32[18432]{0:T(1024)S(1)}, f32[18432]{0:T(1024)S(1)}, u32[]{:S(2)}, u32[]{:S(2)}) collective-permute-start(f32[18432]{0:T(1024)S(1)} %pad_maximum_fusion.3), channel_id=1, source_target_pairs={{0,16},{16,0},{1,17},{17,1},{2,18},{18,2},{3,19},{19,3},{4,20},{20... | collective-permute-start | bytes 221192 | tf_op jit(solution)/shard_map/ppermute | solution.py:675
  13.1 244.7 %collective-permute-start.1 = (s32[2,256]{1,0:T(2,128)}, s32[2,256]{1,0:T(2,128)S(1)}, u32[]{:S(2)}, u32[]{:S(2)}) collective-permute-start(s32[2,256]{1,0:T(2,128)} %param.13), channel_id=1, source_target_pairs={{0,4},{4,0},{1,5},{5,1},{2,6},{6,2},{3,7},{7,3},{8,12},{12,8},{9,1... | collective-permute-start | bytes 6152 | tf_op jit(solution)/shard_map/ppermute | solution.py:675
  15.2 242.6 %copy-start.21 = (s32[2,256]{1,0:T(2,128)S(1)}, s32[2,256]{1,0:T(2,128)}, u32[]{:S(2)}) copy-start(s32[2,256]{1,0:T(2,128)} %param.13) | copy-start | bytes 6148
  15.2 244.6 %copy-start.16 = (f32[1,4096]{1,0:T(1,128)S(1)}, f32[1,4096]{1,0:T(1,128)}, u32[]{:S(2)}) copy-start(f32[1,4096]{1,0:T(1,128)} %param.18) | copy-start | bytes 49156
  1006.9 114.8 %copy-start.11 = (f32[4,8,2048]{2,1,0:T(8,128)S(1)}, f32[4,8,2048]{2,1,0:T(8,128)}, u32[]{:S(2)}) copy-start(f32[4,8,2048]{2,1,0:T(8,128)} %get-tuple-element.121) | copy-start | bytes 786436
  1121.7 151.2 %copy-start.12 = (f32[4,2048]{1,0:T(4,128)}, f32[4,2048]{1,0:T(4,128)S(1)}, u32[]{:S(2)}) copy-start(f32[4,2048]{1,0:T(4,128)S(1)} %reduce_sum.83) | copy-start | bytes 98308
  1121.8 151.1 %copy-start.13 = (f32[4,2048]{1,0:T(4,128)}, f32[4,2048]{1,0:T(4,128)S(1)}, u32[]{:S(2)}) copy-start(f32[4,2048]{1,0:T(4,128)S(1)} %reduce_sum.87) | copy-start | bytes 98308
  1121.9 151.1 %copy-start = (bf16[2,1,256,1024]{3,2,1,0:T(8,128)(2,1)S(1)}, bf16[2,1,256,1024]{3,2,1,0:T(8,128)(2,1)}, u32[]{:S(2)}) copy-start(bf16[2,1,256,1024]{3,2,1,0:T(8,128)(2,1)} %get-tuple-element.129) | copy-start | bytes 3145732
  1275.4 204.8 %collective-permute-start.5 = (bf16[2,1,256,1024]{3,2,1,0:T(8,128)(2,1)}, bf16[2,1,256,1024]{3,2,1,0:T(8,128)(2,1)}, u32[]{:S(2)}, u32[]{:S(2)}) collective-permute-start(bf16[2,1,256,1024]{3,2,1,0:T(8,128)(2,1)} %bitcast_select_fusion.1), channel_id=1, source_target_pairs={{0,16},{16,0},{1,17},{17,1},{2,18},{18,2},{3,19},{19,3},{4,20},{20... | collective-permute-start | bytes 3145736 | tf_op jit(solution)/shard_map/ppermute | solution.py:675
  1276.6 63.6 %copy-start.9 = (bf16[2,1,256,256]{3,2,1,0:T(8,128)(2,1)S(1)}, bf16[2,1,256,256]{3,2,1,0:T(8,128)(2,1)}, u32[]{:S(2)}) copy-start(bf16[2,1,256,256]{3,2,1,0:T(8,128)(2,1)} %get-tuple-element.125) | copy-start | bytes 786436
  1277.7 64.6 %copy-start.15 = (f32[2,8,2048]{2,1,0:T(8,128)S(1)}, f32[2,8,2048]{2,1,0:T(8,128)}, u32[]{:S(2)}) copy-start(f32[2,8,2048]{2,1,0:T(8,128)} %get-tuple-element.116) | copy-start | bytes 393220
  1277.7 64.6 %slice-start = ((f32[4,2048]{1,0:T(4,128)}), f32[1,2048]{1,0:T(1,128)S(1)}, s32[]{:S(2)}) async-start(f32[4,2048]{1,0:T(4,128)} %copy-done.12), calls=%async_computation.1 | async-start | bytes 16384 | tf_op jit(solution)/shard_map/slice | solution.py:889
  1277.7 64.7 %copy-start.20 = (f32[3,8,256]{2,1,0:T(8,128)S(1)}, f32[3,8,256]{2,1,0:T(8,128)}, u32[]{:S(2)}) copy-start(f32[3,8,256]{2,1,0:T(8,128)} %get-tuple-element.118) | copy-start | bytes 73732
  1277.7 64.9 %copy-start.18 = (f32[8,1024]{1,0:T(8,128)S(1)}, f32[8,1024]{1,0:T(8,128)}, u32[]{:S(2)}) copy-start(f32[8,1024]{1,0:T(8,128)} %get-tuple-element.119) | copy-start | bytes 98308
  1277.7 65.0 %copy-start.14 = (f32[2,8,2048]{2,1,0:T(8,128)S(1)}, f32[2,8,2048]{2,1,0:T(8,128)}, u32[]{:S(2)}) copy-start(f32[2,8,2048]{2,1,0:T(8,128)} %get-tuple-element.120) | copy-start | bytes 393220
  1277.7 65.1 %slice-start.1 = ((f32[4,2048]{1,0:T(4,128)}), f32[1,2048]{1,0:T(1,128)S(1)}, s32[]{:S(2)}) async-start(f32[4,2048]{1,0:T(4,128)} %copy-done.13), calls=%async_computation.2 | async-start | bytes 16384 | tf_op jit(solution)/shard_map/slice | solution.py:889
  1277.7 65.2 %copy-start.19 = (f32[3,8,256]{2,1,0:T(8,128)S(1)}, f32[3,8,256]{2,1,0:T(8,128)}, u32[]{:S(2)}) copy-start(f32[3,8,256]{2,1,0:T(8,128)} %get-tuple-element.122) | copy-start | bytes 73732
  1277.7 65.3 %copy-start.17 = (f32[8,1024]{1,0:T(8,128)S(1)}, f32[8,1024]{1,0:T(8,128)}, u32[]{:S(2)}) copy-start(f32[8,1024]{1,0:T(8,128)} %get-tuple-element.123) | copy-start | bytes 98308
  1277.7 218.7 %collective-permute-start.4 = (bf16[2,1,256,1024]{3,2,0,1:T(8,128)(2,1)}, bf16[2,1,256,1024]{3,2,0,1:T(8,128)(2,1)}, u32[]{:S(2)}, u32[]{:S(2)}) collective-permute-start(bf16[2,1,256,1024]{3,2,0,1:T(8,128)(2,1)} %bitcast_select_fusion.4), channel_id=1, source_target_pairs={{0,16},{16,0},{1,17},{17,1},{2,18},{18,2},{3,19},{19,3},{4,20},{20... | collective-permute-start | bytes 3145736 | tf_op jit(solution)/shard_map/ppermute | solution.py:675
  1278.6 65.4 %copy-start.7 = (bf16[2,3,256,256]{3,2,1,0:T(8,128)(2,1)S(1)}, bf16[2,3,256,256]{3,2,1,0:T(8,128)(2,1)}, u32[]{:S(2)}) copy-start(bf16[2,3,256,256]{3,2,1,0:T(8,128)(2,1)} %get-tuple-element.115) | copy-start | bytes 2359300
  1341.3 129.4 %collective-permute-start.3 = (bf16[2,1,256,256]{3,2,1,0:T(8,128)(2,1)S(1)}, bf16[2,1,256,256]{3,2,1,0:T(8,128)(2,1)S(1)}, u32[]{:S(2)}, u32[]{:S(2)}) collective-permute-start(bf16[2,1,256,256]{3,2,1,0:T(8,128)(2,1)S(1)} %bitcast_select_fusion.7), channel_id=1, source_target_pairs={{0,16},{16,0},{1,17},{17,1},{2,18},{18,2},{3,19},{19,3},{4,20},{20... | collective-permute-start | bytes 786440 | tf_op jit(solution)/shard_map/ppermute | solution.py:675
  1345.1 127.4 %collective-permute-start.2 = (bf16[2,3,256,256]{3,2,1,0:T(8,128)(2,1)}, bf16[2,3,256,256]{3,2,1,0:T(8,128)(2,1)}, u32[]{:S(2)}, u32[]{:S(2)}) collective-permute-start(bf16[2,3,256,256]{3,2,1,0:T(8,128)(2,1)} %broadcast_select_fusion), channel_id=1, source_target_pairs={{0,16},{16,0},{1,17},{17,1},{2,18},{18,2},{3,19},{19,3},{4,20},{20... | collective-permute-start | bytes 2359304 | tf_op jit(solution)/shard_map/ppermute | solution.py:675
  1346.2 124.4 %copy-start.10 = (bf16[2,1,256,256]{3,2,1,0:T(8,128)(2,1)S(1)}, bf16[2,1,256,256]{3,2,1,0:T(8,128)(2,1)}, u32[]{:S(2)}) copy-start(bf16[2,1,256,256]{3,2,1,0:T(8,128)(2,1)} %get-tuple-element.124) | copy-start | bytes 786436
  (7 other events, 30.1 us)
Sparse Core Ops, SparseCore 0:
  1344.2 121.8 all-reduce.1

commit v3 on v1

v3 whole, which is shorter than its diff:
```python
import functools

import jax
import jax.numpy as jnp
from jax import lax
from jax.experimental import pallas as pl
from jax.experimental.pallas import tpu as pltpu
from jax.sharding import Mesh, PartitionSpec as P

HEADS = 32
HEAD_DIM = 64
GROUP = 256
EPS = 1e-05
BF = jnp.bfloat16
F32 = jnp.float32
DP = ("zh", "zl", "y")
MESH = pl.DeviceIdType.MESH
REL = ((1, 1), (0, 1), (1, 0), (0, 0))
CHUNK = 16
PARTS = 4
FAR = 1e30


def dot(a, b):
    return jnp.dot(a, b, preferred_element_type=F32)


def dot_t(a, b):
    return lax.dot_general(a, b, (((1,), (1,)), ((), ())), preferred_element_type=F32)


def row_dot(a, b):
    return lax.dot_general(a, b, (((0,), (0,)), ((), ())), preferred_element_type=F32)


def normalize(v):
    centred = v - jnp.mean(v, axis=-1, keepdims=True)
    scale = lax.rsqrt(jnp.mean(centred * centred, axis=-1, keepdims=True) + EPS)
    return centred * scale, scale


def geometry(segment):
    length = segment.shape[0]
    places = jnp.arange(length, dtype=jnp.int32)
    same_seg = segment[:, None] == segment[None, :]
    starts = jnp.min(jnp.where(same_seg, places[None, :], length), axis=1)
    prompt_len = jnp.sum((segment == 0).astype(jnp.int32))
    position = jnp.where(segment == 0, places, prompt_len + places - starts)
    allowed = (position[None, :] <= position[:, None]) & ((segment[None, :] == 0) | same_seg)
    offset = (position[:, None] - position[None, :]).astype(F32)
    return jnp.where(allowed, offset, FAR)


class Place:
    def __init__(self):
        self.s, self.zh, self.zl, self.y, self.t = (lax.axis_index(a) for a in ("s", "zh", "zl", "y", "t"))
        self.outer = lax.axis_size("zh")
        self.far = self.outer * 2

    def block(self, zh, zl, y):
        return (zh * 2 + zl) * 2 + y

    def meet(self):
        barrier = pltpu.get_barrier_semaphore()
        others = [{"t": self.t ^ 1}, {"y": self.y ^ 1}]
        others += [{"s": self.s ^ 1, "zl": self.zl ^ k} for k in range(2)]
        others += [{"zh": self.zh ^ (k // 2), "zl": self.zl ^ (k % 2)} for k in range(1, self.far)]
        for other in others:
            pl.semaphore_signal(barrier, inc=1, device_id=other, device_id_type=MESH)
        pl.semaphore_wait(barrier, len(others))


def remote(src, dst, send, recv, **where):
    return pltpu.make_async_remote_copy(
        src_ref=src, dst_ref=dst, send_sem=send, recv_sem=recv, device_id=where, device_id_type=MESH
    )


def row_loop(kinds, rows, fn):
    per = rows // CHUNK

    def step(j, carry):
        fn(j // per, pl.ds(pl.multiple_of((j % per) * CHUNK, CHUNK), CHUNK))
        return carry

    lax.fori_loop(0, kinds * per, step, 0)


class Sums:
    def __init__(self, me, part, full, tbuf, rbuf, sems):
        self.me, self.part, self.full, self.tbuf, self.rbuf, self.sems = me, part, full, tbuf, rbuf, sems
        s, zl, t = me.s, me.zl, me.t
        self.core = [
            remote(part.at[zl ^ dzl, :, s ^ ds, t ^ 1], tbuf.at[i], sems.at[0, i], sems.at[1, i], t=t ^ 1)
            for i, (ds, dzl) in enumerate(REL)
        ]
        self.sect = [
            remote(part.at[zl ^ dzl, :, s ^ 1, t], rbuf.at[i], sems.at[2, i], sems.at[3, i], s=s ^ 1)
            for i, dzl in enumerate((1, 0))
        ]
        self.pair = remote(part.at[zl ^ 1, :, s, t], rbuf.at[2], sems.at[2, 2], sems.at[3, 2], zl=zl ^ 1)

    def to_core(self, *which):
        for i in which:
            self.core[i].start()

    def merge(self, i, *extra):
        me, part, tbuf, rbuf = self.me, self.part, self.tbuf, self.rbuf
        ds, dzl = REL[i]
        a, b = me.zl ^ dzl, me.s ^ ds
        self.core[i].wait_recv()

        def add(m, r):
            v = part[a, m, b, me.t, r].astype(F32) + tbuf[i, m, r].astype(F32)
            for e in extra:
                v = v + rbuf[e, m, r].astype(F32)
            part[a, m, b, me.t, r] = v.astype(BF)

        row_loop(part.shape[1], part.shape[4], add)

    def to_section(self, i):
        self.merge(2 * i)
        self.sect[i].start()

    def to_pair(self):
        self.sect[0].wait_recv()
        self.merge(1, 0)
        self.pair.start()

    def finish(self, row_fn):
        me, part, tbuf, rbuf, full = self.me, self.part, self.tbuf, self.rbuf, self.full
        self.core[3].wait_recv()
        self.sect[1].wait_recv()
        self.pair.wait_recv()

        def add(m, r):
            v = part[me.zl, m, me.s, me.t, r].astype(F32) + tbuf[3, m, r].astype(F32)
            v = v + rbuf[1, m, r].astype(F32) + rbuf[2, m, r].astype(F32)
            full[me.zl, m, me.s, me.t, r] = row_fn(m, r, v)

        row_loop(part.shape[1], part.shape[4], add)
        for c in self.core + self.sect + [self.pair]:
            c.wait_send()

    def piece(self, ds, dzl):
        return self.full.at[self.me.zl ^ dzl, :, self.me.s ^ ds, self.me.t]

    def send(self, kind, i, piece, **where):
        c = remote(piece, piece, self.sems.at[kind, i], self.sems.at[kind + 1, i], **where)
        c.start()
        return c

    def spread(self):
        me, own = self.me, self.piece(0, 0)
        self.over_z = self.send(4, 0, own, zl=me.zl ^ 1)
        self.over_s = self.send(4, 1, own, s=me.s ^ 1)
        self.cross = [self.send(6, 0, own, t=me.t ^ 1)]

    def collect(self, between=None):
        me = self.me
        self.over_z.wait_recv()
        other = self.piece(0, 1)
        both = self.send(4, 2, other, s=me.s ^ 1)
        self.cross.append(self.send(6, 1, other, t=me.t ^ 1))
        self.over_s.wait_recv()
        self.cross.append(self.send(6, 2, self.piece(1, 0), t=me.t ^ 1))
        if between:
            between()
        both.wait_recv()
        self.cross.append(self.send(6, 3, self.piece(1, 1), t=me.t ^ 1))
        for c in self.cross:
            c.wait_recv()
        for c in self.cross + [self.over_z, self.over_s, both]:
            c.wait_send()


def sums_scratch(mb, share, width):
    return [
        pltpu.VMEM((2, mb, 2, 2, share, width), BF),
        pltpu.VMEM((4, mb, share, width), BF),
        pltpu.VMEM((3, mb, share, width), BF),
        pltpu.SemaphoreType.DMA((8, 4)),
    ]


class Staged:
    def __init__(self, src, dst, buf, sems):
        self.load = pltpu.make_async_copy(src, buf, sems.at[0])
        self.store = pltpu.make_async_copy(buf, dst, sems.at[1])

    def start(self):
        self.load.start()

    def turn(self):
        self.load.wait()
        self.store.start()

    def wait(self):
        self.store.wait()


class Fetch:
    def __init__(self, me, layer, pairs, sems, bufs):
        self.me, self.pairs, self.sems = me, pairs, sems
        self.first, self.far, self.parts, self.near = [], {}, {}, []
        home = me.block(me.zh, me.zl, me.y)
        for p, (half, whole) in enumerate(pairs):
            c = whole.shape[-1]
            src = lambda q, half=half, c=c: half.at[layer, :, :, pl.ds(pl.multiple_of(q * c, c), c)]
            dst = whole.at[:, home]
            self.first.append(Staged(src(me.zl), dst, bufs[p], sems.at[p, 4]))
            for k in range(1, me.far):
                where = {"zh": me.zh ^ (k // 2), "zl": me.zl ^ (k % 2)}
                cut = half.shape[2] // PARTS
                for q in range(PARTS):
                    r = pl.ds(q * cut, cut)
                    self.parts[p, k, q] = remote(
                        src(where["zl"]).at[:, r], dst.at[:, r], sems.at[p, 0, k], sems.at[p, 1, k], **where
                    )
                self.far[p, k] = remote(src(where["zl"]), dst, sems.at[p, 0, k], sems.at[p, 1, k], **where)
            self.near.append([remote(src(me.zl), dst, sems.at[p, 2, 0], sems.at[p, 3, 0], y=me.y ^ 1)])
        self.waves = waves(me.far)

    def start(self, *ps):
        for p in ps:
            self.near[p][0].start()
            self.first[p].start()

    def turn(self, *ps):
        for p in ps:
            self.first[p].turn()

    def send(self, p, wave, q):
        for k in self.waves[wave]:
            self.parts[p, k, q].start()

    def units(self, ps, before=None):
        for wave in range(2):
            for q in range(PARTS):
                first = wave == 0 and q == 0
                second = wave == 0 and q == 1

                def issue(wave=wave, q=q, first=first, second=second):
                    if first:
                        if before:
                            before()
                        self.start(*ps)
                    if second:
                        self.turn(*ps)
                    for p in ps:
                        self.send(p, wave, q)

                def forward(wave=wave):
                    for p in ps:
                        self.pass_on(p, wave)

                yield issue, forward if q == PARTS - 1 else None

    def pass_on(self, p, wave):
        me = self.me
        for k in self.waves[wave]:
            self.far[p, k].wait_recv()
            whole = self.pairs[p][1]
            piece = whole.at[:, me.block(me.zh ^ (k // 2), me.zl ^ (k % 2), me.y)]
            on = remote(piece, piece, self.sems.at[p, 2, k], self.sems.at[p, 3, k], y=me.y ^ 1)
            on.start()
            self.near[p].append(on)

    def ready(self, *ps):
        for p in ps:
            self.first[p].wait()
            for c in self.near[p]:
                c.wait_recv()

    def finish(self):
        for c in list(self.far.values()) + [c for near in self.near for c in near]:
            c.wait_send()


class Pump:
    def __init__(self, *units, lag=5):
        self.units = [u for group in units for u in group]
        self.issued, self.clock, self.lag, self.waiting = 0, 0, lag, []

    def step(self, n=1):
        for _ in range(n):
            self.clock += 1
            if self.issued < len(self.units):
                issue, forward = self.units[self.issued]
                issue()
                self.issued += 1
                if forward:
                    self.waiting.append((self.clock, self.issued, forward))
            while self.waiting and self.waiting[0][0] + self.lag <= self.clock:
                self.waiting.pop(0)[2]()

    def through(self, n):
        self.step(max(0, min(n, len(self.units)) - self.issued))
        while self.waiting and self.waiting[0][1] <= n:
            self.waiting.pop(0)[2]()


def fetch_scratch(shapes, far, rows):
    return [pltpu.SemaphoreType.DMA((len(shapes), 5, far))] + [pltpu.VMEM((k, rows, c), BF) for k, c in shapes]


class YSum:
    def __init__(self, me, terms, own, total, sems):
        self.me, self.own, self.total, self.terms = me, own, total, terms
        self.copies, self.loads = [], []
        for k in range(1, me.far):
            zh, zl = me.zh ^ (k // 2), me.zl ^ (k % 2)
            src = terms.at[:, me.block(zh, zl, me.y ^ 1)]
            self.copies.append((k, remote(src, total.at[:, k - 1], sems.at[0, k], sems.at[1, k], y=me.y ^ 1)))
            if own is not None:
                here = terms.at[:, me.block(zh, zl, me.y)]
                self.loads.append(pltpu.make_async_copy(here, own.at[:, k - 1], sems.at[2, k]))

    def start(self):
        for _, c in self.copies:
            c.start()
        for c in self.loads:
            c.start()

    def add(self):
        me = self.me
        for c in self.loads:
            c.wait()
        for k, c in self.copies:
            c.wait_recv()
            b = me.block(me.zh ^ (k // 2), me.zl ^ (k % 2), me.y)

            def one(m, r, k=k, b=b):
                mine = self.terms[m, b, r] if self.own is None else self.own[m, k - 1, r]
                self.total[m, k - 1, r] = (self.total[m, k - 1, r].astype(F32) + mine.astype(F32)).astype(BF)

            row_loop(self.total.shape[0], self.total.shape[2], one)

    def finish(self):
        for _, c in self.copies:
            c.wait_send()


class ZSum:
    def __init__(self, me, total, terms, got, own, near, out, sems):
        self.me, self.total, self.got, self.own, self.near, self.out = me, total, got, own, near, out
        self.copies, self.parts = {}, {}
        cut = total.shape[2] // PARTS
        for k in range(1, me.far):
            where = {"zh": me.zh ^ (k // 2), "zl": me.zl ^ (k % 2)}
            src, dst, a, b = total.at[:, k - 1], got.at[:, k - 1], sems.at[0, k], sems.at[1, k]
            self.copies[k] = remote(src, dst, a, b, **where)
            for q in range(PARTS):
                r = pl.ds(q * cut, cut)
                self.parts[k, q] = remote(src.at[:, r], dst.at[:, r], a, b, **where)
        self.load = pltpu.make_async_copy(terms.at[:, me.block(me.zh, me.zl, me.y)], own, sems.at[2, 0])
        self.home = remote(
            terms.at[:, me.block(me.zh, me.zl, me.y ^ 1)], near, sems.at[0, 0], sems.at[1, 0], y=me.y ^ 1
        )

    def start(self):
        self.load.start()
        self.home.start()

    def units(self):
        for wave in waves(self.me.far):
            for q in range(PARTS):
                yield lambda wave=wave, q=q: [self.parts[k, q].start() for k in wave], None

    def add(self):
        me, c = self.me, self.total.shape[3]
        self.load.wait()
        self.home.wait_recv()
        for copy in self.copies.values():
            copy.wait_recv()

        def one(m, r):
            same = self.own[m, r].astype(F32) + self.near[m, r].astype(F32)
            other = self.got[m, 0, r].astype(F32)
            for k in range(2, me.far):
                if k % 2:
                    other = other + self.got[m, k - 1, r].astype(F32)
                else:
                    same = same + self.got[m, k - 1, r].astype(F32)
            self.out[m, r, pl.ds(pl.multiple_of(me.zl * c, c), c)] = same.astype(BF)
            self.out[m, r, pl.ds(pl.multiple_of((me.zl ^ 1) * c, c), c)] = other.astype(BF)

        row_loop(self.total.shape[0], self.total.shape[2], one)

    def finish(self):
        for copy in self.copies.values():
            copy.wait_send()
        self.home.wait_send()


def z_scratch(k, c, far, rows):
    return [
        pltpu.VMEM((k, far - 1, rows, c), BF),
        pltpu.VMEM((k, rows, c), BF),
        pltpu.VMEM((k, rows, c), BF),
        pltpu.SemaphoreType.DMA((3, far)),
    ]


def waves(far):
    ks = range(1, far)
    return [[k for k in ks if k % 2 == 0 or k == 1], [k for k in ks if k % 2 and k > 1]]


class XMove:
    def __init__(self, me, layer, src, dst, sems):
        self.me, self.layer = me, layer
        half = src.shape[1] // 2
        self.copies = []
        for i in range(2):
            r = pl.ds(i * half, half)
            self.copies.append(remote(src.at[:, r], dst.at[:, r], sems.at[0, i], sems.at[1, i], s=me.s ^ 1))

    def start(self, i):
        @pl.when(self.me.s != self.layer)
        def _():
            self.copies[i].start()

    def finish(self):
        @pl.when(self.me.s != self.layer)
        def _():
            for c in self.copies:
                c.wait_send()

        @pl.when(self.me.s == self.layer)
        def _():
            for c in self.copies:
                c.wait_recv()


class Moves:
    def __init__(self, me, plan, chain, x_layer, ins, outs, scratch):
        ny, nz, nx = plan
        scratch = list(scratch)
        self.y = [YSum(me, ins[i], scratch[2 * i], outs[i], scratch[2 * i + 1]) for i in range(ny)]
        scratch = scratch[2 * ny :]
        zs, terms, xs = ins[ny : ny + nz], ins[ny + nz : ny + 2 * nz], ins[ny + 2 * nz :]
        self.z = []
        for i in range(nz):
            got, own, near, sems = scratch[4 * i : 4 * i + 4]
            self.z.append(ZSum(me, zs[i], terms[i], got, own, near, outs[ny + i], sems))
        scratch = scratch[4 * nz :]
        self.x = [XMove(me, x_layer, xs[i], outs[ny + nz + i], scratch[i]) for i in range(nx)]
        scratch = scratch[nx:]
        self.after = []
        for i in range(ny if chain else 0):
            got, own, near, sems = scratch[4 * i : 4 * i + 4]
            self.after.append(ZSum(me, outs[i], ins[i], got, own, near, outs[ny + nz + nx + i], sems))

        self.pump = Pump(*(c.units() for c in self.z))

    def start(self, n):
        self.step(n)
        for c in self.x:
            c.start(0)
        for c in self.y + self.z + self.after:
            c.start()

    def step(self, n=1):
        self.pump.step(n)

    def middle(self):
        for c in self.y:
            c.add()
        for group in zip(*(c.units() for c in self.after)):
            self.pump.units.append((lambda group=group: [u() for u, _ in group], None))

    def more_x(self):
        for c in self.x:
            c.start(1)

    def finish(self):
        self.pump.through(len(self.pump.units))
        for c in self.z + self.after:
            c.add()
        for c in self.y + self.z + self.x + self.after:
            c.finish()


def moves_parts(plan, chain, far, rows):
    ys, zs, xs = plan
    cs = ys if chain else ()
    specs = [AN] * len(ys) + [VM] * len(zs) + [AN] * (len(zs) + len(xs))
    outs = [((k, far - 1, rows, c), BF) for k, c in ys]
    outs += [((k, rows, 2 * c), BF) for group in (zs, xs, cs) for k, c in group]
    out_specs = [VM] * len(ys) + [VM] * len(zs) + [AN] * len(xs) + [VM] * len(cs)
    scratch = []
    for k, c in ys:
        scratch += [pltpu.VMEM((k, far - 1, rows, c), BF), pltpu.SemaphoreType.DMA((3, far))]
    for k, c in zs:
        scratch += z_scratch(k, c, far, rows)
    scratch += [pltpu.SemaphoreType.DMA((2, 2))] * len(xs)
    for k, c in cs:
        scratch += z_scratch(k, c, far, rows)
    return specs, outs, out_specs, scratch


VM = pl.BlockSpec(memory_space=pltpu.VMEM)
SM = pl.BlockSpec(memory_space=pltpu.SMEM)
AN = pl.BlockSpec(memory_space=pl.ANY)


def call(body, cid, ins, in_specs, outs, out_specs, scratch, flops=0):
    return pl.pallas_call(
        body,
        out_shape=[jax.ShapeDtypeStruct(sh, dt) for sh, dt in outs],
        in_specs=in_specs,
        out_specs=out_specs,
        scratch_shapes=scratch,
        compiler_params=pltpu.CompilerParams(
            collective_id=cid, has_side_effects=True, vmem_limit_bytes=60 * 1024 * 1024
        ),
    )(*ins)


def rows_of(ref, a, m):
    v = ref[a, m]
    return v.reshape(-1, v.shape[-1])


def put_rows(ref, a, m, v):
    ref[a, m] = v.reshape(ref.shape[2:])


def norm_rows(src, dst, a, m, gain, shift):
    share = src.shape[4]

    def one(q, r):
        vh, _ = normalize(src[a, m, q // 2, q % 2, r].astype(F32))
        dst[a, m, q // 2, q % 2, r] = (vh * gain + shift).astype(BF)

    row_loop(4, share, one)


def lanes(width):
    return lax.broadcasted_iota(jnp.int32, (1, width), 1)


def head_mask(h):
    return (lanes(2 * HEAD_DIM) // HEAD_DIM) == h


def softmax_parts(q, k, pen, slope):
    sc = dot_t(q * jnp.asarray(HEAD_DIM**-0.5, BF), k) - slope * pen
    lifted = jnp.exp(sc - jnp.max(sc, axis=-1, keepdims=True))
    return lifted * (1.0 / jnp.sum(lifted, axis=-1, keepdims=True))


def halves_of(me, mb, group, sums, hook=None):
    lax.fori_loop(0, mb, lambda m, c: (group(me.zl ^ 1, m), c)[1], 0)
    sums.to_core(0, 1)
    group(me.zl, 0)
    sums.to_section(0)
    if hook:
        hook()
    lax.fori_loop(1, mb, lambda m, c: (group(me.zl, m), c)[1], 0)
    sums.to_core(2, 3)
    sums.to_section(1)
    sums.to_pair()


def halves_apart(me, mb, group, sums, hook):
    for i in range(2 * mb):
        group((me.zl ^ 1) if i < mb else me.zl, i % mb)
        if i == mb - 1:
            sums.to_core(0, 1)
        if i == mb:
            sums.to_section(0)
        hook(i)
    sums.to_core(2, 3)
    sums.to_section(1)
    sums.to_pair()
    hook(2 * mb)


def product(dst, k, left, right, nt=256):
    rows = dst.shape[2]

    def step(j, carry):
        cols = pl.ds(pl.multiple_of(j * nt, nt), nt)
        v = row_dot(left[:, :, :, :, :, cols].reshape(-1, nt), right()).astype(BF)
        dst[k, pl.ds(j * (nt // rows), nt // rows)] = v.reshape(nt // rows, rows, v.shape[-1])
        return carry

    lax.fori_loop(0, left.shape[-1] // nt, step, 0)


def flat(ref):
    v = ref[...]
    return v.reshape(-1, v.shape[-1])


PACE = (
    (0, 1, 1, 1, 2),
    (5, 3),
    (1, 1, 1, 1),
    (1, 0, 0, 0, 2),
    (5, 3),
    (2, 2, 2, 2, 2),
    (5, 2),
)


def forward_all(
    qkv, o, up, dn, x_in, cot, own_qv, own_up, own_vecs, slopes, own_pen,
    c_all, x1, vecs, bias_up, pen, qkv_h, o_h, up_h, dn_h, wqkv0, wo0, wup0, wdn0, wqkv1, wo1, wup1, wdn1,
    normed0, proj0, mixed0, xo0, hid0, nt0, normed1, proj1, mixed1, xo1, hid1, nt1,
    part, tbuf, rbuf, sems0, sems1, sems2, xbuf, normed, two, proj, mixed, act, hidden, x_own,
    wqkv, wo, wup, wdn, wsems, stash_sems, msems, xsems, cot_stage, psems, bias, wide_up, *rest
):
    stage, packs = rest[:4], rest[4:]
    me = Place()
    me.meet()
    mb = part.shape[1]
    cq, hq = wo.shape[-1], wup.shape[-1]
    tile = 512
    quarter = me.s * 2 + me.zl

    swaps = [
        remote(src, dst.at[me.s], psems.at[0, i], psems.at[1, i], s=me.s ^ 1)
        for i, (src, dst) in enumerate(((own_vecs, vecs), (own_qv, bias), (own_up, wide_up)))
    ]
    swaps.append(remote(own_pen, pen.at[me.zl], psems.at[0, 3], psems.at[1, 3], zl=me.zl ^ 1))
    for c in swaps:
        c.start()
    vecs[me.s] = own_vecs[...]
    bias[me.s] = own_qv[...]
    wide_up[me.s] = own_up[...]
    pen[me.zl] = own_pen[...]

    jobs = []
    for p, (own, half) in enumerate(((qkv, qkv_h), (o, o_h), (up, up_h), (dn, dn_h))):
        w = own.shape[-1] // 2
        cols = lambda q, w=w: pl.ds(pl.multiple_of(q * w, w), w)
        there = remote(own.at[:, :, cols(me.s ^ 1)], half.at[me.s], msems.at[p, 0], msems.at[p, 1], s=me.s ^ 1)
        here = Staged(own.at[:, :, cols(me.s)], half.at[me.s], stage[p], msems.at[p, pl.ds(2, 2)])
        jobs.append((there, here))
    for there, _ in jobs[:2]:
        there.start()
    x_local = pltpu.make_async_copy(x_in, xbuf.at[me.zl], xsems.at[0, 4])
    x_across = remote(
        x_in.at[:, :, me.t], xbuf.at[me.zl, :, :, me.t], xsems.at[0, 0], xsems.at[0, 1], zl=me.zl ^ 1
    )
    x_piece = xbuf.at[me.zl ^ 1, :, :, me.t]
    x_cross = remote(x_piece, x_piece, xsems.at[0, 2], xsems.at[0, 3], t=me.t ^ 1)
    c_local = Staged(cot, c_all.at[me.zl], cot_stage, xsems.at[1, pl.ds(4, 2)])
    c_across = remote(cot.at[:, :, me.t], c_all.at[me.zl, :, :, me.t], xsems.at[1, 0], xsems.at[1, 1], zl=me.zl ^ 1)
    c_piece = c_all.at[me.zl ^ 1, :, :, me.t]
    c_cross = remote(c_piece, c_piece, xsems.at[1, 2], xsems.at[1, 3], t=me.t ^ 1)
    x_across.start()
    for _, here in jobs:
        here.start()
    x_local.start()
    c_local.start()
    for _, here in jobs:
        here.turn()
    c_local.turn()
    x_local.wait()

    def norm(a, layer):
        for m in range(mb):
            norm_rows(xbuf, normed, a, m, vecs[layer, 0:1], vecs[layer, 1:2])

    for c in swaps:
        c.wait()
    up_cols = pl.ds(pl.multiple_of(quarter * hq, hq), hq)
    for layer in range(2):
        bias_up[layer] = wide_up[layer, :, up_cols]
    qv_cols = pl.ds(pl.multiple_of(quarter * cq, cq), cq)
    for there, here in jobs[:2]:
        here.wait()
        there.wait_recv()
    att0 = Fetch(me, 0, ((qkv_h, wqkv0), (o_h, wo0)), packs[0], packs[1:3])
    ff0 = Fetch(me, 0, ((up_h, wup0), (dn_h, wdn0)), packs[3], packs[4:6])
    att1 = Fetch(me, 1, ((qkv_h, wqkv1), (o_h, wo1)), packs[6], packs[1:3])
    ff1 = Fetch(me, 1, ((up_h, wup1), (dn_h, wdn1)), packs[7], packs[4:6])

    def gate(*js):
        def wait():
            for j in js:
                jobs[j][1].wait()
                jobs[j][0].wait_recv()

        return wait

    per = 2 * PARTS
    pump = Pump(
        att0.units((0, 1)),
        ff0.units((0,), gate(2)),
        ff0.units((1,), gate(3)),
        att1.units((0, 1)),
        ff1.units((0,)),
        ff1.units((1,)),
    )
    pump.step(per)
    for there, _ in jobs[2:]:
        there.start()
    x_across.wait_recv()
    x_cross.start()
    norm(me.zl, 0)
    pump.waiting.pop(0)[2]()
    x_cross.wait()
    norm(me.zl ^ 1, 0)
    pump.step(per)
    pump.through(per)
    c_across.start()

    loads = {}

    def load(i, src, dst):
        loads[i] = pltpu.make_async_copy(src, dst, wsems.at[i])
        loads[i].start()

    stashes = []

    def stash(src, dst):
        c = pltpu.make_async_copy(src, dst, stash_sems.at[len(stashes)])
        c.start()
        stashes.append(c)

    def attention(layer, sums, hook):
        def group(a, m):
            if layer:
                norm_rows(xbuf, normed, a, m, vecs[layer, 0:1], vecs[layer, 1:2])
            nv = rows_of(normed, a, m)
            for k in range(3):
                v = dot(nv, flat(wqkv.at[k]))
                if k == 0:
                    v = v + bias[layer, 0:1, qv_cols]
                if k == 2:
                    v = v + bias[layer, 1:2, qv_cols]
                proj[k, a, m] = v.astype(BF)
            pv = pen[a, m].astype(F32)
            for pair in range(cq // (2 * HEAD_DIM)):
                cols = slice(pair * 2 * HEAD_DIM, (pair + 1) * 2 * HEAD_DIM)
                q, k, v = proj[0, a, m, :, cols], proj[1, a, m, :, cols], proj[2, a, m, :, cols]
                got = []
                for h in range(2):
                    probs = softmax_parts(jnp.where(head_mask(h), q, jnp.zeros_like(q)), k, pv, slopes[pair * 2 + h])
                    got.append(dot(probs.astype(BF), v))
                mixed[a, m, :, cols] = jnp.where(head_mask(0), got[0], got[1]).astype(BF)
            put_rows(part, a, m, dot_t(mixed[a, m], flat(wo)).astype(BF))

        halves_apart(me, mb, group, sums, hook)

    def attention_rows(layer):
        def rows(m, r, v):
            xr = xbuf[me.zl, m, me.s, me.t, r]
            x_own[m, r] = xr
            hid = xr.astype(F32) + v + vecs[layer, 4:5]
            hidden[m, r] = hid
            vh, _ = normalize(hid)
            return (vh * vecs[layer, 2:3] + vecs[layer, 3:4]).astype(BF)

        return rows

    sums = Sums(me, part, two, tbuf, rbuf, sems0)
    att0.ready(0, 1)
    load(0, wqkv0, wqkv)
    load(1, wo0, wo)
    loads[0].wait()
    loads[1].wait()

    def paced(*steps):
        return lambda i: pump.step(steps[i]) if i < len(steps) else None

    attention(0, sums, paced(*PACE[0]))
    stash(normed, normed0)
    stash(proj, proj0)
    stash(mixed, mixed0)
    sums.finish(attention_rows(0))
    sums.spread()
    pump.step(PACE[1][0])
    stash(hidden, hid0)
    stash(x_own, xo0)
    c_across.wait_recv()
    c_cross.start()
    sums.collect(lambda: pump.step(PACE[1][1]))
    stash(two, nt0)
    pump.through(2 * per)
    ff0.ready(0)
    load(2, wup0, wup)
    loads[2].wait()

    def up_group(a, m):
        nv = rows_of(two, a, m)
        for j in range(hq // tile):
            cols = slice(j * tile, (j + 1) * tile)
            u = dot(nv, wup[:, :, :, cols].reshape(-1, tile)) + bias_up[0, :, cols]
            act[a, m, :, cols] = (u * (0.5 + 0.5 * lax.erf(u * (0.5**0.5)))).astype(BF)

    for i in range(2 * mb):
        up_group(i // mb, i % mb)
        pump.step(PACE[2][i])
    pump.through(3 * per)
    ff0.ready(1)
    load(3, wdn0, wdn)
    loads[3].wait()
    sums = Sums(me, part, xbuf, tbuf, rbuf, sems1)
    halves_apart(
        me, mb, lambda a, m: put_rows(part, a, m, dot_t(act[a, m], flat(wdn)).astype(BF)), sums, paced(*PACE[3])
    )
    sums.finish(lambda m, r, v: (hidden[m, r] + v + vecs[0, 5:6]).astype(BF))
    sums.spread()
    pump.step(PACE[4][0])
    sums.collect(lambda: pump.step(PACE[4][1]))
    stash(xbuf.at[me.zl], x1)
    for c in stashes[:-1]:
        c.wait()
    pump.through(4 * per)
    att1.ready(0, 1)
    load(4, wqkv1, wqkv)
    load(5, wo1, wo)
    loads[4].wait()
    loads[5].wait()

    sums = Sums(me, part, two, tbuf, rbuf, sems2)

    attention(1, sums, paced(*PACE[5]))
    n_done = len(stashes) - 1
    stash(normed, normed1)
    stash(proj, proj1)
    stash(mixed, mixed1)
    sums.finish(attention_rows(1))
    sums.spread()
    pump.step(PACE[6][0])
    stash(hidden, hid1)
    stash(x_own, xo1)
    sums.collect(lambda: pump.step(PACE[6][1]))
    stash(two, nt1)
    pump.through(6 * per)
    ff1.ready(0, 1)
    for c in (att0, ff0, att1, ff1):
        c.finish()
    for c in stashes[n_done:]:
        c.wait()
    for there, _ in jobs:
        there.wait_send()
    x_across.wait_send()
    c_local.wait()
    c_across.wait_send()
    c_cross.wait()


def ln_back(e, v, gain):
    vh, r = normalize(v)
    f = e * gain
    grad = r * (f - jnp.mean(f, -1, keepdims=True) - vh * jnp.mean(f * vh, -1, keepdims=True))
    return grad, e * vh


def fold(v):
    return v[:8] + v[8:]


PACE_FF = (3, (1, 1, 1, 1, 1), 2, 4, 2, 2)
PACE_ATT = ((3, (0, 1, 1, 0, 2), 0, 2), (3, (1, 1, 1, 1, 1), 2, 4, 2))


def ff_backward(layer, plan, g, normed_two, wup, wdn, vecs, hidden, bias, *rest):
    rest = list(rest)
    vecs, bias = vecs.at[layer], bias.at[layer]
    chain = bool(plan[0])
    n_in, n_out = sum(plan) + plan[1], sum(plan) + (plan[0] if chain else 0)
    ins, rest = rest[:n_in], rest[n_in:]
    g_up_out, g_dn_out, act_out, grad_hidden, small, small_up, full, dn_sum = rest[:8]
    outs, rest = rest[8 : 8 + n_out], rest[8 + n_out :]
    part, tbuf, rbuf, sems, gu, ysems, g_up, g_dn, act, osems = rest[:10]
    writes = [
        pltpu.make_async_copy(a, b, osems.at[i])
        for i, (a, b) in enumerate(((act, act_out), (g_dn, g_dn_out), (g_up, g_up_out)))
    ]
    me = Place()
    me.meet()
    moves = Moves(me, plan, chain, layer + 1, ins, outs, rest[10:])
    moves.start(PACE_FF[0])
    sums = Sums(me, part, full, tbuf, rbuf, sems)
    mb = g.shape[1]
    hq = wup.shape[-1]
    tile = 512
    small[...] = jnp.zeros_like(small)
    small_up[...] = jnp.zeros_like(small_up)

    def group(a, m):
        gv = rows_of(g, a, m)
        nv = rows_of(normed_two, a, m)
        for j in range(hq // tile):
            cols = slice(j * tile, (j + 1) * tile)
            u = dot(nv, wup[:, cols]) + bias[:, cols]
            cdf = 0.5 + 0.5 * lax.erf(u * (0.5**0.5))
            act[a, m, :, cols] = (u * cdf).astype(BF)
            slope = cdf + u * (jnp.exp(-0.5 * u * u) * 0.3989422804014327)
            v = (dot(gv, wdn[:, cols]) * slope).astype(BF)
            gu[a, m, :, cols] = v
            small_up[:, cols] += jnp.sum(v.astype(F32).reshape(-1, 8, tile), axis=0)
        put_rows(part, a, m, dot_t(gu[a, m], wup[...]).astype(BF))

    halves_apart(me, mb, group, sums, lambda i: moves.step(PACE_FF[1][i]))
    product(g_dn, 0, g, lambda: flat(act))
    for c in writes[:2]:
        c.start()
    down = YSum(me, g_dn, None, dn_sum, ysems)
    down.start()
    moves.middle()
    moves.step(PACE_FF[2])

    def rows(m, r, e):
        grad, ev = ln_back(e, hidden[m, r], vecs[2:3])
        go = g[me.zl, m, me.s, me.t, r].astype(F32)
        grad = go + grad
        grad_hidden[m, r] = grad
        small[0] += fold(ev)
        small[1] += fold(e)
        small[2] += fold(grad)
        small[3] += fold(go)
        return grad.astype(BF)

    sums.finish(rows)
    sums.spread()
    moves.step(PACE_FF[3])
    moves.more_x()
    product(g_up, 0, normed_two, lambda: flat(gu))
    writes[2].start()
    moves.step(PACE_FF[4])
    sums.collect(lambda: moves.step(PACE_FF[5]))
    moves.finish()
    down.add()
    down.finish()
    for c in writes:
        c.wait()


class LocalSpread:
    def __init__(self, me, layer, full, sems):
        self.me, self.layer = me, layer
        here, there = full.at[:, me.s, me.t], full.at[:, me.s ^ 1, me.t]
        self.across = remote(here, here, sems.at[0, 0], sems.at[1, 0], s=me.s ^ 1)
        self.crosses = [
            remote(piece, piece, sems.at[0, i + 1], sems.at[1, i + 1], t=me.t ^ 1)
            for i, piece in enumerate((here, there))
        ]

    def start(self):
        @pl.when(self.me.s != self.layer)
        def _():
            self.across.start()

        self.crosses[0].start()

    def finish(self):
        @pl.when(self.me.s == self.layer)
        def _():
            self.across.wait_recv()
            self.crosses[1].start()
            self.crosses[1].wait()

        self.crosses[0].wait()

        @pl.when(self.me.s != self.layer)
        def _():
            self.across.wait_send()


class Rows:
    def __init__(self, me, ref):
        self.me, self.ref = me, ref

    def __setitem__(self, idx, value):
        _, m, s, t, r = idx
        self.ref[m, s, t, r] = value


def att_backward(layer, last, plan, gb, x_own, normed_in, proj, mixed_in, wqkv, wo, vecs, slopes, pen, grad_hidden, *rest):
    vecs = vecs.at[layer]
    rest = list(rest)
    n_in, n_out = sum(plan) + plan[1], sum(plan) + (plan[0] if last else 0)
    ins, rest = rest[:n_in], rest[n_in:]
    g_qkv_out, g_o_out, small, small_p, full = rest[:5]
    outs, rest = rest[5 : 5 + n_out], rest[5 + n_out :]
    if last:
        x_dn0, tot_qkv, tot_o = rest[:3]
        rest = rest[3:]
    part, tbuf, rbuf, sems, gp, lsems, dsems, ysems, normed, mixed, g_qkv, g_o, osems = rest[:13]
    reads = [pltpu.make_async_copy(normed_in, normed, osems.at[0]), pltpu.make_async_copy(mixed_in, mixed, osems.at[1])]
    writes = [pltpu.make_async_copy(g_o, g_o_out, osems.at[2]), pltpu.make_async_copy(g_qkv, g_qkv_out, osems.at[3])]
    for c in reads:
        c.start()
    me = Place()
    me.meet()
    moves = Moves(me, plan, last, layer + 1, ins, outs, rest[13:])
    pace = PACE_ATT[1 if last else 0]
    moves.start(pace[0])
    if last:
        early = XMove(me, layer, moves.z[0].out, x_dn0, dsems)
    sums = Sums(me, part, Rows(me, full) if last else full, tbuf, rbuf, sems)
    mb = gb.shape[1]
    cq = wo.shape[-1]
    small[...] = jnp.zeros_like(small)
    small_p[...] = jnp.zeros_like(small_p)
    scale = float(HEAD_DIM) ** -0.5

    def group(a, m):
        gm_all = dot(rows_of(gb, a, m), wo[...]).astype(BF)
        pv = pen[a, m].astype(F32)
        for pair in range(cq // (2 * HEAD_DIM)):
            cols = slice(pair * 2 * HEAD_DIM, (pair + 1) * 2 * HEAD_DIM)
            q, k, v = proj[0, a, m, :, cols], proj[1, a, m, :, cols], proj[2, a, m, :, cols]
            gm = gm_all[:, cols]
            gq, gk, gv = [], [], []
            for h in range(2):
                zero = jnp.zeros_like(q)
                probs = softmax_parts(jnp.where(head_mask(h), q, zero), k, pv, slopes[pair * 2 + h])
                gpr = dot_t(jnp.where(head_mask(h), gm, zero), v)
                gv.append(row_dot(probs.astype(BF), gm))
                pg = probs * gpr
                gs = (pg - probs * jnp.sum(pg, axis=-1, keepdims=True)).astype(BF)
                gq.append(dot(gs, k))
                gk.append(row_dot(gs, q))
            for i, (both, f) in enumerate(((gq, scale), (gk, scale), (gv, 1.0))):
                out = (jnp.where(head_mask(0), both[0], both[1]) * f).astype(BF)
                gp[i, a, m, :, cols] = out
                small_p[i, :, cols] += jnp.sum(out.astype(F32).reshape(-1, 8, 2 * HEAD_DIM), axis=0)
        total = dot_t(gp[0, a, m], wqkv[0]) + dot_t(gp[1, a, m], wqkv[1]) + dot_t(gp[2, a, m], wqkv[2])
        put_rows(part, a, m, total.astype(BF))

    halves_apart(me, mb, group, sums, lambda i: moves.step(pace[1][i]))
    for c in reads:
        c.wait()
    product(g_o, 0, gb, lambda: mixed[...].reshape(-1, cq))
    writes[0].start()

    def rows(m, r, e):
        grad, ev = ln_back(e, x_own[m, r].astype(F32), vecs[0:1])
        small[0] += fold(ev)
        small[1] += fold(e)
        return (grad_hidden[m, r] + grad).astype(BF)

    def qkv_products():
        for k in range(3):
            product(g_qkv, k, normed, lambda k=k: gp[k].reshape(-1, cq))
        writes[1].start()

    if last:
        moves.middle()
        moves.step(pace[2])
        qkv_products()
        here = [YSum(me, g_qkv, None, tot_qkv, ysems.at[0]), YSum(me, g_o, None, tot_o, ysems.at[1])]
        for c in here:
            c.start()
        sums.finish(rows)
        local = LocalSpread(me, layer, full, lsems)
        local.start()
        moves.step(pace[3])
        moves.more_x()
        moves.z[0].add()
        early.start(0)
        early.start(1)
        local.finish()
        moves.step(pace[4])
        for c in here:
            c.add()
        moves.z[0].finish()
        moves.z = moves.z[1:]
        moves.finish()
        for c in here:
            c.finish()
        early.finish()
    else:
        sums.finish(rows)
        sums.spread()
        moves.step(pace[3])
        moves.middle()
        qkv_products()
        sums.collect()
        moves.finish()
    for c in writes:
        c.wait()


def last_sums(
    log_outer, act, wdn, hidden, vecs, sf0, su0, sa0, sp0, sf1, su1, sa1, sp1, t_qkv, t_o, g_qkv, g_o, h_up0,
    x_up0, h_qkv0, h_o0, x_qkv0, x_o0, sec, total,
    part, tbuf, rbuf, sems, lsems, xsems, heap, hsems, *zbufs
):
    me = Place()
    me.meet()
    zs = [
        ZSum(me, a, b, *zbufs[4 * i : 4 * i + 3], c, zbufs[4 * i + 3])
        for i, (a, b, c) in enumerate(((t_qkv, g_qkv, h_qkv0), (t_o, g_o, h_o0)))
    ]
    pump = Pump([(lambda group=group: [u() for u, _ in group], None) for group in zip(*(z.units() for z in zs))])
    pump.step(2)
    for z in zs:
        z.start()
    xs = [
        XMove(me, 0, a, b, xsems.at[i])
        for i, (a, b) in enumerate(((h_up0, x_up0), (h_qkv0, x_qkv0), (h_o0, x_o0)))
    ]
    xs[0].start(0)
    mb = act.shape[1]
    sums = Sums(me, part, Rows(me, sec), tbuf, rbuf, sems)

    def group(a, m):
        put_rows(part, a, m, dot_t(act[a, m], wdn[...]).astype(BF))

    width, cq, hq = total.shape[1], sp0.shape[-1], su0.shape[-1]
    place = me.t * 4 + me.s * 2 + me.zl
    total[...] = jnp.zeros_like(total)
    for layer, (sf, su, sa, sp) in enumerate(((sf0, su0, sa0, sp0), (sf1, su1, sa1, sp1))):
        base = layer * (total.shape[0] // 2)
        for i, v in enumerate((sa[0], sf[0], sa[1], sf[1], sf[2], sf[3])):
            total[base + i : base + i + 1] = jnp.sum(v, axis=0, keepdims=True)
        for i, j in enumerate((0, 2)):
            cols = pl.ds(pl.multiple_of(place * cq, cq), cq)
            total[base + 6 + i : base + 7 + i, cols] = jnp.sum(sp[j], axis=0, keepdims=True)
        for i in range(8 * hq // width):

            @pl.when(place // (width // hq) == i)
            def _(i=i, base=base, su=su):
                cols = pl.ds(pl.multiple_of((place % (width // hq)) * hq, hq), hq)
                total[base + 8 + i : base + 9 + i, cols] = jnp.sum(su[...], axis=0, keepdims=True)

    peers = [{"t": me.t ^ 1}, {"y": me.y ^ 1}, {"s": me.s ^ 1}, {"zl": me.zl ^ 1}]
    peers += [{"zh": me.zh ^ (1 << b)} for b in range(log_outer)]

    def butterfly(lo, hi):
        for i in range(lo, min(hi, len(peers))):
            c = remote(total, heap.at[i], hsems.at[0, i], hsems.at[1, i], **peers[i])
            c.start()
            c.wait()
            total[...] += heap[i]

    halves_of(me, mb, group, sums)
    pump.step(2)
    xs[0].start(1)
    butterfly(0, 2)
    pump.step(4)
    sums.finish(lambda m, r, v: (hidden[m, r] + v + vecs[1, 5:6]).astype(BF))
    local = LocalSpread(me, 1, sec, lsems)
    local.start()
    butterfly(2, 3)
    for z, x in zip(zs, xs[1:]):
        z.add()
        x.start(0)
        x.start(1)
    local.finish()
    butterfly(3, 99)
    for c in zs + xs:
        c.finish()


def pick(v, index, dim):
    return lax.dynamic_index_in_dim(v, index, dim, keepdims=False)


def shards(x_in, cotangent, layout, w_qkv, b_qv, w_out, w_fc1, b_fc1, w_fc2, gains, biases):
    s, zl, t = (lax.axis_index(a) for a in ("s", "zl", "t"))
    outer = lax.axis_size("zh")
    far, nb = outer * 2, outer * 4
    log_outer = outer.bit_length() - 1
    mb, rows_mb, width = x_in.shape
    wrows = w_out.shape[1]
    block = w_out.shape[2]
    hid = w_fc1.shape[2]
    cq, hq = block // 4, hid // 4
    share = rows_mb // 4
    tokens = (2, mb, 2, 2, share, width)

    quarter = s * 2 + zl
    own_vecs = jnp.concatenate([jnp.stack([gains[0, 0], biases[0, 0], gains[0, 1], biases[0, 1]]), biases[0, 2:]])
    own_pen = jax.vmap(geometry)(layout.reshape(mb, rows_mb)).astype(BF)
    local_heads = cq // HEAD_DIM
    head_ids = t * (block // HEAD_DIM) + quarter * local_heads + jnp.arange(local_heads, dtype=jnp.int32)
    slopes = jnp.exp2(-8.0 * (head_ids + 1).astype(F32) / HEADS)

    own_shape = (mb, 2, 2, share, width)
    qk, oo, ff = (3, cq), (1, cq), (1, hq)
    att_w = [((3, nb, wrows, cq), BF), ((1, nb, wrows, cq), BF)]
    ff_w = [((1, nb, wrows, hq), BF)] * 2
    own_rows = (mb, share, width)
    hidden_shape = (2, mb, rows_mb, hq)
    proj_shape = (3, 2, mb, rows_mb, cq)
    mixed_shape = (2, mb, rows_mb, cq)
    act_scratch = sums_scratch(mb, share, width)
    halves = [((2, k, wrows, 2 * c), BF) for k, c in (qk, oo, ff, ff)]
    stash_outs = [
        (tokens, BF),
        (proj_shape, BF),
        (mixed_shape, BF),
        (own_rows, BF),
        (own_rows, F32),
        (tokens, BF),
    ]
    outs = [(tokens, BF), (own_shape, BF)]
    outs += [((2, 6, width), F32), ((2, 1, hq), F32), ((2, mb, GROUP, GROUP), BF)]
    outs += halves + (att_w + ff_w) * 2 + stash_outs * 2
    sem = pltpu.SemaphoreType.DMA
    cot, x1, vecs, bias_up, pen, _, _, _, _, wqkv0, wo0, wup0, wdn0, wqkv1, wo1, wup1, wdn1, *stashed = call(
        forward_all,
        0,
        (
            w_qkv[0].transpose(1, 0, 2),
            w_out,
            w_fc1,
            w_fc2,
            x_in.reshape(own_shape),
            cotangent.reshape(own_shape),
            b_qv[0],
            b_fc1,
            own_vecs,
            slopes,
            own_pen,
        ),
        [AN] * 6 + [VM] * 3 + [SM, VM],
        outs,
        [AN] * 2 + [VM] * 3 + [AN] * (len(outs) - 5),
        act_scratch
        + [sem((8, 4))] * 2
        + [pltpu.VMEM(tokens, BF)] * 3
        + [pltpu.VMEM(sh, BF) for sh in (proj_shape, mixed_shape, hidden_shape)]
        + [pltpu.VMEM(own_rows, F32), pltpu.VMEM(own_rows, BF)]
        + [pltpu.VMEM(sh, dt) for sh, dt in att_w + ff_w]
        + [sem((6,)), sem((13,)), sem((4, 4)), sem((2, 6)), pltpu.VMEM(own_shape, BF)]
        + [sem((2, 4)), pltpu.VMEM((2, 2, block), F32), pltpu.VMEM((2, 1, hid), F32)]
        + [pltpu.VMEM((k, wrows, 2 * c), BF) for k, c in (qk, oo, ff, ff)]
        + fetch_scratch((qk, oo), far, wrows)
        + fetch_scratch((ff, ff), far, wrows)
        + [sem((2, 5, far))] * 2,
    )
    normed0, proj0, mixed0, xo0, hidden0, nt0, normed1, proj1, mixed1, xo1, hidden1, nt1 = stashed
    wup0, wdn0, wup1, wdn1 = (w.reshape(width, hq) for w in (wup0, wdn0, wup1, wdn1))

    def ff_bwd(layer, cid, ins, plan, arrays):
        m_specs, m_outs, m_out_specs, m_scratch = moves_parts(plan, bool(plan[0]), far, wrows)
        outs = [
            ((1, nb, wrows, hq), BF),
            ((1, nb, wrows, hq), BF),
            (hidden_shape, BF),
            (own_rows, F32),
            ((4, 8, width), F32),
            ((8, hq), F32),
            (tokens, BF),
            ((1, far - 1, wrows, hq), BF),
        ]
        scratch = act_scratch + [
            pltpu.VMEM(hidden_shape, BF),
            pltpu.SemaphoreType.DMA((3, far)),
            pltpu.VMEM((1, nb, wrows, hq), BF),
            pltpu.VMEM((1, nb, wrows, hq), BF),
            pltpu.VMEM(hidden_shape, BF),
            sem((3,)),
        ]
        return call(
            functools.partial(ff_backward, layer, tuple(len(p) for p in plan)),
            cid,
            list(ins) + list(arrays),
            [VM] * len(ins) + m_specs,
            outs + m_outs,
            [AN] * 3 + [VM] * (len(outs) - 3) + m_out_specs,
            scratch + m_scratch,
        )

    def att_bwd(layer, cid, ins, plan, arrays):
        last = layer == 0
        m_specs, m_outs, m_out_specs, m_scratch = moves_parts(plan, last, far, wrows)
        outs = att_w + [((2, 8, width), F32), ((3, 8, cq), F32), (own_shape if last else tokens, BF)]
        scratch = act_scratch + [pltpu.VMEM(proj_shape, BF), sem((2, 3)), sem((2, 2)), sem((2, 3, far))]
        scratch += [pltpu.VMEM(sh, dt) for sh, dt in [(tokens, BF), (mixed_shape, BF)] + att_w] + [sem((4,))]
        return call(
            functools.partial(att_backward, layer, last, tuple(len(p) for p in plan)),
            cid,
            list(ins) + list(arrays),
            [VM, VM, AN, VM, AN] + [VM] * 3 + [SM, VM, VM] + m_specs,
            outs + m_outs + ([((1, wrows, 2 * hq), BF)] + [((k, far - 1, wrows, c), BF) for k, c in (qk, oo)]) * last,
            [AN, AN] + [VM] * (len(outs) - 2) + m_out_specs + [AN, VM, VM] * last,
            scratch + m_scratch,
        )

    wqkv0, wo0 = wqkv0.reshape(3, width, cq), wo0.reshape(width, cq)
    wqkv1, wo1 = wqkv1.reshape(3, width, cq), wo1.reshape(width, cq)
    g_up1, g_dn1, act1, gh1, sf1, su1, gb1, dn1_total = ff_bwd(
        1, 4, (cot, nt1, wup1, wdn1, vecs, hidden1, bias_up), ((), (), ()), ()
    )
    g_qkv1, g_o1, sa1, sp1, g0, up1_total, h_dn1 = att_bwd(
        1,
        5,
        (gb1, xo1, normed1, proj1, mixed1, wqkv1, wo1, vecs, slopes, pen, gh1),
        ((ff,), (ff,), ()),
        (g_up1, dn1_total, g_dn1),
    )
    g_up0, g_dn0, _, gh0, sf0, su0, gb0, dn0_total, _, _, h_up1, x_dn1, h_qkv1, h_o1 = ff_bwd(
        0,
        6,
        (g0, nt0, wup0, wdn0, vecs, hidden0, bias_up),
        ((qk, oo), (ff,), (ff,)),
        (g_qkv1, g_o1, up1_total, g_up1, h_dn1),
    )
    g_qkv0, g_o0, sa0, sp0, gin, _, h_dn0, x_up1, x_qkv1, x_o1, h_up0, x_dn0, qkv0_total, o0_total = att_bwd(
        0,
        7,
        (gb0, xo0, normed0, proj0, mixed0, wqkv0, wo0, vecs, slopes, pen, gh0),
        ((ff,), (ff,), (ff, qk, oo)),
        (g_up0, dn0_total, g_dn0, h_up1, h_qkv1, h_o1),
    )

    n_small = 2 * (6 + (16 * cq + 8 * hq) // width)

    def half(k, c):
        return ((k, wrows, 2 * c), BF)

    x_up0, h_qkv0, h_o0, x_qkv0, x_o0, sec1, total = call(
        functools.partial(last_sums, log_outer),
        8,
        (act1, wdn1, hidden1, vecs, sf0, su0, sa0, sp0, sf1, su1, sa1, sp1)
        + (qkv0_total, o0_total, g_qkv0, g_o0, h_up0),
        [VM] * 14 + [AN] * 3,
        [half(*ff), half(*qk), half(*oo), half(*qk), half(*oo)] + [(own_shape, BF), ((n_small, width), F32)],
        [AN] + [VM] * 2 + [AN] * 2 + [VM] * 2,
        act_scratch
        + [sem((2, 3)), sem((3, 2, 2)), pltpu.VMEM((4 + log_outer, n_small, width), F32), sem((2, 4 + log_outer))]
        + z_scratch(*qk, far, wrows)
        + z_scratch(*oo, far, wrows),
    )

    def home(own0, got0, own1, got1):
        left = jnp.where(s == 0, own0, got1)
        right = jnp.where(s == 0, got0, own1)
        return jnp.concatenate([left, right], axis=-1).astype(F32)

    g_qkv = home(h_qkv0, x_qkv0, h_qkv1, x_qkv1).transpose(1, 0, 2)[None]
    g_out = home(h_o0, x_o0, h_o1, x_o1)
    g_fc1 = home(h_up0, x_up0, h_up1, x_up1)
    g_fc2 = home(h_dn0, x_dn0, h_dn1, x_dn1)

    def of_layer(first, second):
        return jnp.where(s == 0, first.reshape(mb, rows_mb, width), second.reshape(mb, rows_mb, width))[None]

    section_outputs = of_layer(x1, sec1)
    input_grads = of_layer(gin, pick(g0, zl, 0))
    total = pick(total.reshape(2, n_small // 2, width), s, 0)
    n_qv = 16 * cq // width
    grad_gains = total[:2][None]
    grad_biases = total[2:6][None]
    grad_b_qv = pick(total[6 : 6 + n_qv].reshape(1, 2, 2, 4 * cq), t, 2)
    grad_b_fc1 = pick(total[6 + n_qv :].reshape(1, 2, 4 * hq), t, 1)
    return section_outputs, input_grads, g_qkv, grad_b_qv, g_out, g_fc1, grad_b_fc1, g_fc2, grad_gains, grad_biases


def solution(mesh):
    n_s, n_dp, n_t = mesh.shape["section"], mesh.shape["dp"], mesh.shape["tensor"]
    fine = Mesh(mesh.devices.reshape(n_s, n_dp // 4, 2, 2, n_t), ("s", "zh", "zl", "y", "t"))
    return jax.shard_map(
        shards,
        mesh=fine,
        in_specs=(
            P(None, DP, None),
            P(None, DP, None),
            P(None, DP),
            P("s", DP, None, "t"),
            P("s", None, "t"),
            P("s", DP, "t"),
            P("s", DP, "t"),
            P("s", "t"),
            P("s", DP, "t"),
            P("s", None, None),
            P("s", None, None),
        ),
        out_specs=(
            P("s", None, DP, None),
            P("s", None, DP, None),
            P("s", DP, None, "t"),
            P("s", None, "t"),
            P("s", DP, "t"),
            P("s", DP, "t"),
            P("s", "t"),
            P("s", DP, "t"),
            P("s", None, None),
            P("s", None, None),
        ),
        check_vma=False,
    )
```

time: 1780 us -> 870 us (0.49)
  waiting for transfers between devices: 1070 us -> 0 us
  Pallas kernels: 0 us -> 831 us
  local copies, waits for them, and re-layouts: 257 us -> 9.76 us
  other arithmetic: 208 us -> 18.8 us
  matrix products: 138 us -> 0 us
  starting transfers between devices: 74.4 us -> 0 us
    ppermute x84 -> x0, waiting for transfers between devices: 962 us -> none  [swap(): return lax.ppermute(v, axis, [(i, i ^ offset) for i in range(n)])]
    pallas_call x0 -> x6, Pallas kernels: none -> 831 us  [call(): pl.pallas_call(body, out_shape=[jax.ShapeDtypeStruct(sh, dt) for sh, dt i...]
    dot_general x36 -> x0, matrix products: 138 us -> none  [the longest x8 41.3 us: row_dot(): lax.dot_general(a, b, (((0,), (0,)), ((), ())), preferred_element_type=F32)]
    psum x1 -> x0, waiting for transfers between devices: 111 us -> none  [shards(): total = lax.psum(jnp.stack(pieces), ('s', 'zh', 'zl', 'y', 't'))]
    another operation x85 -> x0, other arithmetic: 95.9 us -> none  [the longest x58 48.6 us: in_order(): return jnp.stack([first, second], axis=dim)]
    ppermute x84 -> x0, starting transfers between devices: 74.3 us -> none  [swap(): return lax.ppermute(v, axis, [(i, i ^ offset) for i in range(n)])]
    unnamed x344 -> x37, local copies, waits for them, and re-layouts: 72.9 us -> 3.58 us
    dot_general x7 -> x0, local copies, waits for them, and re-layouts: 45.4 us -> none  [row_dot(): lax.dot_general(a, b, (((0,), (0,)), ((), ())), preferred_element_type=F32)]
  transfers between devices with their start and end apart: 85 -> 0, of which waited for: 49 -> 0; matrix products, arithmetic and copies ran while one was open for 23% -> 0% of each run, Pallas kernels for 0% -> 0%
where the time goes in v3:
time: 870 us; the launch traced here: 860 us
  Pallas kernels  831 us (96%)
  other arithmetic  18.8 us (2%)
  local copies, waits for them, and re-layouts  9.76 us (1%)
    pallas_call x6, Pallas kernels, call(): pl.pallas_call(body, out_shape=[jax.ShapeDtypeStruct(sh, dt) for sh, dt i...  831 us

profile of v3, /device:TPU:0, one launch (start us, length us, event | category | flops | bytes accessed | tf_op | source)
XLA Modules:
  0.0 860.4 jit_solution(13600918472238347390)
XLA Ops:
  1.2 0.9 slice_bitcast_fusion.1
  2.0 0.8 slice_bitcast_fusion
  2.8 0.7 concatenate.39.own_vecs
  3.5 0.8 convert_reduce_fusion
  4.3 1.0 fusion
  5.4 1.7 select_convert_fusion.own_pen
  7.1 373.5 %shard_map.186 = (bf16[2,2,2,2,64,2048]{5,4,3,2,1,0:T(8,128)(2,1)}, bf16[2,2,2,64,2048]{4,3,2,1,0:T(8,128)(2,1)}, f32[2,6,2048]{2,1,0:T(8,128)}, f32[2,1,1024]{2...) custom-call(bf16[3,256,1024]{2,1,0:T(8,128)(2,1)} %bitcast.48, ...), custom_call_target="tpu_custom_call" | custom-call | tf_op jit(solution)/shard_map/pallas_call | solution.py:509
  380.6 78.3 %shard_map.187 = (bf16[1,8,256,1024]{3,2,1,0:T(8,128)(2,1)}, bf16[1,8,256,1024]{3,2,1,0:T(8,128)(2,1)}, bf16[2,2,256,1024]{3,2,1,0:T(8,128)(2,1)}, f32[2,64,2048...) custom-call(bf16[2,2,2,2,64,2048]{5,4,3,2,1,0:T(8,128)(2,1)} %get-tu, ...), custom_call_target="tpu_custom_call" | custom-call | tf_op jit(solution)/shard_map/pallas_call | solution.py:509
  459.0 78.7 %shard_map.188 = (bf16[3,8,256,256]{3,2,1,0:T(8,128)(2,1)}, bf16[1,8,256,256]{3,2,1,0:T(8,128)(2,1)}, f32[2,8,2048]{2,1,0:T(8,128)}, f32[3,8,256]{2,1,0:T(8,128)...) custom-call(bf16[2,2,2,2,64,2048]{5,4,3,2,1,0:T(8,128)(2,1)} %get-tuple, ...), custom_call_target="tpu_custom_call" | custom-call | tf_op jit(solution)/shard_map/pallas_call | solution.py:509
  537.7 108.7 %shard_map.189 = (bf16[1,8,256,1024]{3,2,1,0:T(8,128)(2,1)}, bf16[1,8,256,1024]{3,2,1,0:T(8,128)(2,1)}, bf16[2,2,256,1024]{3,2,1,0:T(8,128)(2,1)}, f32[2,64,2048...) custom-call(bf16[2,2,2,2,64,2048]{5,4,3,2,1,0:T(8,128)(2,1)} %get-tu, ...), custom_call_target="tpu_custom_call" | custom-call | tf_op jit(solution)/shard_map/pallas_call | solution.py:509
  646.4 104.3 %shard_map.190 = (bf16[3,8,256,256]{3,2,1,0:T(8,128)(2,1)}, bf16[1,8,256,256]{3,2,1,0:T(8,128)(2,1)}, f32[2,8,2048]{2,1,0:T(8,128)}, f32[3,8,256]{2,1,0:T(8,128)...) custom-call(bf16[2,2,2,2,64,2048]{5,4,3,2,1,0:T(8,128)(2,1)} %get-tu, ...), custom_call_target="tpu_custom_call" | custom-call | tf_op jit(solution)/shard_map/pallas_call | solution.py:509
  750.7 1.5 broadcast_select_fusion.2
  752.7 2.5 maximum_convert_fusion.1
  755.3 87.3 %shard_map.191 = (bf16[1,256,2048]{2,1,0:T(8,128)(2,1)}, bf16[3,256,512]{2,1,0:T(8,128)(2,1)}, bf16[1,256,512]{2,1,0:T(8,128)(2,1)}, bf16[3,256,512]{2,1,0:T(8,1...) custom-call(bf16[2,2,256,1024]{3,2,1,0:T(8,128)(2,1)} %get-tuple-element.89.act, ...), custom_call_target="tpu_custom_call" | custom-call | tf_op jit(solution)/shard_map/pallas_call | solution.py:509
  842.6 1.3 broadcast_select_fusion.3
  844.0 2.5 maximum_convert_fusion
  846.6 1.1 maximum_convert_fusion.2
  848.8 2.1 convert_bitcast_fusion
  850.9 1.9 constant_dynamic-slice_fusion.5
  853.1 1.7 bitcast_select_fusion
  855.4 0.7 copy-done.6
  856.1 1.5 broadcast_select_fusion
  857.7 0.6 constant_dynamic-slice_fusion.4
  858.4 0.6 dynamic-slice_bitcast_fusion
  (49 shorter events, 4.6 us)
Async XLA Ops:
  646.3 104.4 %copy-start.8 = (bf16[1,256,2048]{2,1,0:T(8,128)(2,1)S(1)}, bf16[1,256,2048]{2,1,0:T(8,128)(2,1)}, u32[]{:S(2)}) copy-start(bf16[1,256,2048]{2,1,0:T(8,128)(2,1)} %get-tuple-element.150) | copy-start | bytes 3145732
  750.7 1.5 copy-start.1
  750.7 1.8 copy-start.10
  752.6 2.5 copy-start.2
  752.7 2.5 copy-start.9
  755.3 87.3 %copy-start = (bf16[1,256,2048]{2,1,0:T(8,128)(2,1)S(1)}, bf16[1,256,2048]{2,1,0:T(8,128)(2,1)}, u32[]{:S(2)}) copy-start(bf16[1,256,2048]{2,1,0:T(8,128)(2,1)} %get-tuple-element.124.rest_3_) | copy-start | bytes 3145732
  843.9 2.6 copy-start.14
  843.9 2.5 copy-start.16
  844.0 2.6 copy-start.7
  844.0 2.6 copy-start.15
  846.5 1.2 copy-start.11
  846.5 1.7 copy-start.13
  846.6 1.9 copy-start.3
  846.6 2.1 copy-start.12
  850.9 2.2 copy-start.5
  853.1 2.2 copy-start.4
  853.1 3.0 copy-start.6
  856.1 1.5 copy-start.17

commit v4 on v3

--- a/solution.py
+++ b/solution.py
@@ -862,7 +862,7 @@
 PACE_ATT = ((3, (0, 1, 1, 0, 2), 0, 2), (3, (1, 1, 1, 1, 1), 2, 4, 2))
 
 
-def ff_backward(layer, plan, g, normed_two, wup, wdn, vecs, hidden, bias, *rest):
+def ff_backward(layer, plan, g_in, nt_in, wup_in, wdn_in, vecs, hidden, bias, *rest):
     rest = list(rest)
     vecs, bias = vecs.at[layer], bias.at[layer]
     chain = bool(plan[0])
@@ -870,15 +870,23 @@
     ins, rest = rest[:n_in], rest[n_in:]
     g_up_out, g_dn_out, act_out, grad_hidden, small, small_up, full, dn_sum = rest[:8]
     outs, rest = rest[8 : 8 + n_out], rest[8 + n_out :]
-    part, tbuf, rbuf, sems, gu, ysems, g_up, g_dn, act, osems = rest[:10]
+    part, tbuf, rbuf, sems, gu, ysems, g_up, g_dn, act, osems, g, normed_two, wup, wdn, isems = rest[:15]
+    reads = [
+        pltpu.make_async_copy(a, b, isems.at[i])
+        for i, (a, b) in enumerate(((g_in, g), (nt_in, normed_two), (wup_in, wup), (wdn_in, wdn)))
+    ]
+    for c in reads:
+        c.start()
     writes = [
         pltpu.make_async_copy(a, b, osems.at[i])
         for i, (a, b) in enumerate(((act, act_out), (g_dn, g_dn_out), (g_up, g_up_out)))
     ]
     me = Place()
     me.meet()
-    moves = Moves(me, plan, chain, layer + 1, ins, outs, rest[10:])
+    moves = Moves(me, plan, chain, layer + 1, ins, outs, rest[15:])
     moves.start(PACE_FF[0])
+    for c in reads:
+        c.wait()
     sums = Sums(me, part, full, tbuf, rbuf, sems)
     mb = g.shape[1]
     hq = wup.shape[-1]
@@ -1083,10 +1091,13 @@
 
 
 def last_sums(
-    log_outer, act, wdn, hidden, vecs, sf0, su0, sa0, sp0, sf1, su1, sa1, sp1, t_qkv, t_o, g_qkv, g_o, h_up0,
+    log_outer, act_in, wdn_in, hidden, vecs, sf0, su0, sa0, sp0, sf1, su1, sa1, sp1, t_qkv, t_o, g_qkv, g_o, h_up0,
     x_up0, h_qkv0, h_o0, x_qkv0, x_o0, sec, total,
-    part, tbuf, rbuf, sems, lsems, xsems, heap, hsems, *zbufs
+    part, tbuf, rbuf, sems, lsems, xsems, heap, hsems, act, wdn, isems, *zbufs
 ):
+    reads = [pltpu.make_async_copy(act_in, act, isems.at[0]), pltpu.make_async_copy(wdn_in, wdn, isems.at[1])]
+    for c in reads:
+        c.start()
     me = Place()
     me.meet()
     zs = [
@@ -1135,6 +1146,8 @@
             c.wait()
             total[...] += heap[i]
 
+    for c in reads:
+        c.wait()
     halves_of(me, mb, group, sums)
     pump.step(2)
     xs[0].start(1)
@@ -1254,12 +1267,17 @@
             pltpu.VMEM((1, nb, wrows, hq), BF),
             pltpu.VMEM(hidden_shape, BF),
             sem((3,)),
+            pltpu.VMEM(tokens, BF),
+            pltpu.VMEM(tokens, BF),
+            pltpu.VMEM((width, hq), BF),
+            pltpu.VMEM((width, hq), BF),
+            sem((4,)),
         ]
         return call(
             functools.partial(ff_backward, layer, tuple(len(p) for p in plan)),
             cid,
             list(ins) + list(arrays),
-            [VM] * len(ins) + m_specs,
+            [AN] * 4 + [VM] * (len(ins) - 4) + m_specs,
             outs + m_outs,
             [AN] * 3 + [VM] * (len(outs) - 3) + m_out_specs,
             scratch + m_scratch,
@@ -1318,11 +1336,12 @@
         8,
         (act1, wdn1, hidden1, vecs, sf0, su0, sa0, sp0, sf1, su1, sa1, sp1)
         + (qkv0_total, o0_total, g_qkv0, g_o0, h_up0),
-        [VM] * 14 + [AN] * 3,
+        [AN] * 2 + [VM] * 12 + [AN] * 3,
         [half(*ff), half(*qk), half(*oo), half(*qk), half(*oo)] + [(own_shape, BF), ((n_small, width), F32)],
         [AN] + [VM] * 2 + [AN] * 2 + [VM] * 2,
         act_scratch
         + [sem((2, 3)), sem((3, 2, 2)), pltpu.VMEM((4 + log_outer, n_small, width), F32), sem((2, 4 + log_outer))]
+        + [pltpu.VMEM(hidden_shape, BF), pltpu.VMEM((width, hq), BF), sem((2,))]
         + z_scratch(*qk, far, wrows)
         + z_scratch(*oo, far, wrows),
     )

time: 870 us -> 864 us (level)
  no operation moved by 1% of the time
where the time goes in v4:
time: 864 us; the launch traced here: 856 us
  Pallas kernels  826 us (96%)
  other arithmetic  18.8 us (2%)
  local copies, waits for them, and re-layouts  9.76 us (1%)
    pallas_call x6, Pallas kernels, call(): pl.pallas_call(body, out_shape=[jax.ShapeDtypeStruct(sh, dt) for sh, dt i...  826 us

profile of v4, /device:TPU:0, one launch (start us, length us, event | category | flops | bytes accessed | tf_op | source)
XLA Modules:
  0.0 855.9 jit_solution(11903225469084696705)
XLA Ops:
  1.2 0.9 slice_bitcast_fusion.1
  2.0 0.8 slice_bitcast_fusion
  2.8 0.7 concatenate.39.own_vecs
  3.5 0.8 convert_reduce_fusion
  4.3 1.0 fusion
  5.4 1.7 select_convert_fusion.own_pen
  7.1 373.5 %shard_map.186 = (bf16[2,2,2,2,64,2048]{5,4,3,2,1,0:T(8,128)(2,1)}, bf16[2,2,2,64,2048]{4,3,2,1,0:T(8,128)(2,1)}, f32[2,6,2048]{2,1,0:T(8,128)}, f32[2,1,1024]{2...) custom-call(bf16[3,256,1024]{2,1,0:T(8,128)(2,1)} %bitcast.48, ...), custom_call_target="tpu_custom_call" | custom-call | tf_op jit(solution)/shard_map/pallas_call | solution.py:509
  380.6 77.1 %shard_map.187 = (bf16[1,8,256,1024]{3,2,1,0:T(8,128)(2,1)}, bf16[1,8,256,1024]{3,2,1,0:T(8,128)(2,1)}, bf16[2,2,256,1024]{3,2,1,0:T(8,128)(2,1)}, f32[2,64,2048...) custom-call(bf16[2,2,2,2,64,2048]{5,4,3,2,1,0:T(8,128)(2,1)} %get-tu, ...), custom_call_target="tpu_custom_call" | custom-call | tf_op jit(solution)/shard_map/pallas_call | solution.py:509
  457.8 81.7 %shard_map.188 = (bf16[3,8,256,256]{3,2,1,0:T(8,128)(2,1)}, bf16[1,8,256,256]{3,2,1,0:T(8,128)(2,1)}, f32[2,8,2048]{2,1,0:T(8,128)}, f32[3,8,256]{2,1,0:T(8,128)...) custom-call(bf16[2,2,2,2,64,2048]{5,4,3,2,1,0:T(8,128)(2,1)} %get-tuple, ...), custom_call_target="tpu_custom_call" | custom-call | tf_op jit(solution)/shard_map/pallas_call | solution.py:509
  539.5 103.9 %shard_map.189 = (bf16[1,8,256,1024]{3,2,1,0:T(8,128)(2,1)}, bf16[1,8,256,1024]{3,2,1,0:T(8,128)(2,1)}, bf16[2,2,256,1024]{3,2,1,0:T(8,128)(2,1)}, f32[2,64,2048...) custom-call(bf16[2,2,2,2,64,2048]{5,4,3,2,1,0:T(8,128)(2,1)} %get-tu, ...), custom_call_target="tpu_custom_call" | custom-call | tf_op jit(solution)/shard_map/pallas_call | solution.py:509
  643.4 103.8 %shard_map.190 = (bf16[3,8,256,256]{3,2,1,0:T(8,128)(2,1)}, bf16[1,8,256,256]{3,2,1,0:T(8,128)(2,1)}, f32[2,8,2048]{2,1,0:T(8,128)}, f32[3,8,256]{2,1,0:T(8,128)...) custom-call(bf16[2,2,2,2,64,2048]{5,4,3,2,1,0:T(8,128)(2,1)} %get-tu, ...), custom_call_target="tpu_custom_call" | custom-call | tf_op jit(solution)/shard_map/pallas_call | solution.py:509
  747.2 1.5 broadcast_select_fusion.2
  749.1 2.5 maximum_convert_fusion.1
  751.8 86.2 %shard_map.191 = (bf16[1,256,2048]{2,1,0:T(8,128)(2,1)}, bf16[3,256,512]{2,1,0:T(8,128)(2,1)}, bf16[1,256,512]{2,1,0:T(8,128)(2,1)}, bf16[3,256,512]{2,1,0:T(8,1...) custom-call(bf16[2,2,256,1024]{3,2,1,0:T(8,128)(2,1)} %get-tuple-element.89.act_in,, ...), custom_call_target="tpu_custom_call" | custom-call | tf_op jit(solution)/shard_map/pallas_call | solution.py:509
  838.0 1.3 broadcast_select_fusion.3
  839.4 2.5 maximum_convert_fusion
  842.1 1.1 maximum_convert_fusion.2
  844.3 2.1 convert_bitcast_fusion
  846.4 1.9 constant_dynamic-slice_fusion.5
  848.6 1.7 bitcast_select_fusion
  850.8 0.7 copy-done.6
  851.6 1.5 broadcast_select_fusion
  853.1 0.6 constant_dynamic-slice_fusion.4
  853.8 0.6 dynamic-slice_bitcast_fusion
  (49 shorter events, 4.6 us)
Async XLA Ops:
  643.4 103.8 %copy-start.8 = (bf16[1,256,2048]{2,1,0:T(8,128)(2,1)S(1)}, bf16[1,256,2048]{2,1,0:T(8,128)(2,1)}, u32[]{:S(2)}) copy-start(bf16[1,256,2048]{2,1,0:T(8,128)(2,1)} %get-tuple-element.150) | copy-start | bytes 3145732
  747.2 1.5 copy-start.1
  747.2 1.8 copy-start.10
  749.1 2.5 copy-start.2
  749.1 2.5 copy-start.9
  751.8 86.2 %copy-start = (bf16[1,256,2048]{2,1,0:T(8,128)(2,1)S(1)}, bf16[1,256,2048]{2,1,0:T(8,128)(2,1)}, u32[]{:S(2)}) copy-start(bf16[1,256,2048]{2,1,0:T(8,128)(2,1)} %get-tuple-element.124.rest_3_) | copy-start | bytes 3145732
  839.4 2.6 copy-start.14
  839.4 2.5 copy-start.16
  839.4 2.6 copy-start.7
  839.4 2.6 copy-start.15
  841.9 1.2 copy-start.11
  841.9 1.7 copy-start.13
  842.0 1.9 copy-start.3
  842.0 2.1 copy-start.12
  846.4 2.2 copy-start.5
  848.6 2.2 copy-start.4
  848.6 3.0 copy-start.6
  851.6 1.5 copy-start.17
